TPU v7x, 128 devices: a whole 4x4x4 slice. The times are simulated.
128 devices in a mesh: grp: 8 (over x, y_lo), loss: 16 (over z, y_hi, core).
Axes of the slice: x: 4, y: 4 (y_hi: 2, y_lo: 2; y = y_hi * 2 + y_lo), z: 4, core: 2. Of those that a mesh axis runs over, the one named last changes fastest.
Arguments:
- image_embeds: bfloat16 [65536, 1152], P(('grp', 'loss')), parts along dimension 0, may hold values from -0.8 to 0.8
- text_embeds: bfloat16 [65536, 1152], P(('grp', 'loss')), parts along dimension 0, may hold values from -0.8 to 0.8
- log_scale: float32 [8], P('grp'), parts along dimension 0, may hold values from 2 to 2.5
- bias: float32 [8], P('grp'), parts along dimension 0, may hold values from -3 to -1
Outputs:
- loss_rows: float32 [65536], P(('grp', 'loss')), parts along dimension 0
- grad_image: bfloat16 [65536, 1152], P(('grp', 'loss')), parts along dimension 0
- grad_text: bfloat16 [65536, 1152], P(('grp', 'loss')), parts along dimension 0
There are 8 independent parts, one for each index of `grp`. A program takes and returns all parts, laid end to end along the dimension named above; each array names one. Nothing has to cross between parts.
All inputs are finite; a program needn't handle non-finite values.
Results may differ from a plain program's by a relative error of at most 0.0034.
Values may be sent and summed in bfloat16 or wider, within the bound.
No kernel may reach another device: no remote copies, remote signals or barrier semaphores. Data moves between devices by JAX's collectives and lax.ppermute only.
A program may use at most 192 MiB of HBM per device.

v0:
```python
import functools
import math

import jax
import jax.numpy as jnp
from jax import lax
from jax.experimental import pallas as pl
from jax.experimental.pallas import tpu as pltpu
from jax.sharding import PartitionSpec as P

BF, F32 = jnp.bfloat16, jnp.float32
SMEM = pl.BlockSpec(memory_space=pltpu.SMEM)
VMEM = pl.BlockSpec(memory_space=pltpu.VMEM)
COST = 2 * 10**10
STEP = 256
CHUNK = 128
PAD = 16
NT = (((1,), (1,)), ((), ()))
TN = (((0,), (0,)), ((), ()))


def call(kernel, name, inputs, outs, after=(), scoped=16, cost=COST, scratch=()):
    count = len(inputs)
    inputs = [*inputs, *after]
    specs = [SMEM if x.ndim == 1 else VMEM for x in inputs]

    def body(*refs):
        kernel(*refs[:count], *refs[len(inputs) :])

    return pl.pallas_call(
        body,
        name=name,
        in_specs=specs,
        out_specs=[VMEM] * len(outs),
        out_shape=outs,
        scratch_shapes=scratch,
        cost_estimate=pl.CostEstimate(flops=cost, bytes_accessed=0, transcendentals=0),
        compiler_params=pltpu.CompilerParams(vmem_limit_bytes=scoped * 2**20),
    )(*[x if x.ndim == 1 else pltpu.with_memory_space_constraint(x, pltpu.VMEM) for x in inputs])


def recip_of(wide):
    return lax.rsqrt(jnp.sum(wide * wide, axis=1, keepdims=True) + 1e-06)


def in_chunks(rows, body):
    lax.fori_loop(0, rows // CHUNK, lambda k, none: body(pl.ds(pl.multiple_of(k * CHUNK, CHUNK), CHUNK)), None)


def normalize_kernel(raw, whole, *halves):
    rows = raw.shape[0]

    def body(at):
        wide = raw[at, :].astype(F32)
        whole[at, :] = (wide * recip_of(wide)).astype(BF)

    in_chunks(rows, body)
    for k, out in enumerate(halves):
        out[...] = whole[k * (rows // 2) : (k + 1) * (rows // 2), :]


def normalize(raw, name, after=()):
    rows, width = raw.shape
    outs = [pltpu.VMEM((rows // p, width), BF) for p in (1, 2, 2)]
    return call(normalize_kernel, name, [raw], outs, after)


def prepare_kernel(scal, raw, unit, factor):
    def body(at):
        wide = raw[at, :].astype(F32)
        recip = recip_of(wide)
        unit[at, :] = wide * recip
        factor[at, :] = jnp.broadcast_to(recip * scal[2], (CHUNK, factor.shape[1]))

    in_chunks(raw.shape[0], body)


def prepare(scal, raw, name, after):
    rows, width = raw.shape
    outs = [pltpu.VMEM((rows, width), F32), pltpu.VMEM((rows, 128), F32)]
    return call(prepare_kernel, name, [scal, raw], outs, after)


def pair_terms(logits, scale, bias, flip):
    z = logits * scale + bias
    if flip is not None:
        z = z * flip
    e = jnp.exp2(z)
    u = 1.0 + e
    w = e * pl.reciprocal(u, approx=True)
    if flip is not None:
        w = w * flip
    half = logits.shape[1] // 2
    terms = jnp.log1p(e[:, :half] + e[:, half:] * u[:, :half])
    total = terms[:, :128]
    for k in range(1, half // 128):
        total = total + terms[:, k * 128 : (k + 1) * 128]
    return w.astype(BF), total


def loss_rows_of(line, width, first):
    hi = line.astype(BF).astype(F32)
    blank = jnp.zeros((1, width - line.shape[1]), F32)
    hi_row = jnp.concatenate([hi, blank], axis=1)
    lo_row = jnp.concatenate([line - hi, blank], axis=1)
    r = lax.broadcasted_iota(jnp.int32, (PAD, width), 0)
    return jnp.where(r == first, hi_row, jnp.where(r == first + 1, lo_row, 0.0))


def line_of(lanes):
    return jnp.sum(jnp.transpose(lanes), axis=0, keepdims=True)


def rows_kernel(n_t, diag, state, finish, scal, images, *refs):
    texts, refs = refs[:n_t], refs[n_t:]
    given, refs = (refs[:2], refs[2:]) if state else (None, refs)
    w_outs, refs = refs[:n_t], refs[n_t:]
    sums, lanes = refs[-2:]
    half = images.shape[0] // 2
    scale, bias = scal[0], scal[1]
    steps = [(j, c) for j in range(n_t) for c in range(0, texts[j].shape[0], STEP)]

    def text(step):
        j, c = step
        return texts[j][c : c + STEP, :]

    def body(k, none):
        at = pl.multiple_of(k * half, half)
        mine = pl.ds(at, half)
        a = images[mine, :]
        acc = given[0][mine, :] if state else None
        loss = given[1][mine, :] if state else None

        def dot(step):
            return lax.dot_general(a, text(step), NT, preferred_element_type=F32)

        logits, ready = dot(steps[0]), None
        for n, (j, c) in enumerate(steps):
            following = dot(steps[n + 1]) if n + 1 < len(steps) else None
            if ready is not None:
                prod = jnp.dot(ready, text(steps[n - 1]), preferred_element_type=F32)
                acc = prod if acc is None else acc + prod
            flip = None
            if diag and j == 0:
                r = lax.broadcasted_iota(jnp.int32, logits.shape, 0) + at
                q = lax.broadcasted_iota(jnp.int32, logits.shape, 1) + c
                flip = jnp.where(r == q, -1.0, 1.0).astype(F32)
            ready, lane = pair_terms(logits, scale, bias, flip)
            w_outs[j][mine, c : c + STEP] = ready
            loss = lane if loss is None else loss + lane
            logits = following
        sums[mine, :] = acc + jnp.dot(ready, text(steps[-1]), preferred_element_type=F32)
        lanes[mine, :] = loss
        return none

    lax.fori_loop(0, 2, body, None)
    if finish:
        for k, out in enumerate(refs[:2]):
            mine = slice(k * half, (k + 1) * half)
            out[:half, :] = sums[mine, :].astype(BF)
            line = line_of(lanes[mine, :])
            out[half:, :] = loss_rows_of(line, sums.shape[1], 2 if finish == "far" else 0).astype(BF)


def rows_step(name, scal, images, texts, state=(), diag=False, finish=None, after=()):
    rows, width = images.shape
    grads = [((rows, width), F32), ((rows, 128), F32)]
    if finish:
        outs, scratch = [((rows // 2 + PAD, width), BF)] * 2, grads
    else:
        outs, scratch = grads, []
    outs = call(
        functools.partial(rows_kernel, len(texts), diag, bool(state), finish),
        name,
        [scal, images, *texts, *state],
        [pltpu.VMEM((rows, t.shape[0]), BF) for t in texts] + [pltpu.VMEM(*g) for g in outs],
        after,
        scratch=[pltpu.VMEM(*g) for g in scratch],
    )
    return outs[: len(texts)], outs[len(texts) :]


def cols_kernel(n_s, n_w, *refs):
    weights, images, outs = refs[: n_s * n_w], refs[n_s * n_w : n_s * (n_w + 1)], refs[n_s * (n_w + 1) :]
    for h in range(n_w):
        acc = None
        for k in range(n_s):
            prod = lax.dot_general(
                weights[k * n_w + h][...], images[k][...], TN, preferred_element_type=F32
            )
            acc = prod if acc is None else acc + prod
        size = acc.shape[0] // len(outs)
        for k, out in enumerate(outs):
            out[h * size : (h + 1) * size, :] = acc[k * size : (k + 1) * size].astype(out.dtype)


def cols_step(name, weights, images, dtypes, after=()):
    width = images[0].shape[1]
    size = sum(w.shape[1] for w in weights[0]) // len(dtypes)
    return call(
        functools.partial(cols_kernel, len(weights), len(weights[0])),
        name,
        [w for group in weights for w in group] + list(images),
        [pltpu.VMEM((size, width), d) for d in dtypes],
        after,
    )


def hold_kernel(*refs):
    count = len(refs) // 2
    for k in range(count):
        refs[count + k][...] = refs[k][...]


def hold(name, values, after):
    return call(hold_kernel, name, list(values), [pltpu.VMEM(v.shape, v.dtype) for v in values], after, cost=1000)


def merge_kernel(a, b, *outs):
    rows = a.shape[0]
    outs[0][:rows, :] = a[...]
    outs[0][rows:, :] = b[...]
    for out, ref in zip(outs[1:], (a, b)):
        out[...] = ref[...]


def merge(name, a, b, after=(), copies=False):
    rows, width = a.shape
    outs = [pltpu.VMEM((2 * rows, width), BF)] + [pltpu.VMEM(a.shape, BF)] * (2 if copies else 0)
    return call(merge_kernel, name, [a, b], outs, after, cost=1000)


def add_kernel(a, b, out):
    out[...] = (a[...] + b[...].astype(F32)).astype(BF)


def add(name, a, b, after=()):
    return call(add_kernel, name, [a, b], [pltpu.VMEM(a.shape, BF)], after)[0]


def sums_kernel(own, lanes, *refs):
    given, outs = refs[:2], refs[2:]
    half = own.shape[0] // 2
    for k in range(2):
        mine = slice(k * half, (k + 1) * half)
        outs[k][:half, :] = (own[mine, :] + given[k][:half, :].astype(F32)).astype(BF)
        pad = loss_rows_of(line_of(lanes[mine, :]), own.shape[1], 0)
        outs[k][half:, :] = (pad + given[k][half:, :].astype(F32)).astype(BF)


def sums(name, state, given, after):
    return call(sums_kernel, name, [*state, *given], [pltpu.VMEM(g.shape, BF) for g in given], after)


def image_base_kernel(own, lanes, near_a, near_b, base, line):
    half = own.shape[0] // 2
    lines = []
    for k, near in enumerate((near_a, near_b)):
        mine = slice(k * half, (k + 1) * half)
        base[mine, :] = own[mine, :] + near[:half, :].astype(F32)
        lines.append(jnp.sum(near[half:, :half].astype(F32), axis=0, keepdims=True))
    line[...] = jnp.broadcast_to(line_of(lanes[...]) + jnp.concatenate(lines, axis=1), line.shape)


def text_base_kernel(own, more, base):
    base[...] = own[...] + more[...].astype(F32)


def tangent_rows(base, late, unit, factor, out, buf, sem):
    half = base.shape[0] // 2
    for k, (more, first) in enumerate(late):

        def body(j, none, k=k, more=more, first=first):
            at = pl.multiple_of(k * half + j * CHUNK, CHUNK)
            rows = pl.ds(at, CHUNK)
            here = pl.ds(pl.multiple_of(first + j * CHUNK, CHUNK), CHUNK)
            total = base[rows, :] + more[here, :].astype(F32)
            u = unit[rows, :]
            along = jnp.sum(u * total, axis=1, keepdims=True)
            buf[rows, :] = ((total - u * along) * factor[rows, :][:, :1]).astype(BF)
            pltpu.make_async_copy(buf.at[rows, :], out.at[rows, :], sem.at[k]).start()
            return none

        lax.fori_loop(0, half // CHUNK, body, None)
    for k in range(2):
        mine = pl.ds(k * half, half)
        pltpu.make_async_copy(buf.at[mine, :], out.at[mine, :], sem.at[k]).wait()


def image_kernel(count, base, line, unit, factor, sum_a, sum_b, grad_ref, loss_ref, done, buf, sem):
    half = base.shape[0] // 2
    done[...] = jnp.zeros(done.shape, F32)
    lines = [jnp.sum(s[half:, :half].astype(F32), axis=0, keepdims=True) for s in (sum_a, sum_b)]
    loss_ref[...] = (line[:1, :] + jnp.concatenate(lines, axis=1)) * (1.0 / count)
    tangent_rows(base, [(sum_a, 0), (sum_b, 0)], unit, factor, grad_ref, buf, sem)


def text_kernel(base, unit, factor, late, done, grad_ref, buf, sem):
    tangent_rows(base, [(late, 0), (late, base.shape[0] // 2)], unit, factor, grad_ref, buf, sem)


def final(kernel, name, inputs, shape, more):
    return pl.pallas_call(
        kernel,
        name=name,
        in_specs=[VMEM] * len(inputs),
        out_specs=[pl.BlockSpec(memory_space=pl.ANY)] + [VMEM] * len(more),
        out_shape=[jax.ShapeDtypeStruct(shape, BF), *more],
        scratch_shapes=[pltpu.VMEM(shape, BF), pltpu.SemaphoreType.DMA((2,))],
        cost_estimate=pl.CostEstimate(flops=1000, bytes_accessed=0, transcendentals=0),
        compiler_params=pltpu.CompilerParams(vmem_limit_bytes=8 * 2**20),
    )(*[pltpu.with_memory_space_constraint(x, pltpu.VMEM) for x in inputs])


def per_device(total, image_embeds, text_embeds, log_scale, bias):
    def move(value, dz=0, dy=0, dc=0):
        pairs = [
            (z * 4 + y * 2 + c, (z + dz) % 4 * 4 + (y + dy) % 2 * 2 + (c + dc) % 2)
            for z in range(4)
            for y in range(2)
            for c in range(2)
        ]
        return lax.ppermute(value, "loss", pairs)

    rows, width = image_embeds.shape
    scale = jnp.exp(log_scale[0])
    scal = jnp.stack([scale * (1.0 / math.log(2.0)), bias[0] * (1.0 / math.log(2.0)), scale])
    txt, txt_a, txt_b = normalize(text_embeds, "norm_text")
    y_a, txt_c = move(txt_a, dy=1), move(txt, dc=1)
    own, a, b = normalize(image_embeds, "norm_image", after=[txt_a])
    prev_a, next_b = move(a, dz=1), move(b, dz=-1)
    a, b = hold("hold_last", [a, b], [txt_c])
    prev_b, next_a = move(b, dz=1), move(a, dz=-1)
    near_t = [txt, txt_c]
    (own_0, own_c), s_own = rows_step("own_c", scal, own, near_t, diag=True, after=[a])
    (y_a,) = hold("hold_ya", [y_a], s_own[1:])
    yc_a = move(y_a, dc=1)
    i_unit, i_factor = prepare(scal, image_embeds, "prep_image", [y_a])
    (txt_b,) = hold("hold_yb", [txt_b], [yc_a, i_factor])
    y_b = move(txt_b, dy=1)
    (far_t_a,) = merge("merge_ya", y_a, yc_a, [txt_b])
    (own_ya,), s_own = rows_step("own_ya", scal, own, [far_t_a], s_own)
    first, prev_a, next_b = merge("merge_first", prev_a, next_b, s_own[1:], copies=True)
    far_a, far_b = move(prev_a, dz=1), move(next_b, dz=-1)
    (first_0, first_c), s_first = rows_step("first_c", scal, first, near_t)
    (first_ya,), s_first = rows_step("first_ya", scal, first, [far_t_a], s_first)
    t_unit, t_factor = prepare(scal, text_embeds, "prep_text", s_first[1:])
    (y_b,) = hold("hold_text", [y_b], [t_factor])
    yc_b = move(y_b, dc=1)
    (last,) = merge("merge_last", prev_b, next_a, [y_b])
    (last_0, last_c), s_last = rows_step("last_c", scal, last, near_t)
    (far_t_b,) = merge("merge_yb", y_b, yc_b, s_last[1:])
    far_t = [far_t_a, far_t_b]
    last_y, (g_prev_b, g_next_a) = rows_step("last_y", scal, last, far_t, s_last, finish="near")
    near_b, near_a = move(g_prev_b, dz=-1), move(g_next_a, dz=1)
    (own_yb,), s_own = rows_step("own_yb", scal, own, [far_t_b], s_own, after=[g_prev_b])
    (first_yb,), s_first = rows_step("first_yb", scal, first, [far_t_b], s_first, after=s_own[1:])
    (far,) = merge("merge_far", far_a, far_b, s_first[1:])
    far_y, s_far = rows_step("far_y", scal, far, far_t)
    images = [own, first, last, far]
    gt_y, gt_yc = cols_step(
        "cols_y", [[own_ya, own_yb], [first_ya, first_yb], last_y, far_y], images, (F32, BF)
    )
    through_y = move(gt_yc, dc=1)
    (far_0, far_c), (g_far_a, g_far_b) = rows_step(
        "far_c", scal, far, near_t, s_far, finish="far", after=[gt_yc]
    )
    through_a, through_b = move(g_far_a, dz=-1), move(g_far_b, dz=1)
    sum_y = add("add_y", gt_y, through_y, after=[g_far_a])
    text_y = move(sum_y, dy=1)
    (gt_c,) = cols_step(
        "cols_c", [[own_c], [first_c], [last_c], [far_c]], images, (BF,), after=[sum_y, near_a, near_b]
    )
    text_c = move(gt_c, dc=1)
    (gt_own,) = cols_step(
        "cols_own", [[own_0], [first_0], [last_0], [far_0]], images, (F32,), after=[gt_c]
    )
    (t_base,) = call(
        text_base_kernel, "text_base", [gt_own, text_c], [pltpu.VMEM((rows, width), F32)], cost=1000
    )
    i_base, line = call(
        image_base_kernel,
        "image_base",
        [*s_own, near_a, near_b],
        [pltpu.VMEM((rows, width), F32), pltpu.VMEM((8, rows), F32)],
        [t_base],
        cost=1000,
    )
    to_prev, to_next = sums("sums", s_first, [through_a, through_b], [i_base])
    sum_a, sum_b = move(to_prev, dz=-1), move(to_next, dz=1)
    grad_image, loss, done = final(
        functools.partial(image_kernel, total),
        "image",
        [i_base, line, i_unit, i_factor, sum_a, sum_b],
        (rows, width),
        [jax.ShapeDtypeStruct((1, rows), F32), pltpu.VMEM((8, 128), F32)],
    )
    (grad_text,) = final(
        text_kernel, "text", [t_base, t_unit, t_factor, text_y, done], (rows, width), []
    )
    return loss.reshape(rows), grad_image, grad_text


def solution(mesh):
    placed = (P(("grp", "loss"), None), P(("grp", "loss"), None), P("grp"), P("grp"))

    def whole(image_embeds, text_embeds, log_scale, bias):
        total = image_embeds.shape[0] // mesh.shape["grp"]
        return jax.shard_map(
            functools.partial(per_device, total),
            mesh=mesh,
            in_specs=placed,
            out_specs=(P(("grp", "loss")), P(("grp", "loss"), None), P(("grp", "loss"), None)),
            check_vma=False,
        )(image_embeds, text_embeds, log_scale, bias)

    return whole
```

profile of v0, /device:TPU:0, one launch (start us, length us, event | category | flops | bytes accessed | tf_op | source)
XLA Modules:
  0.0 113.6 jit_solution(5733001925298064930)
XLA Ops:
  0.7 1.4 %copy-done.5 = bf16[512,1152]{1,0:T(8,128)(2,1)S(1)} copy-done((bf16[512,1152]{1,0:T(8,128)(2,1)S(1)}, bf16[512,1152]{1,0:T(8,128)(2,1)}, u32[]{:S(2)}) %copy-start.5) | copy-done | bytes 1179672
  2.0 0.7 norm_text.1
  2.7 3.4 %collective-permute-start = (bf16[256,1152]{1,0:T(8,128)(2,1)S(1)}, bf16[256,1152]{1,0:T(8,128)(2,1)S(1)}, u32[]{:S(2)}, u32[]{:S(2)}) collective-permute-start(bf16[256,1152]{1,0:T(8,128)(2,1)S(1)} %get-tuple-element.63.refs_1_), channel_id=1, source_target_pairs={{0,2},{1,3},{2,0},{3,1},{4,6},{5,7},{6,4},{7,5},{8,10},{9,11},{10,... | collective-permute-start | bytes 1769480 | tf_op jit(solution)/shard_map/ppermute | solution.py:323
  6.0 0.7 norm_image.1
  6.7 2.0 %collective-permute-start.4 = (bf16[256,1152]{1,0:T(8,128)(2,1)S(1)}, bf16[256,1152]{1,0:T(8,128)(2,1)S(1)}, u32[]{:S(2)}, u32[]{:S(2)}) collective-permute-start(bf16[256,1152]{1,0:T(8,128)(2,1)S(1)} %get-tuple-element.67.refs_0_), channel_id=1, source_target_pairs={{0,4},{1,5},{2,6},{3,7},{4,8},{5,9},{6,10},{7,11},{8,12},{9,13},{1... | collective-permute-start | bytes 1769480 | tf_op jit(solution)/shard_map/ppermute | solution.py:323
  8.7 2.2 %collective-permute-start.5 = (bf16[256,1152]{1,0:T(8,128)(2,1)S(1)}, bf16[256,1152]{1,0:T(8,128)(2,1)S(1)}, u32[]{:S(2)}, u32[]{:S(2)}) collective-permute-start(bf16[256,1152]{1,0:T(8,128)(2,1)S(1)} %get-tuple-element.68.refs_1_), channel_id=1, source_target_pairs={{0,12},{1,13},{2,14},{3,15},{4,0},{5,1},{6,2},{7,3},{8,4},{9,5},{1... | collective-permute-start | bytes 1769480 | tf_op jit(solution)/shard_map/ppermute | solution.py:323
  12.4 2.0 %collective-permute-start.8 = (bf16[256,1152]{1,0:T(8,128)(2,1)S(1)}, bf16[256,1152]{1,0:T(8,128)(2,1)S(1)}, u32[]{:S(2)}, u32[]{:S(2)}) collective-permute-start(bf16[256,1152]{1,0:T(8,128)(2,1)S(1)} %get-tuple-element.69.refs_4_), channel_id=1, source_target_pairs={{0,12},{1,13},{2,14},{3,15},{4,0},{5,1},{6,2},{7,3},{8,4},{9,5},{1... | collective-permute-start | bytes 1769480 | tf_op jit(solution)/shard_map/ppermute | solution.py:323
  14.4 4.0 %own_c.1 = (bf16[512,512]{1,0:T(8,128)(2,1)S(1)}, bf16[512,512]{1,0:T(8,128)(2,1)S(1)}, f32[512,1152]{1,0:T(8,128)S(1)}, f32[512,128]{1,0:T(8,128)S(1)}) custom-call(f32[3]{0:T(128)S(1)} %pad_maximum_fusion.refs_0_, bf16[512,1152]{1,0:T(8,128)(2,1)S(1)} %get-tuple-element.64.refs_1_.refs_8_.refs_4_, bf16[512,1152]{1,0:T(8,128)(2,1)S(1)} %get-tuple-element.66.refs_2_, ...), custom_call_target="tpu_custom_call" | custom-call | flops 20000000000 | tf_op jit(solution)/shard_map/own_c/pallas_call | solution.py:30
  18.5 0.9 collective-permute-done.refs_0_
  19.5 1.1 prep_image.1
  20.7 2.0 %collective-permute-start.7 = (bf16[256,1152]{1,0:T(8,128)(2,1)S(1)}, bf16[256,1152]{1,0:T(8,128)(2,1)S(1)}, u32[]{:S(2)}, u32[]{:S(2)}) collective-permute-start(bf16[256,1152]{1,0:T(8,128)(2,1)S(1)} %get-tuple-element.79), channel_id=1, source_target_pairs={{0,4},{1,5},{2,6},{3,7},{4,8},{5,9},{6,10},{7,11},{8,12},{9,13},{1... | collective-permute-start | bytes 1769480 | tf_op jit(solution)/shard_map/ppermute | solution.py:323
  22.7 3.3 %collective-permute-start.3 = (bf16[256,1152]{1,0:T(8,128)(2,1)S(1)}, bf16[256,1152]{1,0:T(8,128)(2,1)S(1)}, u32[]{:S(2)}, u32[]{:S(2)}) collective-permute-start(bf16[256,1152]{1,0:T(8,128)(2,1)S(1)} %hold_yb.1.refs_2_), channel_id=1, source_target_pairs={{0,2},{1,3},{2,0},{3,1},{4,6},{5,7},{6,4},{7,5},{8,10},{9,11},{10,... | collective-permute-start | bytes 1769480 | tf_op jit(solution)/shard_map/ppermute | solution.py:323
  26.1 2.6 %own_ya.1 = (bf16[512,512]{1,0:T(8,128)(2,1)S(1)}, f32[512,1152]{1,0:T(8,128)S(1)}, f32[512,128]{1,0:T(8,128)S(1)}) custom-call(f32[3]{0:T(128)S(1)} %pad_maximum_fusion.refs_0_, bf16[512,1152]{1,0:T(8,128)(2,1)S(1)} %get-tuple-element.64.refs_1_.refs_8_.refs_4_, bf16[512,1152]{1,0:T(8,128)(2,1)S(1)} %merge_ya.1.refs_2_, ...), custom_call_target="tpu_custom_call" | custom-call | flops 20000000000 | tf_op jit(solution)/shard_map/own_ya/pallas_call | solution.py:30
  28.8 0.2 merge_first.1
  29.0 2.0 %collective-permute-start.11 = (bf16[256,1152]{1,0:T(8,128)(2,1)S(1)}, bf16[256,1152]{1,0:T(8,128)(2,1)S(1)}, u32[]{:S(2)}, u32[]{:S(2)}) collective-permute-start(bf16[256,1152]{1,0:T(8,128)(2,1)S(1)} %get-tuple-element.90), channel_id=1, source_target_pairs={{0,4},{1,5},{2,6},{3,7},{4,8},{5,9},{6,10},{7,11},{8,12},{9,13},{1... | collective-permute-start | bytes 1769480 | tf_op jit(solution)/shard_map/ppermute | solution.py:323
  31.0 1.3 %collective-permute-start.12 = (bf16[256,1152]{1,0:T(8,128)(2,1)S(1)}, bf16[256,1152]{1,0:T(8,128)(2,1)S(1)}, u32[]{:S(2)}, u32[]{:S(2)}) collective-permute-start(bf16[256,1152]{1,0:T(8,128)(2,1)S(1)} %get-tuple-element.91), channel_id=1, source_target_pairs={{0,12},{1,13},{2,14},{3,15},{4,0},{5,1},{6,2},{7,3},{8,4},{9,5},{1... | collective-permute-start | bytes 1769480 | tf_op jit(solution)/shard_map/ppermute | solution.py:323
  32.3 3.7 %first_c.1 = (bf16[512,512]{1,0:T(8,128)(2,1)S(1)}, bf16[512,512]{1,0:T(8,128)(2,1)S(1)}, f32[512,1152]{1,0:T(8,128)S(1)}, f32[512,128]{1,0:T(8,128)S(1)}) custom-call(f32[3]{0:T(128)S(1)} %pad_maximum_fusion.refs_0_, bf16[512,1152]{1,0:T(8,128)(2,1)S(1)} %get-tuple-element.74.refs_1_.refs_9_.refs_5_, bf16[512,1152]{1,0:T(8,128)(2,1)S(1)} %get-tuple-element.66.refs_2_, ...), custom_call_target="tpu_custom_call" | custom-call | flops 20000000000 | tf_op jit(solution)/shard_map/first_c/pallas_call | solution.py:30
  36.0 2.6 %first_ya.1 = (bf16[512,512]{1,0:T(8,128)(2,1)S(1)}, f32[512,1152]{1,0:T(8,128)S(1)}, f32[512,128]{1,0:T(8,128)S(1)}) custom-call(f32[3]{0:T(128)S(1)} %pad_maximum_fusion.refs_0_, bf16[512,1152]{1,0:T(8,128)(2,1)S(1)} %get-tuple-element.74.refs_1_.refs_9_.refs_5_, bf16[512,1152]{1,0:T(8,128)(2,1)S(1)} %merge_ya.1.refs_2_, ...), custom_call_target="tpu_custom_call" | custom-call | flops 20000000000 | tf_op jit(solution)/shard_map/first_ya/pallas_call | solution.py:30
  38.7 1.1 prep_text.1
  39.9 0.3 collective-permute-start.6
  40.2 0.1 merge_last.1.refs_1_.refs_10_.refs_6_
  40.3 0.3 copy-done
  40.5 3.7 %last_c.1 = (bf16[512,512]{1,0:T(8,128)(2,1)S(1)}, bf16[512,512]{1,0:T(8,128)(2,1)S(1)}, f32[512,1152]{1,0:T(8,128)S(1)}, f32[512,128]{1,0:T(8,128)S(1)}) custom-call(f32[3]{0:T(128)S(1)} %pad_maximum_fusion.refs_0_, bf16[512,1152]{1,0:T(8,128)(2,1)S(1)} %merge_last.1.refs_1_.refs_10_.refs_6_, bf16[512,1152]{1,0:T(8,128)(2,1)S(1)} %get-tuple-element.66.refs_2_, ...), custom_call_target="tpu_custom_call" | custom-call | flops 20000000000 | tf_op jit(solution)/shard_map/last_c/pallas_call | solution.py:30
  44.3 0.1 merge_yb.1.refs_3_.refs_2_
  44.3 4.5 %last_y.1 = (bf16[512,512]{1,0:T(8,128)(2,1)S(1)}, bf16[512,512]{1,0:T(8,128)(2,1)S(1)}, bf16[272,1152]{1,0:T(8,128)(2,1)S(1)}, bf16[272,1152]{1,0:T(8,128)(2,1)S(1)}) custom-call(f32[3]{0:T(128)S(1)} %pad_maximum_fusion.refs_0_, bf16[512,1152]{1,0:T(8,128)(2,1)S(1)} %merge_last.1.refs_1_.refs_10_.refs_6_, bf16[512,1152]{1,0:T(8,128)(2,1)S(1)} %merge_ya.1.refs_2_, ...), custom_call_target="tpu_custom_call" | custom-call | flops 20000000000 | tf_op jit(solution)/shard_map/last_y/pallas_call | solution.py:30
  48.8 2.6 %collective-permute-start.10 = (bf16[272,1152]{1,0:T(8,128)(2,1)S(1)}, bf16[272,1152]{1,0:T(8,128)(2,1)S(1)}, u32[]{:S(2)}, u32[]{:S(2)}) collective-permute-start(bf16[272,1152]{1,0:T(8,128)(2,1)S(1)} %get-tuple-element.83.refs_5_), channel_id=1, source_target_pairs={{0,12},{1,13},{2,14},{3,15},{4,0},{5,1},{6,2},{7,3},{8,4},{9,5},{1... | collective-permute-start | bytes 1880072 | tf_op jit(solution)/shard_map/ppermute | solution.py:323
  51.4 2.6 %own_yb.1 = (bf16[512,512]{1,0:T(8,128)(2,1)S(1)}, f32[512,1152]{1,0:T(8,128)S(1)}, f32[512,128]{1,0:T(8,128)S(1)}) custom-call(f32[3]{0:T(128)S(1)} %pad_maximum_fusion.refs_0_, bf16[512,1152]{1,0:T(8,128)(2,1)S(1)} %get-tuple-element.64.refs_1_.refs_8_.refs_4_, bf16[512,1152]{1,0:T(8,128)(2,1)S(1)} %merge_yb.1.refs_3_.refs_2_, ...), custom_call_target="tpu_custom_call" | custom-call | flops 20000000000 | tf_op jit(solution)/shard_map/own_yb/pallas_call | solution.py:30
  54.1 2.6 %first_yb.1 = (bf16[512,512]{1,0:T(8,128)(2,1)S(1)}, f32[512,1152]{1,0:T(8,128)S(1)}, f32[512,128]{1,0:T(8,128)S(1)}) custom-call(f32[3]{0:T(128)S(1)} %pad_maximum_fusion.refs_0_, bf16[512,1152]{1,0:T(8,128)(2,1)S(1)} %get-tuple-element.74.refs_1_.refs_9_.refs_5_, bf16[512,1152]{1,0:T(8,128)(2,1)S(1)} %merge_yb.1.refs_3_.refs_2_, ...), custom_call_target="tpu_custom_call" | custom-call | flops 20000000000 | tf_op jit(solution)/shard_map/first_yb/pallas_call | solution.py:30
  56.7 0.1 merge_far.1.refs_1_.refs_11_.refs_7_
  56.8 3.7 %far_y.1 = (bf16[512,512]{1,0:T(8,128)(2,1)S(1)}, bf16[512,512]{1,0:T(8,128)(2,1)S(1)}, f32[512,1152]{1,0:T(8,128)S(1)}, f32[512,128]{1,0:T(8,128)S(1)}) custom-call(f32[3]{0:T(128)S(1)} %pad_maximum_fusion.refs_0_, bf16[512,1152]{1,0:T(8,128)(2,1)S(1)} %merge_far.1.refs_1_.refs_11_.refs_7_, bf16[512,1152]{1,0:T(8,128)(2,1)S(1)} %merge_ya.1.refs_2_, ...), custom_call_target="tpu_custom_call" | custom-call | flops 20000000000 | tf_op jit(solution)/shard_map/far_y/pallas_call | solution.py:30
  60.6 5.7 %cols_y.1 = (f32[512,1152]{1,0:T(8,128)S(1)}, bf16[512,1152]{1,0:T(8,128)(2,1)S(1)}) custom-call(bf16[512,512]{1,0:T(8,128)(2,1)S(1)} %get-tuple-element.96.refs_0_, bf16[512,512]{1,0:T(8,128)(2,1)S(1)} %get-tuple-element.97.refs_1_, bf16[512,512]{1,0:T(8,128)(2,1)S(1)} %get-tuple-element.98.refs_2_, bf16[512,512]{1,0:T(8,128)(2,1)S(1)} %get-tuple-element.99.refs_3_, ...), custom_call_target="tpu_custom_call" | custom-call | flops 20000000000 | tf_op jit(solution)/shard_map/cols_y/pallas_call | solution.py:30
  66.3 0.5 collective-permute-start.13
  66.8 4.5 %far_c.1 = (bf16[512,512]{1,0:T(8,128)(2,1)S(1)}, bf16[512,512]{1,0:T(8,128)(2,1)S(1)}, bf16[272,1152]{1,0:T(8,128)(2,1)S(1)}, bf16[272,1152]{1,0:T(8,128)(2,1)S(1)}) custom-call(f32[3]{0:T(128)S(1)} %pad_maximum_fusion.refs_0_, bf16[512,1152]{1,0:T(8,128)(2,1)S(1)} %merge_far.1.refs_1_.refs_11_.refs_7_, bf16[512,1152]{1,0:T(8,128)(2,1)S(1)} %get-tuple-element.66.refs_2_, ...), custom_call_target="tpu_custom_call" | custom-call | flops 20000000000 | tf_op jit(solution)/shard_map/far_c/pallas_call | solution.py:30
  71.3 1.0 collective-permute-start.16
  72.3 2.3 %collective-permute-start.15 = (bf16[272,1152]{1,0:T(8,128)(2,1)S(1)}, bf16[272,1152]{1,0:T(8,128)(2,1)S(1)}, u32[]{:S(2)}, u32[]{:S(2)}) collective-permute-start(bf16[272,1152]{1,0:T(8,128)(2,1)S(1)} %get-tuple-element.111.refs_2_), channel_id=1, source_target_pairs={{0,12},{1,13},{2,14},{3,15},{4,0},{5,1},{6,2},{7,3},{8,4},{9,5},{1... | collective-permute-start | bytes 1880072 | tf_op jit(solution)/shard_map/ppermute | solution.py:323
  74.6 0.3 add_y.1.refs_8_
  74.9 3.3 %collective-permute-start.19 = (bf16[512,1152]{1,0:T(8,128)(2,1)S(1)}, bf16[512,1152]{1,0:T(8,128)(2,1)S(1)}, u32[]{:S(2)}, u32[]{:S(2)}) collective-permute-start(bf16[512,1152]{1,0:T(8,128)(2,1)S(1)} %add_y.1.refs_8_), channel_id=1, source_target_pairs={{0,2},{1,3},{2,0},{3,1},{4,6},{5,7},{6,4},{7,5},{8,10},{9,11},{10,... | collective-permute-start | bytes 3538952 | tf_op jit(solution)/shard_map/ppermute | solution.py:323
  78.2 3.0 %cols_c.1.refs_8_ = bf16[512,1152]{1,0:T(8,128)(2,1)S(1)} custom-call(bf16[512,512]{1,0:T(8,128)(2,1)S(1)} %get-tuple-element.106.refs_0_, bf16[512,512]{1,0:T(8,128)(2,1)S(1)} %get-tuple-element.107.refs_1_, bf16[512,512]{1,0:T(8,128)(2,1)S(1)} %get-tuple-element.108.refs_2_, bf16[512,512]{1,0:T(8,128)(2,1)S(1)} %get-tuple-element.109.refs_3_, ...), custom_call_target="tpu_custom_call" | custom-call | flops 20000000000 | tf_op jit(solution)/shard_map/cols_c/pallas_call | solution.py:30
  81.3 2.9 %cols_own.1.refs_0_ = f32[512,1152]{1,0:T(8,128)S(1)} custom-call(bf16[512,512]{1,0:T(8,128)(2,1)S(1)} %get-tuple-element.87.refs_0_, bf16[512,512]{1,0:T(8,128)(2,1)S(1)} %get-tuple-element.88.refs_1_, bf16[512,512]{1,0:T(8,128)(2,1)S(1)} %get-tuple-element.89.refs_2_, bf16[512,512]{1,0:T(8,128)(2,1)S(1)} %get-tuple-element.105.refs_3_, ...), custom_call_target="tpu_custom_call" | custom-call | flops 20000000000 | tf_op jit(solution)/shard_map/cols_own/pallas_call | solution.py:30
  84.2 0.2 text_base.1.refs_4_.base
  84.4 0.3 image_base.1
  84.7 4.5 %collective-permute-done.16.refs_3_ = bf16[272,1152]{1,0:T(8,128)(2,1)S(1)} collective-permute-done((bf16[272,1152]{1,0:T(8,128)(2,1)S(1)}, bf16[272,1152]{1,0:T(8,128)(2,1)S(1)}, u32[]{:S(2)}, u32[]{:S(2)}) %collective-permute-start.16) | collective-permute-done | bytes 626720 | tf_op jit(solution)/shard_map/ppermute | solution.py:323
  89.2 0.5 sums.1
  89.7 3.1 %collective-permute-start.17 = (bf16[272,1152]{1,0:T(8,128)(2,1)S(1)}, bf16[272,1152]{1,0:T(8,128)(2,1)S(1)}, u32[]{:S(2)}, u32[]{:S(2)}) collective-permute-start(bf16[272,1152]{1,0:T(8,128)(2,1)S(1)} %get-tuple-element.117), channel_id=1, source_target_pairs={{0,12},{1,13},{2,14},{3,15},{4,0},{5,1},{6,2},{7,3},{8,4},{9,5},{1... | collective-permute-start | bytes 1880072 | tf_op jit(solution)/shard_map/ppermute | solution.py:323
  92.8 13.1 %collective-permute-done.17.sum_a = bf16[272,1152]{1,0:T(8,128)(2,1)S(1)} collective-permute-done((bf16[272,1152]{1,0:T(8,128)(2,1)S(1)}, bf16[272,1152]{1,0:T(8,128)(2,1)S(1)}, u32[]{:S(2)}, u32[]{:S(2)}) %collective-permute-start.17) | collective-permute-done | bytes 626720 | tf_op jit(solution)/shard_map/ppermute | solution.py:323
  105.9 3.4 %collective-permute-done.18.sum_b = bf16[272,1152]{1,0:T(8,128)(2,1)S(1)} collective-permute-done((bf16[272,1152]{1,0:T(8,128)(2,1)S(1)}, bf16[272,1152]{1,0:T(8,128)(2,1)S(1)}, u32[]{:S(2)}, u32[]{:S(2)}) %collective-permute-start.18) | collective-permute-done | bytes 626720 | tf_op jit(solution)/shard_map/ppermute | solution.py:323
  109.4 2.3 %image.1 = (bf16[512,1152]{1,0:T(8,128)(2,1)}, f32[1,512]{1,0:T(1,128)}, f32[8,128]{1,0:T(8,128)S(1)}) custom-call(f32[512,1152]{1,0:T(8,128)S(1)} %get-tuple-element.112.refs_4_.base, f32[8,512]{1,0:T(8,128)S(1)} %get-tuple-element.113.line, f32[512,1152]{1,0:T(8,128)S(1)} %get-tuple-element.114.unit, f32[512,128]{1,0:T(8,128)S(1)} %copy-done.3, ...), custom_call_target="tpu_custom_call" | custom-call | flops 1000 | tf_op jit(solution)/shard_map/image/pallas_call | solution.py:303
  111.7 1.8 %text.1 = bf16[512,1152]{1,0:T(8,128)(2,1)} custom-call(f32[512,1152]{1,0:T(8,128)S(1)} %text_base.1.refs_4_.base, f32[512,1152]{1,0:T(8,128)S(1)} %get-tuple-element.121.unit, f32[512,128]{1,0:T(8,128)S(1)} %copy-done.1, bf16[512,1152]{1,0:T(8,128)(2,1)S(1)} %collective-permute-done.19.late, f32[8,128]{1,0:T(8,128)S(1)} %get-tuple-element.122.done), custom_call_target="tpu_custom_call" | custom-call | flops 1000 | tf_op jit(solution)/shard_map/text/pallas_call | solution.py:303
  (39 shorter events, 0.7 us)
Async XLA Ops:
  0.6 5.4 %copy-start.4 = (bf16[512,1152]{1,0:T(8,128)(2,1)S(1)}, bf16[512,1152]{1,0:T(8,128)(2,1)}, u32[]{:S(2)}) copy-start(bf16[512,1152]{1,0:T(8,128)(2,1)} %refs_1_.2) | copy-start | bytes 3538948
  0.6 1.4 %copy-start.5 = (bf16[512,1152]{1,0:T(8,128)(2,1)S(1)}, bf16[512,1152]{1,0:T(8,128)(2,1)}, u32[]{:S(2)}) copy-start(bf16[512,1152]{1,0:T(8,128)(2,1)} %refs_1_.3) | copy-start | bytes 3538948
  2.7 16.7 %collective-permute-start = (bf16[256,1152]{1,0:T(8,128)(2,1)S(1)}, bf16[256,1152]{1,0:T(8,128)(2,1)S(1)}, u32[]{:S(2)}, u32[]{:S(2)}) collective-permute-start(bf16[256,1152]{1,0:T(8,128)(2,1)S(1)} %get-tuple-element.63.refs_1_), channel_id=1, source_target_pairs={{0,2},{1,3},{2,0},{3,1},{4,6},{5,7},{6,4},{7,5},{8,10},{9,11},{10,... | collective-permute-start | bytes 1769480 | tf_op jit(solution)/shard_map/ppermute | solution.py:323
  6.0 6.3 %collective-permute-start.1 = (bf16[512,1152]{1,0:T(8,128)(2,1)S(1)}, bf16[512,1152]{1,0:T(8,128)(2,1)S(1)}, u32[]{:S(2)}, u32[]{:S(2)}) collective-permute-start(bf16[512,1152]{1,0:T(8,128)(2,1)S(1)} %get-tuple-element.66.refs_2_), channel_id=1, source_target_pairs={{0,1},{1,0},{2,3},{3,2},{4,5},{5,4},{6,7},{7,6},{8,9},{9,8},{10,11... | collective-permute-start | bytes 3538952 | tf_op jit(solution)/shard_map/ppermute | solution.py:323
  6.7 22.0 %collective-permute-start.4 = (bf16[256,1152]{1,0:T(8,128)(2,1)S(1)}, bf16[256,1152]{1,0:T(8,128)(2,1)S(1)}, u32[]{:S(2)}, u32[]{:S(2)}) collective-permute-start(bf16[256,1152]{1,0:T(8,128)(2,1)S(1)} %get-tuple-element.67.refs_0_), channel_id=1, source_target_pairs={{0,4},{1,5},{2,6},{3,7},{4,8},{5,9},{6,10},{7,11},{8,12},{9,13},{1... | collective-permute-start | bytes 1769480 | tf_op jit(solution)/shard_map/ppermute | solution.py:323
  8.7 20.1 %collective-permute-start.5 = (bf16[256,1152]{1,0:T(8,128)(2,1)S(1)}, bf16[256,1152]{1,0:T(8,128)(2,1)S(1)}, u32[]{:S(2)}, u32[]{:S(2)}) collective-permute-start(bf16[256,1152]{1,0:T(8,128)(2,1)S(1)} %get-tuple-element.68.refs_1_), channel_id=1, source_target_pairs={{0,12},{1,13},{2,14},{3,15},{4,0},{5,1},{6,2},{7,3},{8,4},{9,5},{1... | collective-permute-start | bytes 1769480 | tf_op jit(solution)/shard_map/ppermute | solution.py:323
  12.4 27.7 %collective-permute-start.8 = (bf16[256,1152]{1,0:T(8,128)(2,1)S(1)}, bf16[256,1152]{1,0:T(8,128)(2,1)S(1)}, u32[]{:S(2)}, u32[]{:S(2)}) collective-permute-start(bf16[256,1152]{1,0:T(8,128)(2,1)S(1)} %get-tuple-element.69.refs_4_), channel_id=1, source_target_pairs={{0,12},{1,13},{2,14},{3,15},{4,0},{5,1},{6,2},{7,3},{8,4},{9,5},{1... | collective-permute-start | bytes 1769480 | tf_op jit(solution)/shard_map/ppermute | solution.py:323
  19.4 3.3 %collective-permute-start.2 = (bf16[256,1152]{1,0:T(8,128)(2,1)S(1)}, bf16[256,1152]{1,0:T(8,128)(2,1)S(1)}, u32[]{:S(2)}, u32[]{:S(2)}) collective-permute-start(bf16[256,1152]{1,0:T(8,128)(2,1)S(1)} %hold_ya.1.refs_2_.refs_0_), channel_id=1, source_target_pairs={{0,1},{1,0},{2,3},{3,2},{4,5},{5,4},{6,7},{7,6},{8,9},{9,8},{10,11... | collective-permute-start | bytes 1769480 | tf_op jit(solution)/shard_map/ppermute | solution.py:323
  20.6 5.5 %copy-start.2 = (f32[512,128]{1,0:T(8,128)}, f32[512,128]{1,0:T(8,128)S(1)}, u32[]{:S(2)}) copy-start(f32[512,128]{1,0:T(8,128)S(1)} %get-tuple-element.71.refs_2_.factor) | copy-start | bytes 786436
  20.7 19.5 %collective-permute-start.7 = (bf16[256,1152]{1,0:T(8,128)(2,1)S(1)}, bf16[256,1152]{1,0:T(8,128)(2,1)S(1)}, u32[]{:S(2)}, u32[]{:S(2)}) collective-permute-start(bf16[256,1152]{1,0:T(8,128)(2,1)S(1)} %get-tuple-element.79), channel_id=1, source_target_pairs={{0,4},{1,5},{2,6},{3,7},{4,8},{5,9},{6,10},{7,11},{8,12},{9,13},{1... | collective-permute-start | bytes 1769480 | tf_op jit(solution)/shard_map/ppermute | solution.py:323
  22.7 17.1 %collective-permute-start.3 = (bf16[256,1152]{1,0:T(8,128)(2,1)S(1)}, bf16[256,1152]{1,0:T(8,128)(2,1)S(1)}, u32[]{:S(2)}, u32[]{:S(2)}) collective-permute-start(bf16[256,1152]{1,0:T(8,128)(2,1)S(1)} %hold_yb.1.refs_2_), channel_id=1, source_target_pairs={{0,2},{1,3},{2,0},{3,1},{4,6},{5,7},{6,4},{7,5},{8,10},{9,11},{10,... | collective-permute-start | bytes 1769480 | tf_op jit(solution)/shard_map/ppermute | solution.py:323
  29.0 27.8 %collective-permute-start.11 = (bf16[256,1152]{1,0:T(8,128)(2,1)S(1)}, bf16[256,1152]{1,0:T(8,128)(2,1)S(1)}, u32[]{:S(2)}, u32[]{:S(2)}) collective-permute-start(bf16[256,1152]{1,0:T(8,128)(2,1)S(1)} %get-tuple-element.90), channel_id=1, source_target_pairs={{0,4},{1,5},{2,6},{3,7},{4,8},{5,9},{6,10},{7,11},{8,12},{9,13},{1... | collective-permute-start | bytes 1769480 | tf_op jit(solution)/shard_map/ppermute | solution.py:323
  31.0 25.8 %collective-permute-start.12 = (bf16[256,1152]{1,0:T(8,128)(2,1)S(1)}, bf16[256,1152]{1,0:T(8,128)(2,1)S(1)}, u32[]{:S(2)}, u32[]{:S(2)}) collective-permute-start(bf16[256,1152]{1,0:T(8,128)(2,1)S(1)} %get-tuple-element.91), channel_id=1, source_target_pairs={{0,12},{1,13},{2,14},{3,15},{4,0},{5,1},{6,2},{7,3},{8,4},{9,5},{1... | collective-permute-start | bytes 1769480 | tf_op jit(solution)/shard_map/ppermute | solution.py:323
  36.0 2.7 %copy-start.6 = (bf16[512,1152]{1,0:T(8,128)(2,1)S(1)}, bf16[512,1152]{1,0:T(8,128)(2,1)}, u32[]{:S(2)}) copy-start(bf16[512,1152]{1,0:T(8,128)(2,1)} %refs_1_.3) | copy-start | bytes 3538948
  39.8 0.7 copy-start
  39.9 4.4 %collective-permute-start.6 = (bf16[256,1152]{1,0:T(8,128)(2,1)S(1)}, bf16[256,1152]{1,0:T(8,128)(2,1)S(1)}, u32[]{:S(2)}, u32[]{:S(2)}) collective-permute-start(bf16[256,1152]{1,0:T(8,128)(2,1)S(1)} %hold_text.1.refs_2_.refs_0_), channel_id=1, source_target_pairs={{0,1},{1,0},{2,3},{3,2},{4,5},{5,4},{6,7},{7,6},{8,9},{9,8},{10,11... | collective-permute-start | bytes 1769480 | tf_op jit(solution)/shard_map/ppermute | solution.py:323
  48.8 29.4 %collective-permute-start.10 = (bf16[272,1152]{1,0:T(8,128)(2,1)S(1)}, bf16[272,1152]{1,0:T(8,128)(2,1)S(1)}, u32[]{:S(2)}, u32[]{:S(2)}) collective-permute-start(bf16[272,1152]{1,0:T(8,128)(2,1)S(1)} %get-tuple-element.83.refs_5_), channel_id=1, source_target_pairs={{0,12},{1,13},{2,14},{3,15},{4,0},{5,1},{6,2},{7,3},{8,4},{9,5},{1... | collective-permute-start | bytes 1880072 | tf_op jit(solution)/shard_map/ppermute | solution.py:323
  54.0 24.2 %collective-permute-start.9 = (bf16[272,1152]{1,0:T(8,128)(2,1)S(1)}, bf16[272,1152]{1,0:T(8,128)(2,1)S(1)}, u32[]{:S(2)}, u32[]{:S(2)}) collective-permute-start(bf16[272,1152]{1,0:T(8,128)(2,1)S(1)} %get-tuple-element.86), channel_id=1, source_target_pairs={{0,4},{1,5},{2,6},{3,7},{4,8},{5,9},{6,10},{7,11},{8,12},{9,13},{1... | collective-permute-start | bytes 1880072 | tf_op jit(solution)/shard_map/ppermute | solution.py:323
  66.3 8.3 %collective-permute-start.13 = (bf16[512,1152]{1,0:T(8,128)(2,1)S(1)}, bf16[512,1152]{1,0:T(8,128)(2,1)S(1)}, u32[]{:S(2)}, u32[]{:S(2)}) collective-permute-start(bf16[512,1152]{1,0:T(8,128)(2,1)S(1)} %get-tuple-element.104.refs_6_), channel_id=1, source_target_pairs={{0,1},{1,0},{2,3},{3,2},{4,5},{5,4},{6,7},{7,6},{8,9},{9,8},{10,11... | collective-permute-start | bytes 3538952 | tf_op jit(solution)/shard_map/ppermute | solution.py:323
  71.3 17.9 %collective-permute-start.16 = (bf16[272,1152]{1,0:T(8,128)(2,1)S(1)}, bf16[272,1152]{1,0:T(8,128)(2,1)S(1)}, u32[]{:S(2)}, u32[]{:S(2)}) collective-permute-start(bf16[272,1152]{1,0:T(8,128)(2,1)S(1)} %get-tuple-element.116), channel_id=1, source_target_pairs={{0,4},{1,5},{2,6},{3,7},{4,8},{5,9},{6,10},{7,11},{8,12},{9,13},{1... | collective-permute-start | bytes 1880072 | tf_op jit(solution)/shard_map/ppermute | solution.py:323
  72.3 16.9 %collective-permute-start.15 = (bf16[272,1152]{1,0:T(8,128)(2,1)S(1)}, bf16[272,1152]{1,0:T(8,128)(2,1)S(1)}, u32[]{:S(2)}, u32[]{:S(2)}) collective-permute-start(bf16[272,1152]{1,0:T(8,128)(2,1)S(1)} %get-tuple-element.111.refs_2_), channel_id=1, source_target_pairs={{0,12},{1,13},{2,14},{3,15},{4,0},{5,1},{6,2},{7,3},{8,4},{9,5},{1... | collective-permute-start | bytes 1880072 | tf_op jit(solution)/shard_map/ppermute | solution.py:323
  74.9 36.7 %collective-permute-start.19 = (bf16[512,1152]{1,0:T(8,128)(2,1)S(1)}, bf16[512,1152]{1,0:T(8,128)(2,1)S(1)}, u32[]{:S(2)}, u32[]{:S(2)}) collective-permute-start(bf16[512,1152]{1,0:T(8,128)(2,1)S(1)} %add_y.1.refs_8_), channel_id=1, source_target_pairs={{0,2},{1,3},{2,0},{3,1},{4,6},{5,7},{6,4},{7,5},{8,10},{9,11},{10,... | collective-permute-start | bytes 3538952 | tf_op jit(solution)/shard_map/ppermute | solution.py:323
  81.2 3.0 %collective-permute-start.14 = (bf16[512,1152]{1,0:T(8,128)(2,1)S(1)}, bf16[512,1152]{1,0:T(8,128)(2,1)S(1)}, u32[]{:S(2)}, u32[]{:S(2)}) collective-permute-start(bf16[512,1152]{1,0:T(8,128)(2,1)S(1)} %cols_c.1.refs_8_), channel_id=1, source_target_pairs={{0,1},{1,0},{2,3},{3,2},{4,5},{5,4},{6,7},{7,6},{8,9},{9,8},{10,11... | collective-permute-start | bytes 3538952 | tf_op jit(solution)/shard_map/ppermute | solution.py:323
  89.2 20.2 %copy-start.3 = (f32[512,128]{1,0:T(8,128)S(1)}, f32[512,128]{1,0:T(8,128)}, u32[]{:S(2)}) copy-start(f32[512,128]{1,0:T(8,128)} %copy-done.2) | copy-start | bytes 786436
  89.7 16.2 %collective-permute-start.17 = (bf16[272,1152]{1,0:T(8,128)(2,1)S(1)}, bf16[272,1152]{1,0:T(8,128)(2,1)S(1)}, u32[]{:S(2)}, u32[]{:S(2)}) collective-permute-start(bf16[272,1152]{1,0:T(8,128)(2,1)S(1)} %get-tuple-element.117), channel_id=1, source_target_pairs={{0,12},{1,13},{2,14},{3,15},{4,0},{5,1},{6,2},{7,3},{8,4},{9,5},{1... | collective-permute-start | bytes 1880072 | tf_op jit(solution)/shard_map/ppermute | solution.py:323
  92.8 16.5 %collective-permute-start.18 = (bf16[272,1152]{1,0:T(8,128)(2,1)S(1)}, bf16[272,1152]{1,0:T(8,128)(2,1)S(1)}, u32[]{:S(2)}, u32[]{:S(2)}) collective-permute-start(bf16[272,1152]{1,0:T(8,128)(2,1)S(1)} %get-tuple-element.118), channel_id=1, source_target_pairs={{0,4},{1,5},{2,6},{3,7},{4,8},{5,9},{6,10},{7,11},{8,12},{9,13},{1... | collective-permute-start | bytes 1880072 | tf_op jit(solution)/shard_map/ppermute | solution.py:323
  109.4 2.3 %copy-start.1 = (f32[512,128]{1,0:T(8,128)S(1)}, f32[512,128]{1,0:T(8,128)}, u32[]{:S(2)}) copy-start(f32[512,128]{1,0:T(8,128)} %copy-done) | copy-start | bytes 786436
where the time goes:
time: 114 us
  Pallas kernels  56 us (49%)
  starting transfers between devices  31.5 us (28%)
  waiting for transfers between devices  21.9 us (19%)
  between operations  2.53 us (2%)
  local copies, waits for them, and re-layouts  1.64 us (1%)
    pallas_call x30, Pallas kernels, call(): pl.pallas_call(body, name=name, in_specs=specs, out_specs=[VMEM] * len(ou...  52 us
    ppermute x20, starting transfers between devices, move(): return lax.ppermute(value, 'loss', pairs)  31.5 us
    ppermute x20, waiting for transfers between devices, move(): return lax.ppermute(value, 'loss', pairs)  21.9 us
    pallas_call x2, Pallas kernels, final(): pl.pallas_call(kernel, name=name, in_specs=[VMEM] * len(inputs), out_spec...  4.06 us
  transfers between devices with their start and end apart: 20, of which 4 were waited for; matrix products, arithmetic and copies ran while one was open for 0% of the time, Pallas kernels for 47%

commit v1 on v0

--- a/solution.py
+++ b/solution.py
@@ -59,9 +59,9 @@
         out[...] = whole[k * (rows // 2) : (k + 1) * (rows // 2), :]
 
 
-def normalize(raw, name, after=()):
+def normalize(raw, name, halves, after=()):
     rows, width = raw.shape
-    outs = [pltpu.VMEM((rows // p, width), BF) for p in (1, 2, 2)]
+    outs = [pltpu.VMEM((rows // p, width), BF) for p in ((1, 2, 2) if halves else (1,))]
     return call(normalize_kernel, name, [raw], outs, after)
 
 
@@ -98,20 +98,20 @@
     return w.astype(BF), total
 
 
-def loss_rows_of(line, width, first):
+def loss_rows_of(line, width):
     hi = line.astype(BF).astype(F32)
     blank = jnp.zeros((1, width - line.shape[1]), F32)
     hi_row = jnp.concatenate([hi, blank], axis=1)
     lo_row = jnp.concatenate([line - hi, blank], axis=1)
     r = lax.broadcasted_iota(jnp.int32, (PAD, width), 0)
-    return jnp.where(r == first, hi_row, jnp.where(r == first + 1, lo_row, 0.0))
+    return jnp.where(r == 0, hi_row, jnp.where(r == 1, lo_row, 0.0)).astype(BF)
 
 
 def line_of(lanes):
     return jnp.sum(jnp.transpose(lanes), axis=0, keepdims=True)
 
 
-def rows_kernel(n_t, diag, state, finish, scal, images, *refs):
+def rows_kernel(n_t, diag, state, scal, images, *refs):
     texts, refs = refs[:n_t], refs[n_t:]
     given, refs = (refs[:2], refs[2:]) if state else (None, refs)
     w_outs, refs = refs[:n_t], refs[n_t:]
@@ -154,23 +154,22 @@
         return none
 
     lax.fori_loop(0, 2, body, None)
-    if finish:
-        for k, out in enumerate(refs[:2]):
-            mine = slice(k * half, (k + 1) * half)
-            out[:half, :] = sums[mine, :].astype(BF)
-            line = line_of(lanes[mine, :])
-            out[half:, :] = loss_rows_of(line, sums.shape[1], 2 if finish == "far" else 0).astype(BF)
-
-
-def rows_step(name, scal, images, texts, state=(), diag=False, finish=None, after=()):
+    for k, out in enumerate(refs[:-2]):
+        rows = out.shape[0] - PAD
+        mine = slice(k * rows, (k + 1) * rows)
+        out[:rows, :] = sums[mine, :].astype(BF)
+        out[rows:, :] = loss_rows_of(line_of(lanes[mine, :]), sums.shape[1])
+
+
+def rows_step(name, scal, images, texts, state=(), diag=False, finish=0, after=()):
     rows, width = images.shape
     grads = [((rows, width), F32), ((rows, 128), F32)]
     if finish:
-        outs, scratch = [((rows // 2 + PAD, width), BF)] * 2, grads
+        outs, scratch = [((rows // finish + PAD, width), BF)] * finish, grads
     else:
         outs, scratch = grads, []
     outs = call(
-        functools.partial(rows_kernel, len(texts), diag, bool(state), finish),
+        functools.partial(rows_kernel, len(texts), diag, bool(state)),
         name,
         [scal, images, *texts, *state],
         [pltpu.VMEM((rows, t.shape[0]), BF) for t in texts] + [pltpu.VMEM(*g) for g in outs],
@@ -238,27 +237,14 @@
     return call(add_kernel, name, [a, b], [pltpu.VMEM(a.shape, BF)], after)[0]
 
 
-def sums_kernel(own, lanes, *refs):
-    given, outs = refs[:2], refs[2:]
-    half = own.shape[0] // 2
-    for k in range(2):
-        mine = slice(k * half, (k + 1) * half)
-        outs[k][:half, :] = (own[mine, :] + given[k][:half, :].astype(F32)).astype(BF)
-        pad = loss_rows_of(line_of(lanes[mine, :]), own.shape[1], 0)
-        outs[k][half:, :] = (pad + given[k][half:, :].astype(F32)).astype(BF)
-
-
-def sums(name, state, given, after):
-    return call(sums_kernel, name, [*state, *given], [pltpu.VMEM(g.shape, BF) for g in given], after)
-
-
-def image_base_kernel(own, lanes, near_a, near_b, base, line):
+def image_base_kernel(own, lanes, a_0, a_1, b_0, b_1, base, line):
     half = own.shape[0] // 2
     lines = []
-    for k, near in enumerate((near_a, near_b)):
+    for k, (p, q) in enumerate(((a_0, a_1), (b_0, b_1))):
         mine = slice(k * half, (k + 1) * half)
-        base[mine, :] = own[mine, :] + near[:half, :].astype(F32)
-        lines.append(jnp.sum(near[half:, :half].astype(F32), axis=0, keepdims=True))
+        base[mine, :] = own[mine, :] + p[:half, :].astype(F32) + q[:half, :].astype(F32)
+        tail = p[half:, :half].astype(F32) + q[half:, :half].astype(F32)
+        lines.append(jnp.sum(tail, axis=0, keepdims=True))
     line[...] = jnp.broadcast_to(line_of(lanes[...]) + jnp.concatenate(lines, axis=1), line.shape)
 
 
@@ -267,36 +253,27 @@
 
 
 def tangent_rows(base, late, unit, factor, out, buf, sem):
-    half = base.shape[0] // 2
-    for k, (more, first) in enumerate(late):
-
-        def body(j, none, k=k, more=more, first=first):
-            at = pl.multiple_of(k * half + j * CHUNK, CHUNK)
-            rows = pl.ds(at, CHUNK)
-            here = pl.ds(pl.multiple_of(first + j * CHUNK, CHUNK), CHUNK)
-            total = base[rows, :] + more[here, :].astype(F32)
-            u = unit[rows, :]
-            along = jnp.sum(u * total, axis=1, keepdims=True)
-            buf[rows, :] = ((total - u * along) * factor[rows, :][:, :1]).astype(BF)
-            pltpu.make_async_copy(buf.at[rows, :], out.at[rows, :], sem.at[k]).start()
-            return none
-
-        lax.fori_loop(0, half // CHUNK, body, None)
-    for k in range(2):
-        mine = pl.ds(k * half, half)
-        pltpu.make_async_copy(buf.at[mine, :], out.at[mine, :], sem.at[k]).wait()
-
-
-def image_kernel(count, base, line, unit, factor, sum_a, sum_b, grad_ref, loss_ref, done, buf, sem):
-    half = base.shape[0] // 2
+    def body(at):
+        total = base[at, :] + late[at, :].astype(F32)
+        u = unit[at, :]
+        along = jnp.sum(u * total, axis=1, keepdims=True)
+        buf[at, :] = ((total - u * along) * factor[at, :][:, :1]).astype(BF)
+        pltpu.make_async_copy(buf.at[at, :], out.at[at, :], sem).start()
+
+    in_chunks(base.shape[0], body)
+    pltpu.make_async_copy(buf, out, sem).wait()
+
+
+def image_kernel(count, base, line, unit, factor, late, done, grad_ref, loss_ref, buf, sem):
+    rows = base.shape[0]
+    tail = jnp.sum(late[rows:, :rows].astype(F32), axis=0, keepdims=True)
+    loss_ref[...] = (line[:1, :] + tail) * (1.0 / count)
+    tangent_rows(base, late, unit, factor, grad_ref, buf, sem)
+
+
+def text_kernel(base, unit, factor, late, grad_ref, done, buf, sem):
     done[...] = jnp.zeros(done.shape, F32)
-    lines = [jnp.sum(s[half:, :half].astype(F32), axis=0, keepdims=True) for s in (sum_a, sum_b)]
-    loss_ref[...] = (line[:1, :] + jnp.concatenate(lines, axis=1)) * (1.0 / count)
-    tangent_rows(base, [(sum_a, 0), (sum_b, 0)], unit, factor, grad_ref, buf, sem)
-
-
-def text_kernel(base, unit, factor, late, done, grad_ref, buf, sem):
-    tangent_rows(base, [(late, 0), (late, base.shape[0] // 2)], unit, factor, grad_ref, buf, sem)
+    tangent_rows(base, late, unit, factor, grad_ref, buf, sem)
 
 
 def final(kernel, name, inputs, shape, more):
@@ -306,7 +283,7 @@
         in_specs=[VMEM] * len(inputs),
         out_specs=[pl.BlockSpec(memory_space=pl.ANY)] + [VMEM] * len(more),
         out_shape=[jax.ShapeDtypeStruct(shape, BF), *more],
-        scratch_shapes=[pltpu.VMEM(shape, BF), pltpu.SemaphoreType.DMA((2,))],
+        scratch_shapes=[pltpu.VMEM(shape, BF), pltpu.SemaphoreType.DMA(())],
         cost_estimate=pl.CostEstimate(flops=1000, bytes_accessed=0, transcendentals=0),
         compiler_params=pltpu.CompilerParams(vmem_limit_bytes=8 * 2**20),
     )(*[pltpu.with_memory_space_constraint(x, pltpu.VMEM) for x in inputs])
@@ -325,78 +302,65 @@
     rows, width = image_embeds.shape
     scale = jnp.exp(log_scale[0])
     scal = jnp.stack([scale * (1.0 / math.log(2.0)), bias[0] * (1.0 / math.log(2.0)), scale])
-    txt, txt_a, txt_b = normalize(text_embeds, "norm_text")
-    y_a, txt_c = move(txt_a, dy=1), move(txt, dc=1)
-    own, a, b = normalize(image_embeds, "norm_image", after=[txt_a])
+    (txt,) = normalize(text_embeds, "norm_text", False)
+    txt_y, txt_c = move(txt, dy=1), move(txt, dc=1)
+    own, a, b = normalize(image_embeds, "norm_image", True, after=[txt])
     prev_a, next_b = move(a, dz=1), move(b, dz=-1)
     a, b = hold("hold_last", [a, b], [txt_c])
     prev_b, next_a = move(b, dz=1), move(a, dz=-1)
     near_t = [txt, txt_c]
     (own_0, own_c), s_own = rows_step("own_c", scal, own, near_t, diag=True, after=[a])
-    (y_a,) = hold("hold_ya", [y_a], s_own[1:])
-    yc_a = move(y_a, dc=1)
-    i_unit, i_factor = prepare(scal, image_embeds, "prep_image", [y_a])
-    (txt_b,) = hold("hold_yb", [txt_b], [yc_a, i_factor])
-    y_b = move(txt_b, dy=1)
-    (far_t_a,) = merge("merge_ya", y_a, yc_a, [txt_b])
-    (own_ya,), s_own = rows_step("own_ya", scal, own, [far_t_a], s_own)
     first, prev_a, next_b = merge("merge_first", prev_a, next_b, s_own[1:], copies=True)
     far_a, far_b = move(prev_a, dz=1), move(next_b, dz=-1)
     (first_0, first_c), s_first = rows_step("first_c", scal, first, near_t)
-    (first_ya,), s_first = rows_step("first_ya", scal, first, [far_t_a], s_first)
-    t_unit, t_factor = prepare(scal, text_embeds, "prep_text", s_first[1:])
-    (y_b,) = hold("hold_text", [y_b], [t_factor])
-    yc_b = move(y_b, dc=1)
-    (last,) = merge("merge_last", prev_b, next_a, [y_b])
+    i_unit, i_factor = prepare(scal, image_embeds, "prep_image", s_first[1:])
+    (txt_y,) = hold("hold_text", [txt_y], [i_factor])
+    far_t = [txt_y, move(txt_y, dc=1)]
+    t_unit, t_factor = prepare(scal, text_embeds, "prep_text", [txt_y])
+    (own_y, own_yc), s_own = rows_step("own_y", scal, own, far_t, s_own, after=[t_factor])
+    (first_y, first_yc), (g_prev_a, g_next_b) = rows_step(
+        "first_y", scal, first, far_t, s_first, finish=2, after=s_own[1:]
+    )
+    home_a0, home_b0 = move(g_prev_a, dz=-1), move(g_next_b, dz=1)
+    (last,) = merge("merge_last", prev_b, next_a, [g_prev_a])
     (last_0, last_c), s_last = rows_step("last_c", scal, last, near_t)
-    (far_t_b,) = merge("merge_yb", y_b, yc_b, s_last[1:])
-    far_t = [far_t_a, far_t_b]
-    last_y, (g_prev_b, g_next_a) = rows_step("last_y", scal, last, far_t, s_last, finish="near")
-    near_b, near_a = move(g_prev_b, dz=-1), move(g_next_a, dz=1)
-    (own_yb,), s_own = rows_step("own_yb", scal, own, [far_t_b], s_own, after=[g_prev_b])
-    (first_yb,), s_first = rows_step("first_yb", scal, first, [far_t_b], s_first, after=s_own[1:])
-    (far,) = merge("merge_far", far_a, far_b, s_first[1:])
-    far_y, s_far = rows_step("far_y", scal, far, far_t)
+    (last_y, last_yc), (g_prev_b, g_next_a) = rows_step("last_y", scal, last, far_t, s_last, finish=2)
+    home_b1, home_a1 = move(g_prev_b, dz=-1), move(g_next_a, dz=1)
+    (far,) = merge("merge_far", far_a, far_b, [g_prev_b])
+    (far_y, far_yc), s_far = rows_step("far_y", scal, far, far_t)
     images = [own, first, last, far]
-    gt_y, gt_yc = cols_step(
-        "cols_y", [[own_ya, own_yb], [first_ya, first_yb], last_y, far_y], images, (F32, BF)
-    )
+    (gt_yc,) = cols_step("cols_yc", [[own_yc], [first_yc], [last_yc], [far_yc]], images, (BF,))
     through_y = move(gt_yc, dc=1)
-    (far_0, far_c), (g_far_a, g_far_b) = rows_step(
-        "far_c", scal, far, near_t, s_far, finish="far", after=[gt_yc]
-    )
-    through_a, through_b = move(g_far_a, dz=-1), move(g_far_b, dz=1)
-    sum_y = add("add_y", gt_y, through_y, after=[g_far_a])
+    (gt_y,) = cols_step("cols_y", [[own_y], [first_y], [last_y], [far_y]], images, (F32,), after=[gt_yc])
+    (far_0, far_c), (g_far,) = rows_step("far_c", scal, far, near_t, s_far, finish=1, after=[gt_y])
+    sum_y = add("add_y", gt_y, through_y, after=[g_far, home_a0, home_b0])
     text_y = move(sum_y, dy=1)
-    (gt_c,) = cols_step(
-        "cols_c", [[own_c], [first_c], [last_c], [far_c]], images, (BF,), after=[sum_y, near_a, near_b]
-    )
+    home_far = move(g_far, dz=2)
+    (gt_c,) = cols_step("cols_c", [[own_c], [first_c], [last_c], [far_c]], images, (BF,), after=[sum_y])
     text_c = move(gt_c, dc=1)
     (gt_own,) = cols_step(
         "cols_own", [[own_0], [first_0], [last_0], [far_0]], images, (F32,), after=[gt_c]
     )
-    (t_base,) = call(
-        text_base_kernel, "text_base", [gt_own, text_c], [pltpu.VMEM((rows, width), F32)], cost=1000
-    )
     i_base, line = call(
         image_base_kernel,
         "image_base",
-        [*s_own, near_a, near_b],
+        [*s_own, home_a0, home_a1, home_b0, home_b1],
         [pltpu.VMEM((rows, width), F32), pltpu.VMEM((8, rows), F32)],
-        [t_base],
+        [gt_own],
         cost=1000,
     )
-    to_prev, to_next = sums("sums", s_first, [through_a, through_b], [i_base])
-    sum_a, sum_b = move(to_prev, dz=-1), move(to_next, dz=1)
-    grad_image, loss, done = final(
+    (t_base,) = call(
+        text_base_kernel, "text_base", [gt_own, text_c], [pltpu.VMEM((rows, width), F32)], [line], cost=1000
+    )
+    grad_text, done = final(
+        text_kernel, "text", [t_base, t_unit, t_factor, text_y], (rows, width), [pltpu.VMEM((8, 128), F32)]
+    )
+    grad_image, loss = final(
         functools.partial(image_kernel, total),
         "image",
-        [i_base, line, i_unit, i_factor, sum_a, sum_b],
+        [i_base, line, i_unit, i_factor, home_far, done],
         (rows, width),
-        [jax.ShapeDtypeStruct((1, rows), F32), pltpu.VMEM((8, 128), F32)],
-    )
-    (grad_text,) = final(
-        text_kernel, "text", [t_base, t_unit, t_factor, text_y, done], (rows, width), []
+        [jax.ShapeDtypeStruct((1, rows), F32)],
     )
     return loss.reshape(rows), grad_image, grad_text
 

time: 114 us -> 111 us (0.974)
  starting transfers between devices: 31.5 us -> 24.8 us
  waiting for transfers between devices: 21.9 us -> 25.9 us
  Pallas kernels: 56 us -> 54.5 us
    ppermute x20 -> x17, starting transfers between devices: 31.5 us -> 24.8 us  [move(): return lax.ppermute(value, 'loss', pairs)]
    ppermute x20 -> x17, waiting for transfers between devices: 21.9 us -> 25.9 us  [move(): return lax.ppermute(value, 'loss', pairs)]
    pallas_call x30 -> x24, Pallas kernels: 52 us -> 50.4 us  [call(): pl.pallas_call(body, name=name, in_specs=specs, out_specs=[VMEM] * len(ou...]
    unnamed x14 -> x18, local copies, waits for them, and re-layouts: 1.64 us -> 2.66 us
  transfers between devices with their start and end apart: 20 -> 17, of which waited for: 4 -> 3; matrix products, arithmetic and copies ran while one was open for 0% -> 0% of each run, Pallas kernels for 47% -> 47%
where the time goes in v1:
time: 111 us; the launch traced here: 110 us
  Pallas kernels  54.5 us (49%)
  waiting for transfers between devices  25.9 us (23%)
  starting transfers between devices  24.8 us (22%)
  local copies, waits for them, and re-layouts  2.66 us (2%)
  between operations  2.5 us (2%)
    pallas_call x24, Pallas kernels, call(): pl.pallas_call(body, name=name, in_specs=specs, out_specs=[VMEM] * len(ou...  50.4 us
    ppermute x17, waiting for transfers between devices, move(): return lax.ppermute(value, 'loss', pairs)  25.9 us
    ppermute x17, starting transfers between devices, move(): return lax.ppermute(value, 'loss', pairs)  24.8 us
    pallas_call x2, Pallas kernels, final(): pl.pallas_call(kernel, name=name, in_specs=[VMEM] * len(inputs), out_spec...  4.07 us
    unnamed x18, local copies, waits for them, and re-layouts  2.66 us
  transfers between devices with their start and end apart: 17, of which 3 were waited for; matrix products, arithmetic and copies ran while one was open for 0% of the time, Pallas kernels for 47%

profile of v1, /device:TPU:0, one launch (start us, length us, event | category | flops | bytes accessed | tf_op | source)
XLA Modules:
  0.0 110.5 jit_solution(2349458164219397386)
XLA Ops:
  0.7 1.4 %copy-done.7 = bf16[512,1152]{1,0:T(8,128)(2,1)S(1)} copy-done((bf16[512,1152]{1,0:T(8,128)(2,1)S(1)}, bf16[512,1152]{1,0:T(8,128)(2,1)}, u32[]{:S(2)}) %copy-start.7) | copy-done | bytes 1179672
  2.0 0.6 norm_text.1.refs_1_.refs_2_
  2.6 0.1 collective-permute-start.3
  2.7 3.4 %collective-permute-start = (bf16[512,1152]{1,0:T(8,128)(2,1)S(1)}, bf16[512,1152]{1,0:T(8,128)(2,1)S(1)}, u32[]{:S(2)}, u32[]{:S(2)}) collective-permute-start(bf16[512,1152]{1,0:T(8,128)(2,1)S(1)} %norm_text.1.refs_1_.refs_2_), channel_id=1, source_target_pairs={{0,2},{1,3},{2,0},{3,1},{4,6},{5,7},{6,4},{7,5},{8,10},{9,11},{10,... | collective-permute-start | bytes 3538952 | tf_op jit(solution)/shard_map/ppermute | solution.py:300
  6.1 0.7 norm_image.1
  6.7 2.0 %collective-permute-start.1 = (bf16[256,1152]{1,0:T(8,128)(2,1)S(1)}, bf16[256,1152]{1,0:T(8,128)(2,1)S(1)}, u32[]{:S(2)}, u32[]{:S(2)}) collective-permute-start(bf16[256,1152]{1,0:T(8,128)(2,1)S(1)} %get-tuple-element.53.refs_0_), channel_id=1, source_target_pairs={{0,4},{1,5},{2,6},{3,7},{4,8},{5,9},{6,10},{7,11},{8,12},{9,13},{1... | collective-permute-start | bytes 1769480 | tf_op jit(solution)/shard_map/ppermute | solution.py:300
  8.7 2.2 %collective-permute-start.2 = (bf16[256,1152]{1,0:T(8,128)(2,1)S(1)}, bf16[256,1152]{1,0:T(8,128)(2,1)S(1)}, u32[]{:S(2)}, u32[]{:S(2)}) collective-permute-start(bf16[256,1152]{1,0:T(8,128)(2,1)S(1)} %get-tuple-element.54.refs_1_), channel_id=1, source_target_pairs={{0,12},{1,13},{2,14},{3,15},{4,0},{5,1},{6,2},{7,3},{8,4},{9,5},{1... | collective-permute-start | bytes 1769480 | tf_op jit(solution)/shard_map/ppermute | solution.py:300
  12.3 0.1 pad_maximum_fusion.refs_0_
  12.3 0.1 hold_last.1
  12.5 3.2 %collective-permute-start.7 = (bf16[256,1152]{1,0:T(8,128)(2,1)S(1)}, bf16[256,1152]{1,0:T(8,128)(2,1)S(1)}, u32[]{:S(2)}, u32[]{:S(2)}) collective-permute-start(bf16[256,1152]{1,0:T(8,128)(2,1)S(1)} %get-tuple-element.55.refs_4_), channel_id=1, source_target_pairs={{0,12},{1,13},{2,14},{3,15},{4,0},{5,1},{6,2},{7,3},{8,4},{9,5},{1... | collective-permute-start | bytes 1769480 | tf_op jit(solution)/shard_map/ppermute | solution.py:300
  15.7 4.1 %own_c.1 = (bf16[512,512]{1,0:T(8,128)(2,1)S(1)}, bf16[512,512]{1,0:T(8,128)(2,1)S(1)}, f32[512,1152]{1,0:T(8,128)S(1)}, f32[512,128]{1,0:T(8,128)S(1)}) custom-call(f32[3]{0:T(128)S(1)} %pad_maximum_fusion.refs_0_, bf16[512,1152]{1,0:T(8,128)(2,1)S(1)} %get-tuple-element.52.refs_1_.refs_4_, bf16[512,1152]{1,0:T(8,128)(2,1)S(1)} %norm_text.1.refs_1_.refs_2_, ...), custom_call_target="tpu_custom_call" | custom-call | flops 20000000000 | tf_op jit(solution)/shard_map/own_c/pallas_call | solution.py:30
  19.8 5.1 %collective-permute-done.1.refs_0_ = bf16[256,1152]{1,0:T(8,128)(2,1)S(1)} collective-permute-done((bf16[256,1152]{1,0:T(8,128)(2,1)S(1)}, bf16[256,1152]{1,0:T(8,128)(2,1)S(1)}, u32[]{:S(2)}, u32[]{:S(2)}) %collective-permute-start.1) | collective-permute-done | bytes 589856 | tf_op jit(solution)/shard_map/ppermute | solution.py:300
  25.0 0.2 merge_first.1
  25.1 2.0 %collective-permute-start.11 = (bf16[256,1152]{1,0:T(8,128)(2,1)S(1)}, bf16[256,1152]{1,0:T(8,128)(2,1)S(1)}, u32[]{:S(2)}, u32[]{:S(2)}) collective-permute-start(bf16[256,1152]{1,0:T(8,128)(2,1)S(1)} %get-tuple-element.75), channel_id=1, source_target_pairs={{0,4},{1,5},{2,6},{3,7},{4,8},{5,9},{6,10},{7,11},{8,12},{9,13},{1... | collective-permute-start | bytes 1769480 | tf_op jit(solution)/shard_map/ppermute | solution.py:300
  27.1 1.5 %collective-permute-start.12 = (bf16[256,1152]{1,0:T(8,128)(2,1)S(1)}, bf16[256,1152]{1,0:T(8,128)(2,1)S(1)}, u32[]{:S(2)}, u32[]{:S(2)}) collective-permute-start(bf16[256,1152]{1,0:T(8,128)(2,1)S(1)} %get-tuple-element.76), channel_id=1, source_target_pairs={{0,12},{1,13},{2,14},{3,15},{4,0},{5,1},{6,2},{7,3},{8,4},{9,5},{1... | collective-permute-start | bytes 1769480 | tf_op jit(solution)/shard_map/ppermute | solution.py:300
  28.6 3.8 %first_c.1 = (bf16[512,512]{1,0:T(8,128)(2,1)S(1)}, bf16[512,512]{1,0:T(8,128)(2,1)S(1)}, f32[512,1152]{1,0:T(8,128)S(1)}, f32[512,128]{1,0:T(8,128)S(1)}) custom-call(f32[3]{0:T(128)S(1)} %pad_maximum_fusion.refs_0_, bf16[512,1152]{1,0:T(8,128)(2,1)S(1)} %get-tuple-element.57.refs_1_.refs_5_, bf16[512,1152]{1,0:T(8,128)(2,1)S(1)} %norm_text.1.refs_1_.refs_2_, ...), custom_call_target="tpu_custom_call" | custom-call | flops 20000000000 | tf_op jit(solution)/shard_map/first_c/pallas_call | solution.py:30
  32.4 1.1 %prep_image.1 = (f32[512,1152]{1,0:T(8,128)S(1)}, f32[512,128]{1,0:T(8,128)S(1)}) custom-call(f32[3]{0:T(128)S(1)} %pad_maximum_fusion.refs_0_, bf16[512,1152]{1,0:T(8,128)(2,1)S(1)} %copy-done.6, f32[512,128]{1,0:T(8,128)S(1)} %get-tuple-element.58.refs_2_.refs_5_), custom_call_target="tpu_custom_call" | custom-call | flops 20000000000 | tf_op jit(solution)/shard_map/prep_image/pallas_call | solution.py:30
  33.6 0.1 hold_text.1.refs_2_
  33.7 0.6 copy-done
  34.3 0.7 copy-done.8
  34.9 1.1 %prep_text.1 = (f32[512,1152]{1,0:T(8,128)S(1)}, f32[512,128]{1,0:T(8,128)S(1)}) custom-call(f32[3]{0:T(128)S(1)} %pad_maximum_fusion.refs_0_, bf16[512,1152]{1,0:T(8,128)(2,1)S(1)} %copy-done.8, bf16[512,1152]{1,0:T(8,128)(2,1)S(1)} %hold_text.1.refs_2_), custom_call_target="tpu_custom_call" | custom-call | flops 20000000000 | tf_op jit(solution)/shard_map/prep_text/pallas_call | solution.py:30
  36.1 1.0 collective-permute-done.4.refs_3_
  37.1 4.4 %own_y.1 = (bf16[512,512]{1,0:T(8,128)(2,1)S(1)}, bf16[512,512]{1,0:T(8,128)(2,1)S(1)}, f32[512,1152]{1,0:T(8,128)S(1)}, f32[512,128]{1,0:T(8,128)S(1)}) custom-call(f32[3]{0:T(128)S(1)} %pad_maximum_fusion.refs_0_, bf16[512,1152]{1,0:T(8,128)(2,1)S(1)} %get-tuple-element.52.refs_1_.refs_4_, bf16[512,1152]{1,0:T(8,128)(2,1)S(1)} %hold_text.1.refs_2_, ...), custom_call_target="tpu_custom_call" | custom-call | flops 20000000000 | tf_op jit(solution)/shard_map/own_y/pallas_call | solution.py:30
  41.5 4.5 %first_y.1 = (bf16[512,512]{1,0:T(8,128)(2,1)S(1)}, bf16[512,512]{1,0:T(8,128)(2,1)S(1)}, bf16[272,1152]{1,0:T(8,128)(2,1)S(1)}, bf16[272,1152]{1,0:T(8,128)(2,1)S(1)}) custom-call(f32[3]{0:T(128)S(1)} %pad_maximum_fusion.refs_0_, bf16[512,1152]{1,0:T(8,128)(2,1)S(1)} %get-tuple-element.57.refs_1_.refs_5_, bf16[512,1152]{1,0:T(8,128)(2,1)S(1)} %hold_text.1.refs_2_, ...), custom_call_target="tpu_custom_call" | custom-call | flops 20000000000 | tf_op jit(solution)/shard_map/first_y/pallas_call | solution.py:30
  46.0 0.6 collective-permute-start.9
  46.6 2.7 %collective-permute-start.5 = (bf16[272,1152]{1,0:T(8,128)(2,1)S(1)}, bf16[272,1152]{1,0:T(8,128)(2,1)S(1)}, u32[]{:S(2)}, u32[]{:S(2)}) collective-permute-start(bf16[272,1152]{1,0:T(8,128)(2,1)S(1)} %get-tuple-element.65.refs_2_), channel_id=1, source_target_pairs={{0,12},{1,13},{2,14},{3,15},{4,0},{5,1},{6,2},{7,3},{8,4},{9,5},{1... | collective-permute-start | bytes 1880072 | tf_op jit(solution)/shard_map/ppermute | solution.py:300
  49.4 0.1 merge_last.1.refs_1_.refs_6_
  49.4 3.8 %last_c.1 = (bf16[512,512]{1,0:T(8,128)(2,1)S(1)}, bf16[512,512]{1,0:T(8,128)(2,1)S(1)}, f32[512,1152]{1,0:T(8,128)S(1)}, f32[512,128]{1,0:T(8,128)S(1)}) custom-call(f32[3]{0:T(128)S(1)} %pad_maximum_fusion.refs_0_, bf16[512,1152]{1,0:T(8,128)(2,1)S(1)} %merge_last.1.refs_1_.refs_6_, bf16[512,1152]{1,0:T(8,128)(2,1)S(1)} %norm_text.1.refs_1_.refs_2_, ...), custom_call_target="tpu_custom_call" | custom-call | flops 20000000000 | tf_op jit(solution)/shard_map/last_c/pallas_call | solution.py:30
  53.2 4.5 %last_y.1 = (bf16[512,512]{1,0:T(8,128)(2,1)S(1)}, bf16[512,512]{1,0:T(8,128)(2,1)S(1)}, bf16[272,1152]{1,0:T(8,128)(2,1)S(1)}, bf16[272,1152]{1,0:T(8,128)(2,1)S(1)}) custom-call(f32[3]{0:T(128)S(1)} %pad_maximum_fusion.refs_0_, bf16[512,1152]{1,0:T(8,128)(2,1)S(1)} %merge_last.1.refs_1_.refs_6_, bf16[512,1152]{1,0:T(8,128)(2,1)S(1)} %hold_text.1.refs_2_, ...), custom_call_target="tpu_custom_call" | custom-call | flops 20000000000 | tf_op jit(solution)/shard_map/last_y/pallas_call | solution.py:30
  57.8 0.1 collective-permute-start.8
  57.9 3.2 %collective-permute-start.10 = (bf16[272,1152]{1,0:T(8,128)(2,1)S(1)}, bf16[272,1152]{1,0:T(8,128)(2,1)S(1)}, u32[]{:S(2)}, u32[]{:S(2)}) collective-permute-start(bf16[272,1152]{1,0:T(8,128)(2,1)S(1)} %get-tuple-element.71.refs_2_), channel_id=1, source_target_pairs={{0,12},{1,13},{2,14},{3,15},{4,0},{5,1},{6,2},{7,3},{8,4},{9,5},{1... | collective-permute-start | bytes 1880072 | tf_op jit(solution)/shard_map/ppermute | solution.py:300
  61.1 0.1 merge_far.1.refs_1_.refs_7_
  61.2 3.7 %far_y.1 = (bf16[512,512]{1,0:T(8,128)(2,1)S(1)}, bf16[512,512]{1,0:T(8,128)(2,1)S(1)}, f32[512,1152]{1,0:T(8,128)S(1)}, f32[512,128]{1,0:T(8,128)S(1)}) custom-call(f32[3]{0:T(128)S(1)} %pad_maximum_fusion.refs_0_, bf16[512,1152]{1,0:T(8,128)(2,1)S(1)} %merge_far.1.refs_1_.refs_7_, bf16[512,1152]{1,0:T(8,128)(2,1)S(1)} %hold_text.1.refs_2_, ...), custom_call_target="tpu_custom_call" | custom-call | flops 20000000000 | tf_op jit(solution)/shard_map/far_y/pallas_call | solution.py:30
  64.9 3.0 %cols_yc.1.refs_8_ = bf16[512,1152]{1,0:T(8,128)(2,1)S(1)} custom-call(bf16[512,512]{1,0:T(8,128)(2,1)S(1)} %get-tuple-element.83.refs_0_, bf16[512,512]{1,0:T(8,128)(2,1)S(1)} %get-tuple-element.84.refs_1_, bf16[512,512]{1,0:T(8,128)(2,1)S(1)} %get-tuple-element.85.refs_2_, bf16[512,512]{1,0:T(8,128)(2,1)S(1)} %get-tuple-element.86.refs_3_, ...), custom_call_target="tpu_custom_call" | custom-call | flops 20000000000 | tf_op jit(solution)/shard_map/cols_yc/pallas_call | solution.py:30
  67.9 0.1 collective-permute-start.13
  68.0 3.0 %cols_y.1.refs_6_.refs_0_ = f32[512,1152]{1,0:T(8,128)S(1)} custom-call(bf16[512,512]{1,0:T(8,128)(2,1)S(1)} %get-tuple-element.79.refs_0_, bf16[512,512]{1,0:T(8,128)(2,1)S(1)} %get-tuple-element.80.refs_1_, bf16[512,512]{1,0:T(8,128)(2,1)S(1)} %get-tuple-element.81.refs_2_, bf16[512,512]{1,0:T(8,128)(2,1)S(1)} %get-tuple-element.82.refs_3_, ...), custom_call_target="tpu_custom_call" | custom-call | flops 20000000000 | tf_op jit(solution)/shard_map/cols_y/pallas_call | solution.py:30
  71.0 4.6 %far_c.1 = (bf16[512,512]{1,0:T(8,128)(2,1)S(1)}, bf16[512,512]{1,0:T(8,128)(2,1)S(1)}, bf16[528,1152]{1,0:T(8,128)(2,1)S(1)}) custom-call(f32[3]{0:T(128)S(1)} %pad_maximum_fusion.refs_0_, bf16[512,1152]{1,0:T(8,128)(2,1)S(1)} %merge_far.1.refs_1_.refs_7_, bf16[512,1152]{1,0:T(8,128)(2,1)S(1)} %norm_text.1.refs_1_.refs_2_, ...), custom_call_target="tpu_custom_call" | custom-call | flops 20000000000 | tf_op jit(solution)/shard_map/far_c/pallas_call | solution.py:30
  75.6 0.3 collective-permute-start.14
  76.0 0.3 add_y.1.refs_8_
  76.2 3.3 %collective-permute-start.16 = (bf16[512,1152]{1,0:T(8,128)(2,1)S(1)}, bf16[512,1152]{1,0:T(8,128)(2,1)S(1)}, u32[]{:S(2)}, u32[]{:S(2)}) collective-permute-start(bf16[512,1152]{1,0:T(8,128)(2,1)S(1)} %add_y.1.refs_8_), channel_id=1, source_target_pairs={{0,2},{1,3},{2,0},{3,1},{4,6},{5,7},{6,4},{7,5},{8,10},{9,11},{10,... | collective-permute-start | bytes 3538952 | tf_op jit(solution)/shard_map/ppermute | solution.py:300
  79.5 3.0 %cols_c.1.refs_8_ = bf16[512,1152]{1,0:T(8,128)(2,1)S(1)} custom-call(bf16[512,512]{1,0:T(8,128)(2,1)S(1)} %get-tuple-element.88.refs_0_, bf16[512,512]{1,0:T(8,128)(2,1)S(1)} %get-tuple-element.89.refs_1_, bf16[512,512]{1,0:T(8,128)(2,1)S(1)} %get-tuple-element.90.refs_2_, bf16[512,512]{1,0:T(8,128)(2,1)S(1)} %get-tuple-element.91.refs_3_, ...), custom_call_target="tpu_custom_call" | custom-call | flops 20000000000 | tf_op jit(solution)/shard_map/cols_c/pallas_call | solution.py:30
  82.5 0.1 collective-permute-start.15
  82.6 3.0 %cols_own.1.refs_6_.refs_0_ = f32[512,1152]{1,0:T(8,128)S(1)} custom-call(bf16[512,512]{1,0:T(8,128)(2,1)S(1)} %get-tuple-element.72.refs_0_, bf16[512,512]{1,0:T(8,128)(2,1)S(1)} %get-tuple-element.73.refs_1_, bf16[512,512]{1,0:T(8,128)(2,1)S(1)} %get-tuple-element.74.refs_2_, bf16[512,512]{1,0:T(8,128)(2,1)S(1)} %get-tuple-element.87.refs_3_, ...), custom_call_target="tpu_custom_call" | custom-call | flops 20000000000 | tf_op jit(solution)/shard_map/cols_own/pallas_call | solution.py:30
  85.6 0.7 image_base.1
  86.3 0.2 text_base.1.base
  86.5 19.7 %collective-permute-done.16.late = bf16[512,1152]{1,0:T(8,128)(2,1)S(1)} collective-permute-done((bf16[512,1152]{1,0:T(8,128)(2,1)S(1)}, bf16[512,1152]{1,0:T(8,128)(2,1)S(1)}, u32[]{:S(2)}, u32[]{:S(2)}) %collective-permute-start.16) | collective-permute-done | bytes 1179680 | tf_op jit(solution)/shard_map/ppermute | solution.py:300
  106.2 1.7 %text.1 = (bf16[512,1152]{1,0:T(8,128)(2,1)}, f32[8,128]{1,0:T(8,128)S(1)}) custom-call(f32[512,1152]{1,0:T(8,128)S(1)} %text_base.1.base, f32[512,1152]{1,0:T(8,128)S(1)} %get-tuple-element.96.unit, f32[512,128]{1,0:T(8,128)S(1)} %copy-done.3, bf16[512,1152]{1,0:T(8,128)(2,1)S(1)} %collective-permute-done.16.late), custom_call_target="tpu_custom_call" | custom-call | flops 1000 | tf_op jit(solution)/shard_map/text/pallas_call | solution.py:280
  107.9 2.4 %image.1 = (bf16[512,1152]{1,0:T(8,128)(2,1)}, f32[1,512]{1,0:T(1,128)}) custom-call(f32[512,1152]{1,0:T(8,128)S(1)} %get-tuple-element.93.base, f32[8,512]{1,0:T(8,128)S(1)} %get-tuple-element.94.refs_2_.line, f32[512,1152]{1,0:T(8,128)S(1)} %get-tuple-element.95.unit, f32[512,128]{1,0:T(8,128)S(1)} %copy-done.1, ...), custom_call_target="tpu_custom_call" | custom-call | flops 1000 | tf_op jit(solution)/shard_map/image/pallas_call | solution.py:280
  (31 shorter events, 0.2 us)
Async XLA Ops:
  0.6 5.4 %copy-start.6 = (bf16[512,1152]{1,0:T(8,128)(2,1)S(1)}, bf16[512,1152]{1,0:T(8,128)(2,1)}, u32[]{:S(2)}) copy-start(bf16[512,1152]{1,0:T(8,128)(2,1)} %refs_1_.2) | copy-start | bytes 3538948
  0.6 1.4 %copy-start.7 = (bf16[512,1152]{1,0:T(8,128)(2,1)S(1)}, bf16[512,1152]{1,0:T(8,128)(2,1)}, u32[]{:S(2)}) copy-start(bf16[512,1152]{1,0:T(8,128)(2,1)} %refs_1_.3) | copy-start | bytes 3538948
  2.6 9.7 %collective-permute-start.3 = (bf16[512,1152]{1,0:T(8,128)(2,1)S(1)}, bf16[512,1152]{1,0:T(8,128)(2,1)S(1)}, u32[]{:S(2)}, u32[]{:S(2)}) collective-permute-start(bf16[512,1152]{1,0:T(8,128)(2,1)S(1)} %norm_text.1.refs_1_.refs_2_), channel_id=1, source_target_pairs={{0,1},{1,0},{2,3},{3,2},{4,5},{5,4},{6,7},{7,6},{8,9},{9,8},{10,11... | collective-permute-start | bytes 3538952 | tf_op jit(solution)/shard_map/ppermute | solution.py:300
  2.7 30.9 %collective-permute-start = (bf16[512,1152]{1,0:T(8,128)(2,1)S(1)}, bf16[512,1152]{1,0:T(8,128)(2,1)S(1)}, u32[]{:S(2)}, u32[]{:S(2)}) collective-permute-start(bf16[512,1152]{1,0:T(8,128)(2,1)S(1)} %norm_text.1.refs_1_.refs_2_), channel_id=1, source_target_pairs={{0,2},{1,3},{2,0},{3,1},{4,6},{5,7},{6,4},{7,5},{8,10},{9,11},{10,... | collective-permute-start | bytes 3538952 | tf_op jit(solution)/shard_map/ppermute | solution.py:300
  6.7 18.2 %collective-permute-start.1 = (bf16[256,1152]{1,0:T(8,128)(2,1)S(1)}, bf16[256,1152]{1,0:T(8,128)(2,1)S(1)}, u32[]{:S(2)}, u32[]{:S(2)}) collective-permute-start(bf16[256,1152]{1,0:T(8,128)(2,1)S(1)} %get-tuple-element.53.refs_0_), channel_id=1, source_target_pairs={{0,4},{1,5},{2,6},{3,7},{4,8},{5,9},{6,10},{7,11},{8,12},{9,13},{1... | collective-permute-start | bytes 1769480 | tf_op jit(solution)/shard_map/ppermute | solution.py:300
  8.7 16.2 %collective-permute-start.2 = (bf16[256,1152]{1,0:T(8,128)(2,1)S(1)}, bf16[256,1152]{1,0:T(8,128)(2,1)S(1)}, u32[]{:S(2)}, u32[]{:S(2)}) collective-permute-start(bf16[256,1152]{1,0:T(8,128)(2,1)S(1)} %get-tuple-element.54.refs_1_), channel_id=1, source_target_pairs={{0,12},{1,13},{2,14},{3,15},{4,0},{5,1},{6,2},{7,3},{8,4},{9,5},{1... | collective-permute-start | bytes 1769480 | tf_op jit(solution)/shard_map/ppermute | solution.py:300
  12.4 34.2 %collective-permute-start.6 = (bf16[256,1152]{1,0:T(8,128)(2,1)S(1)}, bf16[256,1152]{1,0:T(8,128)(2,1)S(1)}, u32[]{:S(2)}, u32[]{:S(2)}) collective-permute-start(bf16[256,1152]{1,0:T(8,128)(2,1)S(1)} %get-tuple-element.66), channel_id=1, source_target_pairs={{0,4},{1,5},{2,6},{3,7},{4,8},{5,9},{6,10},{7,11},{8,12},{9,13},{1... | collective-permute-start | bytes 1769480 | tf_op jit(solution)/shard_map/ppermute | solution.py:300
  12.5 36.8 %collective-permute-start.7 = (bf16[256,1152]{1,0:T(8,128)(2,1)S(1)}, bf16[256,1152]{1,0:T(8,128)(2,1)S(1)}, u32[]{:S(2)}, u32[]{:S(2)}) collective-permute-start(bf16[256,1152]{1,0:T(8,128)(2,1)S(1)} %get-tuple-element.55.refs_4_), channel_id=1, source_target_pairs={{0,12},{1,13},{2,14},{3,15},{4,0},{5,1},{6,2},{7,3},{8,4},{9,5},{1... | collective-permute-start | bytes 1769480 | tf_op jit(solution)/shard_map/ppermute | solution.py:300
  25.1 32.8 %collective-permute-start.11 = (bf16[256,1152]{1,0:T(8,128)(2,1)S(1)}, bf16[256,1152]{1,0:T(8,128)(2,1)S(1)}, u32[]{:S(2)}, u32[]{:S(2)}) collective-permute-start(bf16[256,1152]{1,0:T(8,128)(2,1)S(1)} %get-tuple-element.75), channel_id=1, source_target_pairs={{0,4},{1,5},{2,6},{3,7},{4,8},{5,9},{6,10},{7,11},{8,12},{9,13},{1... | collective-permute-start | bytes 1769480 | tf_op jit(solution)/shard_map/ppermute | solution.py:300
  27.1 34.0 %collective-permute-start.12 = (bf16[256,1152]{1,0:T(8,128)(2,1)S(1)}, bf16[256,1152]{1,0:T(8,128)(2,1)S(1)}, u32[]{:S(2)}, u32[]{:S(2)}) collective-permute-start(bf16[256,1152]{1,0:T(8,128)(2,1)S(1)} %get-tuple-element.76), channel_id=1, source_target_pairs={{0,12},{1,13},{2,14},{3,15},{4,0},{5,1},{6,2},{7,3},{8,4},{9,5},{1... | collective-permute-start | bytes 1769480 | tf_op jit(solution)/shard_map/ppermute | solution.py:300
  33.6 0.7 copy-start
  33.6 1.4 %copy-start.8 = (bf16[512,1152]{1,0:T(8,128)(2,1)S(1)}, bf16[512,1152]{1,0:T(8,128)(2,1)}, u32[]{:S(2)}) copy-start(bf16[512,1152]{1,0:T(8,128)(2,1)} %refs_1_.3) | copy-start | bytes 3538948
  34.3 2.8 %collective-permute-start.4 = (bf16[512,1152]{1,0:T(8,128)(2,1)S(1)}, bf16[512,1152]{1,0:T(8,128)(2,1)S(1)}, u32[]{:S(2)}, u32[]{:S(2)}) collective-permute-start(bf16[512,1152]{1,0:T(8,128)(2,1)S(1)} %hold_text.1.refs_2_), channel_id=1, source_target_pairs={{0,1},{1,0},{2,3},{3,2},{4,5},{5,4},{6,7},{7,6},{8,9},{9,8},{10,11... | collective-permute-start | bytes 3538952 | tf_op jit(solution)/shard_map/ppermute | solution.py:300
  36.1 5.4 %copy-start.2 = (f32[512,128]{1,0:T(8,128)}, f32[512,128]{1,0:T(8,128)S(1)}, u32[]{:S(2)}) copy-start(f32[512,128]{1,0:T(8,128)S(1)} %get-tuple-element.61.refs_6_.factor) | copy-start | bytes 786436
  41.5 4.5 %copy-start.4 = (f32[512,128]{1,0:T(8,128)}, f32[512,128]{1,0:T(8,128)S(1)}, u32[]{:S(2)}) copy-start(f32[512,128]{1,0:T(8,128)S(1)} %get-tuple-element.63.refs_6_.refs_1_) | copy-start | bytes 786436
  46.0 29.6 %collective-permute-start.9 = (bf16[272,1152]{1,0:T(8,128)(2,1)S(1)}, bf16[272,1152]{1,0:T(8,128)(2,1)S(1)}, u32[]{:S(2)}, u32[]{:S(2)}) collective-permute-start(bf16[272,1152]{1,0:T(8,128)(2,1)S(1)} %get-tuple-element.70), channel_id=1, source_target_pairs={{0,4},{1,5},{2,6},{3,7},{4,8},{5,9},{6,10},{7,11},{8,12},{9,13},{1... | collective-permute-start | bytes 1880072 | tf_op jit(solution)/shard_map/ppermute | solution.py:300
  46.6 29.3 %collective-permute-start.5 = (bf16[272,1152]{1,0:T(8,128)(2,1)S(1)}, bf16[272,1152]{1,0:T(8,128)(2,1)S(1)}, u32[]{:S(2)}, u32[]{:S(2)}) collective-permute-start(bf16[272,1152]{1,0:T(8,128)(2,1)S(1)} %get-tuple-element.65.refs_2_), channel_id=1, source_target_pairs={{0,12},{1,13},{2,14},{3,15},{4,0},{5,1},{6,2},{7,3},{8,4},{9,5},{1... | collective-permute-start | bytes 1880072 | tf_op jit(solution)/shard_map/ppermute | solution.py:300
  57.8 27.8 %collective-permute-start.8 = (bf16[272,1152]{1,0:T(8,128)(2,1)S(1)}, bf16[272,1152]{1,0:T(8,128)(2,1)S(1)}, u32[]{:S(2)}, u32[]{:S(2)}) collective-permute-start(bf16[272,1152]{1,0:T(8,128)(2,1)S(1)} %get-tuple-element.69), channel_id=1, source_target_pairs={{0,4},{1,5},{2,6},{3,7},{4,8},{5,9},{6,10},{7,11},{8,12},{9,13},{1... | collective-permute-start | bytes 1880072 | tf_op jit(solution)/shard_map/ppermute | solution.py:300
  57.9 27.7 %collective-permute-start.10 = (bf16[272,1152]{1,0:T(8,128)(2,1)S(1)}, bf16[272,1152]{1,0:T(8,128)(2,1)S(1)}, u32[]{:S(2)}, u32[]{:S(2)}) collective-permute-start(bf16[272,1152]{1,0:T(8,128)(2,1)S(1)} %get-tuple-element.71.refs_2_), channel_id=1, source_target_pairs={{0,12},{1,13},{2,14},{3,15},{4,0},{5,1},{6,2},{7,3},{8,4},{9,5},{1... | collective-permute-start | bytes 1880072 | tf_op jit(solution)/shard_map/ppermute | solution.py:300
  67.9 8.0 %collective-permute-start.13 = (bf16[512,1152]{1,0:T(8,128)(2,1)S(1)}, bf16[512,1152]{1,0:T(8,128)(2,1)S(1)}, u32[]{:S(2)}, u32[]{:S(2)}) collective-permute-start(bf16[512,1152]{1,0:T(8,128)(2,1)S(1)} %cols_yc.1.refs_8_), channel_id=1, source_target_pairs={{0,1},{1,0},{2,3},{3,2},{4,5},{5,4},{6,7},{7,6},{8,9},{9,8},{10,11... | collective-permute-start | bytes 3538952 | tf_op jit(solution)/shard_map/ppermute | solution.py:300
  75.6 32.3 %collective-permute-start.14 = (bf16[528,1152]{1,0:T(8,128)(2,1)S(1)}, bf16[528,1152]{1,0:T(8,128)(2,1)S(1)}, u32[]{:S(2)}, u32[]{:S(2)}) collective-permute-start(bf16[528,1152]{1,0:T(8,128)(2,1)S(1)} %get-tuple-element.92.refs_2_), channel_id=1, source_target_pairs={{0,8},{1,9},{2,10},{3,11},{4,12},{5,13},{6,14},{7,15},{8,0},{9,1},... | collective-permute-start | bytes 3649544 | tf_op jit(solution)/shard_map/ppermute | solution.py:300
  76.2 29.9 %collective-permute-start.16 = (bf16[512,1152]{1,0:T(8,128)(2,1)S(1)}, bf16[512,1152]{1,0:T(8,128)(2,1)S(1)}, u32[]{:S(2)}, u32[]{:S(2)}) collective-permute-start(bf16[512,1152]{1,0:T(8,128)(2,1)S(1)} %add_y.1.refs_8_), channel_id=1, source_target_pairs={{0,2},{1,3},{2,0},{3,1},{4,6},{5,7},{6,4},{7,5},{8,10},{9,11},{10,... | collective-permute-start | bytes 3538952 | tf_op jit(solution)/shard_map/ppermute | solution.py:300
  82.5 3.8 %collective-permute-start.15 = (bf16[512,1152]{1,0:T(8,128)(2,1)S(1)}, bf16[512,1152]{1,0:T(8,128)(2,1)S(1)}, u32[]{:S(2)}, u32[]{:S(2)}) collective-permute-start(bf16[512,1152]{1,0:T(8,128)(2,1)S(1)} %cols_c.1.refs_8_), channel_id=1, source_target_pairs={{0,1},{1,0},{2,3},{3,2},{4,5},{5,4},{6,7},{7,6},{8,9},{9,8},{10,11... | collective-permute-start | bytes 3538952 | tf_op jit(solution)/shard_map/ppermute | solution.py:300
  82.6 3.0 %copy-start.5 = (f32[512,128]{1,0:T(8,128)S(1)}, f32[512,128]{1,0:T(8,128)}, u32[]{:S(2)}) copy-start(f32[512,128]{1,0:T(8,128)} %copy-done.4) | copy-start | bytes 786436
  86.2 19.9 %copy-start.3 = (f32[512,128]{1,0:T(8,128)S(1)}, f32[512,128]{1,0:T(8,128)}, u32[]{:S(2)}) copy-start(f32[512,128]{1,0:T(8,128)} %copy-done.2) | copy-start | bytes 786436
  106.2 1.7 %copy-start.1 = (f32[512,128]{1,0:T(8,128)S(1)}, f32[512,128]{1,0:T(8,128)}, u32[]{:S(2)}) copy-start(f32[512,128]{1,0:T(8,128)} %copy-done) | copy-start | bytes 786436

commit v2 on v1

--- a/solution.py
+++ b/solution.py
@@ -111,11 +111,10 @@
     return jnp.sum(jnp.transpose(lanes), axis=0, keepdims=True)
 
 
-def rows_kernel(n_t, diag, state, scal, images, *refs):
+def rows_kernel(n_t, diag, state, finish, scal, images, *refs):
     texts, refs = refs[:n_t], refs[n_t:]
     given, refs = (refs[:2], refs[2:]) if state else (None, refs)
     w_outs, refs = refs[:n_t], refs[n_t:]
-    sums, lanes = refs[-2:]
     half = images.shape[0] // 2
     scale, bias = scal[0], scal[1]
     steps = [(j, c) for j in range(n_t) for c in range(0, texts[j].shape[0], STEP)]
@@ -149,27 +148,37 @@
             w_outs[j][mine, c : c + STEP] = ready
             loss = lane if loss is None else loss + lane
             logits = following
-        sums[mine, :] = acc + jnp.dot(ready, text(steps[-1]), preferred_element_type=F32)
-        lanes[mine, :] = loss
+        acc = acc + jnp.dot(ready, text(steps[-1]), preferred_element_type=F32)
+        if finish == 2:
+            for i, out in enumerate(refs):
+
+                @pl.when(k == i)
+                def _(out=out):
+                    out[:half, :] = acc.astype(BF)
+                    out[half:, :] = loss_rows_of(line_of(loss), acc.shape[1])
+
+        elif finish == 1:
+            refs[0][mine, :] = acc.astype(BF)
+            refs[1][mine, :] = loss
+        else:
+            refs[0][mine, :] = acc
+            refs[1][mine, :] = loss
         return none
 
     lax.fori_loop(0, 2, body, None)
-    for k, out in enumerate(refs[:-2]):
-        rows = out.shape[0] - PAD
-        mine = slice(k * rows, (k + 1) * rows)
-        out[:rows, :] = sums[mine, :].astype(BF)
-        out[rows:, :] = loss_rows_of(line_of(lanes[mine, :]), sums.shape[1])
+    if finish == 1:
+        refs[0][2 * half :, :] = loss_rows_of(line_of(refs[1][...]), images.shape[1])
 
 
 def rows_step(name, scal, images, texts, state=(), diag=False, finish=0, after=()):
     rows, width = images.shape
     grads = [((rows, width), F32), ((rows, 128), F32)]
     if finish:
-        outs, scratch = [((rows // finish + PAD, width), BF)] * finish, grads
+        outs, scratch = [((rows // finish + PAD, width), BF)] * finish, grads[1:] if finish == 1 else []
     else:
         outs, scratch = grads, []
     outs = call(
-        functools.partial(rows_kernel, len(texts), diag, bool(state)),
+        functools.partial(rows_kernel, len(texts), diag, bool(state), finish),
         name,
         [scal, images, *texts, *state],
         [pltpu.VMEM((rows, t.shape[0]), BF) for t in texts] + [pltpu.VMEM(*g) for g in outs],
@@ -264,15 +273,15 @@
     pltpu.make_async_copy(buf, out, sem).wait()
 
 
-def image_kernel(count, base, line, unit, factor, late, done, grad_ref, loss_ref, buf, sem):
+def image_kernel(count, base, line, unit, factor, late, ready, grad_ref, loss_ref, done, buf, sem):
     rows = base.shape[0]
+    done[...] = jnp.zeros(done.shape, F32)
     tail = jnp.sum(late[rows:, :rows].astype(F32), axis=0, keepdims=True)
     loss_ref[...] = (line[:1, :] + tail) * (1.0 / count)
     tangent_rows(base, late, unit, factor, grad_ref, buf, sem)
 
 
-def text_kernel(base, unit, factor, late, grad_ref, done, buf, sem):
-    done[...] = jnp.zeros(done.shape, F32)
+def text_kernel(base, unit, factor, late, done, grad_ref, buf, sem):
     tangent_rows(base, late, unit, factor, grad_ref, buf, sem)
 
 
@@ -302,10 +311,11 @@
     rows, width = image_embeds.shape
     scale = jnp.exp(log_scale[0])
     scal = jnp.stack([scale * (1.0 / math.log(2.0)), bias[0] * (1.0 / math.log(2.0)), scale])
-    (txt,) = normalize(text_embeds, "norm_text", False)
-    txt_y, txt_c = move(txt, dy=1), move(txt, dc=1)
-    own, a, b = normalize(image_embeds, "norm_image", True, after=[txt])
+    raw_y, raw_c = move(text_embeds, dy=1), move(text_embeds, dc=1)
+    own, a, b = normalize(image_embeds, "norm_image", True)
     prev_a, next_b = move(a, dz=1), move(b, dz=-1)
+    (txt,) = normalize(text_embeds, "norm_text", False, after=[a])
+    (txt_c,) = normalize(raw_c, "norm_c", False, after=[txt])
     a, b = hold("hold_last", [a, b], [txt_c])
     prev_b, next_a = move(b, dz=1), move(a, dz=-1)
     near_t = [txt, txt_c]
@@ -313,18 +323,18 @@
     first, prev_a, next_b = merge("merge_first", prev_a, next_b, s_own[1:], copies=True)
     far_a, far_b = move(prev_a, dz=1), move(next_b, dz=-1)
     (first_0, first_c), s_first = rows_step("first_c", scal, first, near_t)
-    i_unit, i_factor = prepare(scal, image_embeds, "prep_image", s_first[1:])
-    (txt_y,) = hold("hold_text", [txt_y], [i_factor])
+    (txt_y,) = normalize(raw_y, "norm_y", False, after=s_first[1:])
     far_t = [txt_y, move(txt_y, dc=1)]
-    t_unit, t_factor = prepare(scal, text_embeds, "prep_text", [txt_y])
-    (own_y, own_yc), s_own = rows_step("own_y", scal, own, far_t, s_own, after=[t_factor])
+    (last,) = merge("merge_last", prev_b, next_a, [txt_y])
+    (last_0, last_c), s_last = rows_step("last_c", scal, last, near_t)
+    (own_y, own_yc), s_own = rows_step("own_y", scal, own, far_t, s_own, after=s_last[1:])
     (first_y, first_yc), (g_prev_a, g_next_b) = rows_step(
         "first_y", scal, first, far_t, s_first, finish=2, after=s_own[1:]
     )
     home_a0, home_b0 = move(g_prev_a, dz=-1), move(g_next_b, dz=1)
-    (last,) = merge("merge_last", prev_b, next_a, [g_prev_a])
-    (last_0, last_c), s_last = rows_step("last_c", scal, last, near_t)
-    (last_y, last_yc), (g_prev_b, g_next_a) = rows_step("last_y", scal, last, far_t, s_last, finish=2)
+    (last_y, last_yc), (g_prev_b, g_next_a) = rows_step(
+        "last_y", scal, last, far_t, s_last, finish=2, after=[g_prev_a]
+    )
     home_b1, home_a1 = move(g_prev_b, dz=-1), move(g_next_a, dz=1)
     (far,) = merge("merge_far", far_a, far_b, [g_prev_b])
     (far_y, far_yc), s_far = rows_step("far_y", scal, far, far_t)
@@ -352,16 +362,16 @@
     (t_base,) = call(
         text_base_kernel, "text_base", [gt_own, text_c], [pltpu.VMEM((rows, width), F32)], [line], cost=1000
     )
-    grad_text, done = final(
-        text_kernel, "text", [t_base, t_unit, t_factor, text_y], (rows, width), [pltpu.VMEM((8, 128), F32)]
-    )
-    grad_image, loss = final(
+    i_unit, i_factor = prepare(scal, image_embeds, "prep_image", [t_base])
+    t_unit, t_factor = prepare(scal, text_embeds, "prep_text", [i_factor])
+    grad_image, loss, done = final(
         functools.partial(image_kernel, total),
         "image",
-        [i_base, line, i_unit, i_factor, home_far, done],
+        [i_base, line, i_unit, i_factor, home_far, t_factor],
         (rows, width),
-        [jax.ShapeDtypeStruct((1, rows), F32)],
-    )
+        [jax.ShapeDtypeStruct((1, rows), F32), pltpu.VMEM((8, 128), F32)],
+    )
+    (grad_text,) = final(text_kernel, "text", [t_base, t_unit, t_factor, text_y, done], (rows, width), [])
     return loss.reshape(rows), grad_image, grad_text
 
 

time: 111 us -> 117 us (1.054)
  waiting for transfers between devices: 25.9 us -> 34.1 us
  starting transfers between devices: 24.8 us -> 22.1 us
    ppermute x17, waiting for transfers between devices: 25.9 us -> 34.1 us  [move(): return lax.ppermute(value, 'loss', pairs)]
    ppermute x17, starting transfers between devices: 24.8 us -> 22.1 us  [move(): return lax.ppermute(value, 'loss', pairs)]
    pallas_call x24 -> x25, Pallas kernels: 50.4 us -> 51.2 us  [call(): pl.pallas_call(body, name=name, in_specs=specs, out_specs=[VMEM] * len(ou...]
    unnamed x18 -> x12, local copies, waits for them, and re-layouts: 2.66 us -> 2.44 us
  transfers between devices with their start and end apart: 17 -> 17, of which waited for: 3 -> 4; matrix products, arithmetic and copies ran while one was open for 0% -> 0% of each run, Pallas kernels for 47% -> 46%
where the time goes in v2:
time: 117 us; the launch traced here: 116 us
  Pallas kernels  55.2 us (47%)
  waiting for transfers between devices  34.1 us (29%)
  starting transfers between devices  22.1 us (19%)
  between operations  2.48 us (2%)
  local copies, waits for them, and re-layouts  2.44 us (2%)
    pallas_call x25, Pallas kernels, call(): pl.pallas_call(body, name=name, in_specs=specs, out_specs=[VMEM] * len(ou...  51.2 us
    ppermute x17, waiting for transfers between devices, move(): return lax.ppermute(value, 'loss', pairs)  34.1 us
    ppermute x17, starting transfers between devices, move(): return lax.ppermute(value, 'loss', pairs)  22.1 us
    pallas_call x2, Pallas kernels, final(): pl.pallas_call(kernel, name=name, in_specs=[VMEM] * len(inputs), out_spec...  4.04 us
    unnamed x12, local copies, waits for them, and re-layouts  2.44 us
  transfers between devices with their start and end apart: 17, of which 4 were waited for; matrix products, arithmetic and copies ran while one was open for 0% of the time, Pallas kernels for 46%

profile of v2, /device:TPU:0, one launch (start us, length us, event | category | flops | bytes accessed | tf_op | source)
XLA Modules:
  0.0 116.4 jit_solution(4726315481535123820)
XLA Ops:
  0.6 3.4 %collective-permute-start = (bf16[512,1152]{1,0:T(8,128)(2,1)}, bf16[512,1152]{1,0:T(8,128)(2,1)S(1)}, u32[]{:S(2)}, u32[]{:S(2)}) collective-permute-start(bf16[512,1152]{1,0:T(8,128)(2,1)} %refs_1_.3), channel_id=1, source_target_pairs={{0,2},{1,3},{2,0},{3,1},{4,6},{5,7},{6,4},{7,5},{8,10},{9,11},{10,... | collective-permute-start | bytes 3538952 | tf_op jit(solution)/shard_map/ppermute | solution.py:309
  4.0 1.3 %copy-done.2 = bf16[512,1152]{1,0:T(8,128)(2,1)S(1)} copy-done((bf16[512,1152]{1,0:T(8,128)(2,1)S(1)}, bf16[512,1152]{1,0:T(8,128)(2,1)}, u32[]{:S(2)}) %copy-start.2) | copy-done | bytes 1179672
  5.3 0.7 norm_image.1
  5.9 4.1 %collective-permute-start.2 = (bf16[256,1152]{1,0:T(8,128)(2,1)S(1)}, bf16[256,1152]{1,0:T(8,128)(2,1)S(1)}, u32[]{:S(2)}, u32[]{:S(2)}) collective-permute-start(bf16[256,1152]{1,0:T(8,128)(2,1)S(1)} %get-tuple-element.53.refs_1_), channel_id=1, source_target_pairs={{0,12},{1,13},{2,14},{3,15},{4,0},{5,1},{6,2},{7,3},{8,4},{9,5},{1... | collective-permute-start | bytes 1769480 | tf_op jit(solution)/shard_map/ppermute | solution.py:309
  11.4 0.6 norm_text.1.refs_1_.refs_2_
  12.0 0.6 norm_c.1.refs_2_.refs_3_
  12.6 0.1 pad_maximum_fusion.refs_0_
  12.7 0.1 hold_last.1
  12.8 0.1 collective-permute-start.5
  12.9 3.3 %collective-permute-start.6 = (bf16[256,1152]{1,0:T(8,128)(2,1)S(1)}, bf16[256,1152]{1,0:T(8,128)(2,1)S(1)}, u32[]{:S(2)}, u32[]{:S(2)}) collective-permute-start(bf16[256,1152]{1,0:T(8,128)(2,1)S(1)} %get-tuple-element.54.refs_4_), channel_id=1, source_target_pairs={{0,12},{1,13},{2,14},{3,15},{4,0},{5,1},{6,2},{7,3},{8,4},{9,5},{1... | collective-permute-start | bytes 1769480 | tf_op jit(solution)/shard_map/ppermute | solution.py:309
  16.2 4.0 %own_c.1 = (bf16[512,512]{1,0:T(8,128)(2,1)S(1)}, bf16[512,512]{1,0:T(8,128)(2,1)S(1)}, f32[512,1152]{1,0:T(8,128)S(1)}, f32[512,128]{1,0:T(8,128)S(1)}) custom-call(f32[3]{0:T(128)S(1)} %pad_maximum_fusion.refs_0_, bf16[512,1152]{1,0:T(8,128)(2,1)S(1)} %get-tuple-element.51.refs_1_.refs_4_, bf16[512,1152]{1,0:T(8,128)(2,1)S(1)} %norm_text.1.refs_1_.refs_2_, ...), custom_call_target="tpu_custom_call" | custom-call | flops 20000000000 | tf_op jit(solution)/shard_map/own_c/pallas_call | solution.py:30
  20.2 3.5 %collective-permute-done.2.refs_1_ = bf16[256,1152]{1,0:T(8,128)(2,1)S(1)} collective-permute-done((bf16[256,1152]{1,0:T(8,128)(2,1)S(1)}, bf16[256,1152]{1,0:T(8,128)(2,1)S(1)}, u32[]{:S(2)}, u32[]{:S(2)}) %collective-permute-start.2) | collective-permute-done | bytes 589856 | tf_op jit(solution)/shard_map/ppermute | solution.py:309
  23.7 3.7 %collective-permute-done.1.refs_0_ = bf16[256,1152]{1,0:T(8,128)(2,1)S(1)} collective-permute-done((bf16[256,1152]{1,0:T(8,128)(2,1)S(1)}, bf16[256,1152]{1,0:T(8,128)(2,1)S(1)}, u32[]{:S(2)}, u32[]{:S(2)}) %collective-permute-start.1) | collective-permute-done | bytes 589856 | tf_op jit(solution)/shard_map/ppermute | solution.py:309
  27.4 0.2 merge_first.1
  27.7 3.2 %collective-permute-start.12 = (bf16[256,1152]{1,0:T(8,128)(2,1)S(1)}, bf16[256,1152]{1,0:T(8,128)(2,1)S(1)}, u32[]{:S(2)}, u32[]{:S(2)}) collective-permute-start(bf16[256,1152]{1,0:T(8,128)(2,1)S(1)} %get-tuple-element.73), channel_id=1, source_target_pairs={{0,12},{1,13},{2,14},{3,15},{4,0},{5,1},{6,2},{7,3},{8,4},{9,5},{1... | collective-permute-start | bytes 1769480 | tf_op jit(solution)/shard_map/ppermute | solution.py:309
  30.9 3.7 %first_c.1 = (bf16[512,512]{1,0:T(8,128)(2,1)S(1)}, bf16[512,512]{1,0:T(8,128)(2,1)S(1)}, f32[512,1152]{1,0:T(8,128)S(1)}, f32[512,128]{1,0:T(8,128)S(1)}) custom-call(f32[3]{0:T(128)S(1)} %pad_maximum_fusion.refs_0_, bf16[512,1152]{1,0:T(8,128)(2,1)S(1)} %get-tuple-element.56.refs_1_.refs_5_, bf16[512,1152]{1,0:T(8,128)(2,1)S(1)} %norm_text.1.refs_1_.refs_2_, ...), custom_call_target="tpu_custom_call" | custom-call | flops 20000000000 | tf_op jit(solution)/shard_map/first_c/pallas_call | solution.py:30
  34.6 0.6 norm_y.1.refs_2_
  35.2 0.1 collective-permute-start.4
  35.3 4.8 %collective-permute-done.5.refs_0_ = bf16[256,1152]{1,0:T(8,128)(2,1)S(1)} collective-permute-done((bf16[256,1152]{1,0:T(8,128)(2,1)S(1)}, bf16[256,1152]{1,0:T(8,128)(2,1)S(1)}, u32[]{:S(2)}, u32[]{:S(2)}) %collective-permute-start.5) | collective-permute-done | bytes 589856 | tf_op jit(solution)/shard_map/ppermute | solution.py:309
  40.1 0.1 merge_last.1.refs_1_.refs_6_
  40.2 3.7 %last_c.1 = (bf16[512,512]{1,0:T(8,128)(2,1)S(1)}, bf16[512,512]{1,0:T(8,128)(2,1)S(1)}, f32[512,1152]{1,0:T(8,128)S(1)}, f32[512,128]{1,0:T(8,128)S(1)}) custom-call(f32[3]{0:T(128)S(1)} %pad_maximum_fusion.refs_0_, bf16[512,1152]{1,0:T(8,128)(2,1)S(1)} %merge_last.1.refs_1_.refs_6_, bf16[512,1152]{1,0:T(8,128)(2,1)S(1)} %norm_text.1.refs_1_.refs_2_, ...), custom_call_target="tpu_custom_call" | custom-call | flops 20000000000 | tf_op jit(solution)/shard_map/last_c/pallas_call | solution.py:30
  43.9 4.3 %own_y.1 = (bf16[512,512]{1,0:T(8,128)(2,1)S(1)}, bf16[512,512]{1,0:T(8,128)(2,1)S(1)}, f32[512,1152]{1,0:T(8,128)S(1)}, f32[512,128]{1,0:T(8,128)S(1)}) custom-call(f32[3]{0:T(128)S(1)} %pad_maximum_fusion.refs_0_, bf16[512,1152]{1,0:T(8,128)(2,1)S(1)} %get-tuple-element.51.refs_1_.refs_4_, bf16[512,1152]{1,0:T(8,128)(2,1)S(1)} %norm_y.1.refs_2_, ...), custom_call_target="tpu_custom_call" | custom-call | flops 20000000000 | tf_op jit(solution)/shard_map/own_y/pallas_call | solution.py:30
  48.2 4.6 %first_y.1 = (bf16[512,512]{1,0:T(8,128)(2,1)S(1)}, bf16[512,512]{1,0:T(8,128)(2,1)S(1)}, bf16[272,1152]{1,0:T(8,128)(2,1)S(1)}, bf16[272,1152]{1,0:T(8,128)(2,1)S(1)}) custom-call(f32[3]{0:T(128)S(1)} %pad_maximum_fusion.refs_0_, bf16[512,1152]{1,0:T(8,128)(2,1)S(1)} %get-tuple-element.56.refs_1_.refs_5_, bf16[512,1152]{1,0:T(8,128)(2,1)S(1)} %norm_y.1.refs_2_, ...), custom_call_target="tpu_custom_call" | custom-call | flops 20000000000 | tf_op jit(solution)/shard_map/first_y/pallas_call | solution.py:30
  52.8 0.3 collective-permute-start.9
  53.1 3.2 %collective-permute-start.7 = (bf16[272,1152]{1,0:T(8,128)(2,1)S(1)}, bf16[272,1152]{1,0:T(8,128)(2,1)S(1)}, u32[]{:S(2)}, u32[]{:S(2)}) collective-permute-start(bf16[272,1152]{1,0:T(8,128)(2,1)S(1)} %get-tuple-element.64.refs_6_), channel_id=1, source_target_pairs={{0,12},{1,13},{2,14},{3,15},{4,0},{5,1},{6,2},{7,3},{8,4},{9,5},{1... | collective-permute-start | bytes 1880072 | tf_op jit(solution)/shard_map/ppermute | solution.py:309
  56.3 4.6 %last_y.1 = (bf16[512,512]{1,0:T(8,128)(2,1)S(1)}, bf16[512,512]{1,0:T(8,128)(2,1)S(1)}, bf16[272,1152]{1,0:T(8,128)(2,1)S(1)}, bf16[272,1152]{1,0:T(8,128)(2,1)S(1)}) custom-call(f32[3]{0:T(128)S(1)} %pad_maximum_fusion.refs_0_, bf16[512,1152]{1,0:T(8,128)(2,1)S(1)} %merge_last.1.refs_1_.refs_6_, bf16[512,1152]{1,0:T(8,128)(2,1)S(1)} %norm_y.1.refs_2_, ...), custom_call_target="tpu_custom_call" | custom-call | flops 20000000000 | tf_op jit(solution)/shard_map/last_y/pallas_call | solution.py:30
  61.0 3.2 %collective-permute-start.10 = (bf16[272,1152]{1,0:T(8,128)(2,1)S(1)}, bf16[272,1152]{1,0:T(8,128)(2,1)S(1)}, u32[]{:S(2)}, u32[]{:S(2)}) collective-permute-start(bf16[272,1152]{1,0:T(8,128)(2,1)S(1)} %get-tuple-element.68.refs_2_), channel_id=1, source_target_pairs={{0,12},{1,13},{2,14},{3,15},{4,0},{5,1},{6,2},{7,3},{8,4},{9,5},{1... | collective-permute-start | bytes 1880072 | tf_op jit(solution)/shard_map/ppermute | solution.py:309
  64.2 0.1 merge_far.1.refs_1_.refs_7_
  64.3 3.8 %far_y.1 = (bf16[512,512]{1,0:T(8,128)(2,1)S(1)}, bf16[512,512]{1,0:T(8,128)(2,1)S(1)}, f32[512,1152]{1,0:T(8,128)S(1)}, f32[512,128]{1,0:T(8,128)S(1)}) custom-call(f32[3]{0:T(128)S(1)} %pad_maximum_fusion.refs_0_, bf16[512,1152]{1,0:T(8,128)(2,1)S(1)} %merge_far.1.refs_1_.refs_7_, bf16[512,1152]{1,0:T(8,128)(2,1)S(1)} %norm_y.1.refs_2_, ...), custom_call_target="tpu_custom_call" | custom-call | flops 20000000000 | tf_op jit(solution)/shard_map/far_y/pallas_call | solution.py:30
  68.1 2.9 %cols_yc.1.refs_8_ = bf16[512,1152]{1,0:T(8,128)(2,1)S(1)} custom-call(bf16[512,512]{1,0:T(8,128)(2,1)S(1)} %get-tuple-element.80.refs_0_, bf16[512,512]{1,0:T(8,128)(2,1)S(1)} %get-tuple-element.81.refs_1_, bf16[512,512]{1,0:T(8,128)(2,1)S(1)} %get-tuple-element.82.refs_2_, bf16[512,512]{1,0:T(8,128)(2,1)S(1)} %get-tuple-element.83.refs_3_, ...), custom_call_target="tpu_custom_call" | custom-call | flops 20000000000 | tf_op jit(solution)/shard_map/cols_yc/pallas_call | solution.py:30
  71.0 0.1 collective-permute-start.13
  71.1 3.0 %cols_y.1.refs_6_.refs_0_ = f32[512,1152]{1,0:T(8,128)S(1)} custom-call(bf16[512,512]{1,0:T(8,128)(2,1)S(1)} %get-tuple-element.76.refs_0_, bf16[512,512]{1,0:T(8,128)(2,1)S(1)} %get-tuple-element.77.refs_1_, bf16[512,512]{1,0:T(8,128)(2,1)S(1)} %get-tuple-element.78.refs_2_, bf16[512,512]{1,0:T(8,128)(2,1)S(1)} %get-tuple-element.79.refs_3_, ...), custom_call_target="tpu_custom_call" | custom-call | flops 20000000000 | tf_op jit(solution)/shard_map/cols_y/pallas_call | solution.py:30
  74.1 4.5 %far_c.1 = (bf16[512,512]{1,0:T(8,128)(2,1)S(1)}, bf16[512,512]{1,0:T(8,128)(2,1)S(1)}, bf16[528,1152]{1,0:T(8,128)(2,1)S(1)}) custom-call(f32[3]{0:T(128)S(1)} %pad_maximum_fusion.refs_0_, bf16[512,1152]{1,0:T(8,128)(2,1)S(1)} %merge_far.1.refs_1_.refs_7_, bf16[512,1152]{1,0:T(8,128)(2,1)S(1)} %norm_text.1.refs_1_.refs_2_, ...), custom_call_target="tpu_custom_call" | custom-call | flops 20000000000 | tf_op jit(solution)/shard_map/far_c/pallas_call | solution.py:30
  78.6 0.1 collective-permute-start.15
  78.7 0.3 add_y.1.refs_8_
  78.9 0.6 collective-permute-start.16
  79.6 2.9 %cols_c.1.refs_8_ = bf16[512,1152]{1,0:T(8,128)(2,1)S(1)} custom-call(bf16[512,512]{1,0:T(8,128)(2,1)S(1)} %get-tuple-element.85.refs_0_, bf16[512,512]{1,0:T(8,128)(2,1)S(1)} %get-tuple-element.86.refs_1_, bf16[512,512]{1,0:T(8,128)(2,1)S(1)} %get-tuple-element.87.refs_2_, bf16[512,512]{1,0:T(8,128)(2,1)S(1)} %get-tuple-element.88.refs_3_, ...), custom_call_target="tpu_custom_call" | custom-call | flops 20000000000 | tf_op jit(solution)/shard_map/cols_c/pallas_call | solution.py:30
  82.5 0.3 collective-permute-start.14
  82.8 2.9 %cols_own.1.refs_6_.refs_0_ = f32[512,1152]{1,0:T(8,128)S(1)} custom-call(bf16[512,512]{1,0:T(8,128)(2,1)S(1)} %get-tuple-element.69.refs_0_, bf16[512,512]{1,0:T(8,128)(2,1)S(1)} %get-tuple-element.70.refs_1_, bf16[512,512]{1,0:T(8,128)(2,1)S(1)} %get-tuple-element.71.refs_2_, bf16[512,512]{1,0:T(8,128)(2,1)S(1)} %get-tuple-element.84.refs_3_, ...), custom_call_target="tpu_custom_call" | custom-call | flops 20000000000 | tf_op jit(solution)/shard_map/cols_own/pallas_call | solution.py:30
  85.7 22.0 %collective-permute-done.10.refs_5_ = bf16[272,1152]{1,0:T(8,128)(2,1)S(1)} collective-permute-done((bf16[272,1152]{1,0:T(8,128)(2,1)S(1)}, bf16[272,1152]{1,0:T(8,128)(2,1)S(1)}, u32[]{:S(2)}, u32[]{:S(2)}) %collective-permute-start.10) | collective-permute-done | bytes 626720 | tf_op jit(solution)/shard_map/ppermute | solution.py:309
  107.8 0.6 image_base.1
  108.4 0.3 text_base.1.refs_2_.base
  108.7 1.0 copy-done.3
  109.7 1.1 prep_image.1
  110.8 0.1 copy-done.5
  111.0 1.1 prep_text.1
  112.1 2.4 %image.1 = (bf16[512,1152]{1,0:T(8,128)(2,1)}, f32[1,512]{1,0:T(1,128)}, f32[8,128]{1,0:T(8,128)S(1)}) custom-call(f32[512,1152]{1,0:T(8,128)S(1)} %get-tuple-element.90.base, f32[8,512]{1,0:T(8,128)S(1)} %get-tuple-element.91.refs_2_.line, f32[512,1152]{1,0:T(8,128)S(1)} %get-tuple-element.92.unit, f32[512,128]{1,0:T(8,128)S(1)} %get-tuple-element.93.refs_2_.factor, ...), custom_call_target="tpu_custom_call" | custom-call | flops 1000 | tf_op jit(solution)/shard_map/image/pallas_call | solution.py:289
  114.5 1.7 %text.1 = bf16[512,1152]{1,0:T(8,128)(2,1)} custom-call(f32[512,1152]{1,0:T(8,128)S(1)} %text_base.1.refs_2_.base, f32[512,1152]{1,0:T(8,128)S(1)} %get-tuple-element.97.unit, f32[512,128]{1,0:T(8,128)S(1)} %get-tuple-element.94.ready.factor, bf16[512,1152]{1,0:T(8,128)(2,1)S(1)} %collective-permute-done.16.late, f32[8,128]{1,0:T(8,128)S(1)} %get-tuple-element.98.done), custom_call_target="tpu_custom_call" | custom-call | flops 1000 | tf_op jit(solution)/shard_map/text/pallas_call | solution.py:289
  (26 shorter events, 0.2 us)
Async XLA Ops:
  0.6 34.0 %collective-permute-start = (bf16[512,1152]{1,0:T(8,128)(2,1)}, bf16[512,1152]{1,0:T(8,128)(2,1)S(1)}, u32[]{:S(2)}, u32[]{:S(2)}) collective-permute-start(bf16[512,1152]{1,0:T(8,128)(2,1)} %refs_1_.3), channel_id=1, source_target_pairs={{0,2},{1,3},{2,0},{3,1},{4,6},{5,7},{6,4},{7,5},{8,10},{9,11},{10,... | collective-permute-start | bytes 3538952 | tf_op jit(solution)/shard_map/ppermute | solution.py:309
  4.0 8.0 %collective-permute-start.3 = (bf16[512,1152]{1,0:T(8,128)(2,1)}, bf16[512,1152]{1,0:T(8,128)(2,1)S(1)}, u32[]{:S(2)}, u32[]{:S(2)}) collective-permute-start(bf16[512,1152]{1,0:T(8,128)(2,1)} %refs_1_.3), channel_id=1, source_target_pairs={{0,1},{1,0},{2,3},{3,2},{4,5},{5,4},{6,7},{7,6},{8,9},{9,8},{10,11... | collective-permute-start | bytes 3538952 | tf_op jit(solution)/shard_map/ppermute | solution.py:309
  4.0 1.3 %copy-start.2 = (bf16[512,1152]{1,0:T(8,128)(2,1)S(1)}, bf16[512,1152]{1,0:T(8,128)(2,1)}, u32[]{:S(2)}) copy-start(bf16[512,1152]{1,0:T(8,128)(2,1)} %refs_1_.2) | copy-start | bytes 3538948
  5.3 6.1 %copy-start.4 = (bf16[512,1152]{1,0:T(8,128)(2,1)S(1)}, bf16[512,1152]{1,0:T(8,128)(2,1)}, u32[]{:S(2)}) copy-start(bf16[512,1152]{1,0:T(8,128)(2,1)} %refs_1_.3) | copy-start | bytes 3538948
  5.9 17.7 %collective-permute-start.2 = (bf16[256,1152]{1,0:T(8,128)(2,1)S(1)}, bf16[256,1152]{1,0:T(8,128)(2,1)S(1)}, u32[]{:S(2)}, u32[]{:S(2)}) collective-permute-start(bf16[256,1152]{1,0:T(8,128)(2,1)S(1)} %get-tuple-element.53.refs_1_), channel_id=1, source_target_pairs={{0,12},{1,13},{2,14},{3,15},{4,0},{5,1},{6,2},{7,3},{8,4},{9,5},{1... | collective-permute-start | bytes 1769480 | tf_op jit(solution)/shard_map/ppermute | solution.py:309
  10.0 17.4 %collective-permute-start.1 = (bf16[256,1152]{1,0:T(8,128)(2,1)S(1)}, bf16[256,1152]{1,0:T(8,128)(2,1)S(1)}, u32[]{:S(2)}, u32[]{:S(2)}) collective-permute-start(bf16[256,1152]{1,0:T(8,128)(2,1)S(1)} %get-tuple-element.52.refs_1_.refs_0_), channel_id=1, source_target_pairs={{0,4},{1,5},{2,6},{3,7},{4,8},{5,9},{6,10},{7,11},{8,12},{9,13},{1... | collective-permute-start | bytes 1769480 | tf_op jit(solution)/shard_map/ppermute | solution.py:309
  12.8 27.3 %collective-permute-start.5 = (bf16[256,1152]{1,0:T(8,128)(2,1)S(1)}, bf16[256,1152]{1,0:T(8,128)(2,1)S(1)}, u32[]{:S(2)}, u32[]{:S(2)}) collective-permute-start(bf16[256,1152]{1,0:T(8,128)(2,1)S(1)} %get-tuple-element.59), channel_id=1, source_target_pairs={{0,4},{1,5},{2,6},{3,7},{4,8},{5,9},{6,10},{7,11},{8,12},{9,13},{1... | collective-permute-start | bytes 1769480 | tf_op jit(solution)/shard_map/ppermute | solution.py:309
  12.9 27.2 %collective-permute-start.6 = (bf16[256,1152]{1,0:T(8,128)(2,1)S(1)}, bf16[256,1152]{1,0:T(8,128)(2,1)S(1)}, u32[]{:S(2)}, u32[]{:S(2)}) collective-permute-start(bf16[256,1152]{1,0:T(8,128)(2,1)S(1)} %get-tuple-element.54.refs_4_), channel_id=1, source_target_pairs={{0,12},{1,13},{2,14},{3,15},{4,0},{5,1},{6,2},{7,3},{8,4},{9,5},{1... | collective-permute-start | bytes 1769480 | tf_op jit(solution)/shard_map/ppermute | solution.py:309
  27.6 33.4 %collective-permute-start.11 = (bf16[256,1152]{1,0:T(8,128)(2,1)S(1)}, bf16[256,1152]{1,0:T(8,128)(2,1)S(1)}, u32[]{:S(2)}, u32[]{:S(2)}) collective-permute-start(bf16[256,1152]{1,0:T(8,128)(2,1)S(1)} %get-tuple-element.72), channel_id=1, source_target_pairs={{0,4},{1,5},{2,6},{3,7},{4,8},{5,9},{6,10},{7,11},{8,12},{9,13},{1... | collective-permute-start | bytes 1769480 | tf_op jit(solution)/shard_map/ppermute | solution.py:309
  27.7 36.5 %collective-permute-start.12 = (bf16[256,1152]{1,0:T(8,128)(2,1)S(1)}, bf16[256,1152]{1,0:T(8,128)(2,1)S(1)}, u32[]{:S(2)}, u32[]{:S(2)}) collective-permute-start(bf16[256,1152]{1,0:T(8,128)(2,1)S(1)} %get-tuple-element.73), channel_id=1, source_target_pairs={{0,12},{1,13},{2,14},{3,15},{4,0},{5,1},{6,2},{7,3},{8,4},{9,5},{1... | collective-permute-start | bytes 1769480 | tf_op jit(solution)/shard_map/ppermute | solution.py:309
  35.2 8.7 %collective-permute-start.4 = (bf16[512,1152]{1,0:T(8,128)(2,1)S(1)}, bf16[512,1152]{1,0:T(8,128)(2,1)S(1)}, u32[]{:S(2)}, u32[]{:S(2)}) collective-permute-start(bf16[512,1152]{1,0:T(8,128)(2,1)S(1)} %norm_y.1.refs_2_), channel_id=1, source_target_pairs={{0,1},{1,0},{2,3},{3,2},{4,5},{5,4},{6,7},{7,6},{8,9},{9,8},{10,11... | collective-permute-start | bytes 3538952 | tf_op jit(solution)/shard_map/ppermute | solution.py:309
  48.2 4.6 %copy-start = (f32[512,128]{1,0:T(8,128)}, f32[512,128]{1,0:T(8,128)S(1)}, u32[]{:S(2)}) copy-start(f32[512,128]{1,0:T(8,128)S(1)} %get-tuple-element.62.refs_6_.refs_1_) | copy-start | bytes 786436
  52.8 25.7 %collective-permute-start.9 = (bf16[272,1152]{1,0:T(8,128)(2,1)S(1)}, bf16[272,1152]{1,0:T(8,128)(2,1)S(1)}, u32[]{:S(2)}, u32[]{:S(2)}) collective-permute-start(bf16[272,1152]{1,0:T(8,128)(2,1)S(1)} %get-tuple-element.67), channel_id=1, source_target_pairs={{0,4},{1,5},{2,6},{3,7},{4,8},{5,9},{6,10},{7,11},{8,12},{9,13},{1... | collective-permute-start | bytes 1880072 | tf_op jit(solution)/shard_map/ppermute | solution.py:309
  53.1 25.6 %collective-permute-start.7 = (bf16[272,1152]{1,0:T(8,128)(2,1)S(1)}, bf16[272,1152]{1,0:T(8,128)(2,1)S(1)}, u32[]{:S(2)}, u32[]{:S(2)}) collective-permute-start(bf16[272,1152]{1,0:T(8,128)(2,1)S(1)} %get-tuple-element.64.refs_6_), channel_id=1, source_target_pairs={{0,12},{1,13},{2,14},{3,15},{4,0},{5,1},{6,2},{7,3},{8,4},{9,5},{1... | collective-permute-start | bytes 1880072 | tf_op jit(solution)/shard_map/ppermute | solution.py:309
  60.9 24.9 %collective-permute-start.8 = (bf16[272,1152]{1,0:T(8,128)(2,1)S(1)}, bf16[272,1152]{1,0:T(8,128)(2,1)S(1)}, u32[]{:S(2)}, u32[]{:S(2)}) collective-permute-start(bf16[272,1152]{1,0:T(8,128)(2,1)S(1)} %get-tuple-element.66), channel_id=1, source_target_pairs={{0,4},{1,5},{2,6},{3,7},{4,8},{5,9},{6,10},{7,11},{8,12},{9,13},{1... | collective-permute-start | bytes 1880072 | tf_op jit(solution)/shard_map/ppermute | solution.py:309
  61.0 46.8 %collective-permute-start.10 = (bf16[272,1152]{1,0:T(8,128)(2,1)S(1)}, bf16[272,1152]{1,0:T(8,128)(2,1)S(1)}, u32[]{:S(2)}, u32[]{:S(2)}) collective-permute-start(bf16[272,1152]{1,0:T(8,128)(2,1)S(1)} %get-tuple-element.68.refs_2_), channel_id=1, source_target_pairs={{0,12},{1,13},{2,14},{3,15},{4,0},{5,1},{6,2},{7,3},{8,4},{9,5},{1... | collective-permute-start | bytes 1880072 | tf_op jit(solution)/shard_map/ppermute | solution.py:309
  71.0 7.7 %collective-permute-start.13 = (bf16[512,1152]{1,0:T(8,128)(2,1)S(1)}, bf16[512,1152]{1,0:T(8,128)(2,1)S(1)}, u32[]{:S(2)}, u32[]{:S(2)}) collective-permute-start(bf16[512,1152]{1,0:T(8,128)(2,1)S(1)} %cols_yc.1.refs_8_), channel_id=1, source_target_pairs={{0,1},{1,0},{2,3},{3,2},{4,5},{5,4},{6,7},{7,6},{8,9},{9,8},{10,11... | collective-permute-start | bytes 3538952 | tf_op jit(solution)/shard_map/ppermute | solution.py:309
  78.6 33.6 %collective-permute-start.15 = (bf16[528,1152]{1,0:T(8,128)(2,1)S(1)}, bf16[528,1152]{1,0:T(8,128)(2,1)S(1)}, u32[]{:S(2)}, u32[]{:S(2)}) collective-permute-start(bf16[528,1152]{1,0:T(8,128)(2,1)S(1)} %get-tuple-element.89.refs_2_), channel_id=1, source_target_pairs={{0,8},{1,9},{2,10},{3,11},{4,12},{5,13},{6,14},{7,15},{8,0},{9,1},... | collective-permute-start | bytes 3649544 | tf_op jit(solution)/shard_map/ppermute | solution.py:309
  78.9 35.5 %collective-permute-start.16 = (bf16[512,1152]{1,0:T(8,128)(2,1)S(1)}, bf16[512,1152]{1,0:T(8,128)(2,1)S(1)}, u32[]{:S(2)}, u32[]{:S(2)}) collective-permute-start(bf16[512,1152]{1,0:T(8,128)(2,1)S(1)} %add_y.1.refs_8_), channel_id=1, source_target_pairs={{0,2},{1,3},{2,0},{3,1},{4,6},{5,7},{6,4},{7,5},{8,10},{9,11},{10,... | collective-permute-start | bytes 3538952 | tf_op jit(solution)/shard_map/ppermute | solution.py:309
  82.5 25.9 %collective-permute-start.14 = (bf16[512,1152]{1,0:T(8,128)(2,1)S(1)}, bf16[512,1152]{1,0:T(8,128)(2,1)S(1)}, u32[]{:S(2)}, u32[]{:S(2)}) collective-permute-start(bf16[512,1152]{1,0:T(8,128)(2,1)S(1)} %cols_c.1.refs_8_), channel_id=1, source_target_pairs={{0,1},{1,0},{2,3},{3,2},{4,5},{5,4},{6,7},{7,6},{8,9},{9,8},{10,11... | collective-permute-start | bytes 3538952 | tf_op jit(solution)/shard_map/ppermute | solution.py:309
  82.8 25.0 %copy-start.1 = (f32[512,128]{1,0:T(8,128)S(1)}, f32[512,128]{1,0:T(8,128)}, u32[]{:S(2)}) copy-start(f32[512,128]{1,0:T(8,128)} %copy-done) | copy-start | bytes 786436
  108.4 1.3 %copy-start.3 = (bf16[512,1152]{1,0:T(8,128)(2,1)S(1)}, bf16[512,1152]{1,0:T(8,128)(2,1)}, u32[]{:S(2)}) copy-start(bf16[512,1152]{1,0:T(8,128)(2,1)} %refs_1_.2) | copy-start | bytes 3538948
  109.7 1.3 %copy-start.5 = (bf16[512,1152]{1,0:T(8,128)(2,1)S(1)}, bf16[512,1152]{1,0:T(8,128)(2,1)}, u32[]{:S(2)}) copy-start(bf16[512,1152]{1,0:T(8,128)(2,1)} %refs_1_.3) | copy-start | bytes 3538948

commit v3 on v1

--- a/solution.py
+++ b/solution.py
@@ -264,15 +264,15 @@
     pltpu.make_async_copy(buf, out, sem).wait()
 
 
-def image_kernel(count, base, line, unit, factor, late, done, grad_ref, loss_ref, buf, sem):
+def image_kernel(count, base, line, unit, factor, late, ready, grad_ref, loss_ref, done, buf, sem):
     rows = base.shape[0]
+    done[...] = jnp.zeros(done.shape, F32)
     tail = jnp.sum(late[rows:, :rows].astype(F32), axis=0, keepdims=True)
     loss_ref[...] = (line[:1, :] + tail) * (1.0 / count)
     tangent_rows(base, late, unit, factor, grad_ref, buf, sem)
 
 
-def text_kernel(base, unit, factor, late, grad_ref, done, buf, sem):
-    done[...] = jnp.zeros(done.shape, F32)
+def text_kernel(base, unit, factor, late, done, grad_ref, buf, sem):
     tangent_rows(base, late, unit, factor, grad_ref, buf, sem)
 
 
@@ -323,19 +323,21 @@
     )
     home_a0, home_b0 = move(g_prev_a, dz=-1), move(g_next_b, dz=1)
     (last,) = merge("merge_last", prev_b, next_a, [g_prev_a])
-    (last_0, last_c), s_last = rows_step("last_c", scal, last, near_t)
-    (last_y, last_yc), (g_prev_b, g_next_a) = rows_step("last_y", scal, last, far_t, s_last, finish=2)
+    (last_0, last_c, last_y, last_yc), (g_prev_b, g_next_a) = rows_step(
+        "last", scal, last, near_t + far_t, finish=2
+    )
     home_b1, home_a1 = move(g_prev_b, dz=-1), move(g_next_a, dz=1)
     (far,) = merge("merge_far", far_a, far_b, [g_prev_b])
-    (far_y, far_yc), s_far = rows_step("far_y", scal, far, far_t)
+    (far_0, far_c, far_y, far_yc), (g_far,) = rows_step("far", scal, far, near_t + far_t, finish=1)
+    home_far = move(g_far, dz=2)
     images = [own, first, last, far]
-    (gt_yc,) = cols_step("cols_yc", [[own_yc], [first_yc], [last_yc], [far_yc]], images, (BF,))
+    (gt_yc,) = cols_step(
+        "cols_yc", [[own_yc], [first_yc], [last_yc], [far_yc]], images, (BF,), after=[g_far, home_a0, home_b0]
+    )
     through_y = move(gt_yc, dc=1)
     (gt_y,) = cols_step("cols_y", [[own_y], [first_y], [last_y], [far_y]], images, (F32,), after=[gt_yc])
-    (far_0, far_c), (g_far,) = rows_step("far_c", scal, far, near_t, s_far, finish=1, after=[gt_y])
-    sum_y = add("add_y", gt_y, through_y, after=[g_far, home_a0, home_b0])
+    sum_y = add("add_y", gt_y, through_y)
     text_y = move(sum_y, dy=1)
-    home_far = move(g_far, dz=2)
     (gt_c,) = cols_step("cols_c", [[own_c], [first_c], [last_c], [far_c]], images, (BF,), after=[sum_y])
     text_c = move(gt_c, dc=1)
     (gt_own,) = cols_step(
@@ -352,16 +354,14 @@
     (t_base,) = call(
         text_base_kernel, "text_base", [gt_own, text_c], [pltpu.VMEM((rows, width), F32)], [line], cost=1000
     )
-    grad_text, done = final(
-        text_kernel, "text", [t_base, t_unit, t_factor, text_y], (rows, width), [pltpu.VMEM((8, 128), F32)]
-    )
-    grad_image, loss = final(
+    grad_image, loss, done = final(
         functools.partial(image_kernel, total),
         "image",
-        [i_base, line, i_unit, i_factor, home_far, done],
+        [i_base, line, i_unit, i_factor, home_far, t_base],
         (rows, width),
-        [jax.ShapeDtypeStruct((1, rows), F32)],
-    )
+        [jax.ShapeDtypeStruct((1, rows), F32), pltpu.VMEM((8, 128), F32)],
+    )
+    (grad_text,) = final(text_kernel, "text", [t_base, t_unit, t_factor, text_y, done], (rows, width), [])
     return loss.reshape(rows), grad_image, grad_text
 
 

time: 111 us -> 109 us (0.982)
  Pallas kernels: 54.5 us -> 51.2 us
    pallas_call x24 -> x22, Pallas kernels: 50.4 us -> 47.2 us  [call(): pl.pallas_call(body, name=name, in_specs=specs, out_specs=[VMEM] * len(ou...]
    unnamed x18 -> x14, local copies, waits for them, and re-layouts: 2.66 us -> 2.64 us
  transfers between devices with their start and end apart: 17 -> 17, of which waited for: 3 -> 4; matrix products, arithmetic and copies ran while one was open for 0% -> 0% of each run, Pallas kernels for 47% -> 45%
where the time goes in v3:
time: 109 us; the launch traced here: 108 us
  Pallas kernels  51.2 us (47%)
  waiting for transfers between devices  26.6 us (24%)
  starting transfers between devices  25 us (23%)
  local copies, waits for them, and re-layouts  2.64 us (2%)
  between operations  2.44 us (2%)
    pallas_call x22, Pallas kernels, call(): pl.pallas_call(body, name=name, in_specs=specs, out_specs=[VMEM] * len(ou...  47.2 us
    ppermute x17, waiting for transfers between devices, move(): return lax.ppermute(value, 'loss', pairs)  26.6 us
    ppermute x17, starting transfers between devices, move(): return lax.ppermute(value, 'loss', pairs)  25 us
    pallas_call x2, Pallas kernels, final(): pl.pallas_call(kernel, name=name, in_specs=[VMEM] * len(inputs), out_spec...  3.98 us
    unnamed x14, local copies, waits for them, and re-layouts  2.64 us
  transfers between devices with their start and end apart: 17, of which 4 were waited for; matrix products, arithmetic and copies ran while one was open for 0% of the time, Pallas kernels for 45%

profile of v3, /device:TPU:0, one launch (start us, length us, event | category | flops | bytes accessed | tf_op | source)
XLA Modules:
  0.0 108.1 jit_solution(6474353535136494541)
XLA Ops:
  0.7 1.4 %copy-done.5 = bf16[512,1152]{1,0:T(8,128)(2,1)S(1)} copy-done((bf16[512,1152]{1,0:T(8,128)(2,1)S(1)}, bf16[512,1152]{1,0:T(8,128)(2,1)}, u32[]{:S(2)}) %copy-start.5) | copy-done | bytes 1179672
  2.0 0.6 norm_text.1.refs_1_.refs_2_
  2.6 0.1 collective-permute-start.3
  2.7 3.4 %collective-permute-start = (bf16[512,1152]{1,0:T(8,128)(2,1)S(1)}, bf16[512,1152]{1,0:T(8,128)(2,1)S(1)}, u32[]{:S(2)}, u32[]{:S(2)}) collective-permute-start(bf16[512,1152]{1,0:T(8,128)(2,1)S(1)} %norm_text.1.refs_1_.refs_2_), channel_id=1, source_target_pairs={{0,2},{1,3},{2,0},{3,1},{4,6},{5,7},{6,4},{7,5},{8,10},{9,11},{10,... | collective-permute-start | bytes 3538952 | tf_op jit(solution)/shard_map/ppermute | solution.py:300
  6.1 0.7 norm_image.1
  6.7 2.0 %collective-permute-start.1 = (bf16[256,1152]{1,0:T(8,128)(2,1)S(1)}, bf16[256,1152]{1,0:T(8,128)(2,1)S(1)}, u32[]{:S(2)}, u32[]{:S(2)}) collective-permute-start(bf16[256,1152]{1,0:T(8,128)(2,1)S(1)} %get-tuple-element.48.refs_0_), channel_id=1, source_target_pairs={{0,4},{1,5},{2,6},{3,7},{4,8},{5,9},{6,10},{7,11},{8,12},{9,13},{1... | collective-permute-start | bytes 1769480 | tf_op jit(solution)/shard_map/ppermute | solution.py:300
  8.7 2.2 %collective-permute-start.2 = (bf16[256,1152]{1,0:T(8,128)(2,1)S(1)}, bf16[256,1152]{1,0:T(8,128)(2,1)S(1)}, u32[]{:S(2)}, u32[]{:S(2)}) collective-permute-start(bf16[256,1152]{1,0:T(8,128)(2,1)S(1)} %get-tuple-element.49.refs_1_), channel_id=1, source_target_pairs={{0,12},{1,13},{2,14},{3,15},{4,0},{5,1},{6,2},{7,3},{8,4},{9,5},{1... | collective-permute-start | bytes 1769480 | tf_op jit(solution)/shard_map/ppermute | solution.py:300
  12.3 0.1 pad_maximum_fusion.refs_0_
  12.3 0.1 hold_last.1
  12.4 0.1 collective-permute-start.6
  12.5 3.2 %collective-permute-start.7 = (bf16[256,1152]{1,0:T(8,128)(2,1)S(1)}, bf16[256,1152]{1,0:T(8,128)(2,1)S(1)}, u32[]{:S(2)}, u32[]{:S(2)}) collective-permute-start(bf16[256,1152]{1,0:T(8,128)(2,1)S(1)} %get-tuple-element.50.refs_4_), channel_id=1, source_target_pairs={{0,12},{1,13},{2,14},{3,15},{4,0},{5,1},{6,2},{7,3},{8,4},{9,5},{1... | collective-permute-start | bytes 1769480 | tf_op jit(solution)/shard_map/ppermute | solution.py:300
  15.7 4.1 %own_c.1 = (bf16[512,512]{1,0:T(8,128)(2,1)S(1)}, bf16[512,512]{1,0:T(8,128)(2,1)S(1)}, f32[512,1152]{1,0:T(8,128)S(1)}, f32[512,128]{1,0:T(8,128)S(1)}) custom-call(f32[3]{0:T(128)S(1)} %pad_maximum_fusion.refs_0_, bf16[512,1152]{1,0:T(8,128)(2,1)S(1)} %get-tuple-element.47.refs_1_.refs_4_, bf16[512,1152]{1,0:T(8,128)(2,1)S(1)} %norm_text.1.refs_1_.refs_2_, ...), custom_call_target="tpu_custom_call" | custom-call | flops 20000000000 | tf_op jit(solution)/shard_map/own_c/pallas_call | solution.py:30
  19.8 5.1 %collective-permute-done.1.refs_0_ = bf16[256,1152]{1,0:T(8,128)(2,1)S(1)} collective-permute-done((bf16[256,1152]{1,0:T(8,128)(2,1)S(1)}, bf16[256,1152]{1,0:T(8,128)(2,1)S(1)}, u32[]{:S(2)}, u32[]{:S(2)}) %collective-permute-start.1) | collective-permute-done | bytes 589856 | tf_op jit(solution)/shard_map/ppermute | solution.py:300
  25.0 0.2 merge_first.1
  25.1 2.0 %collective-permute-start.11 = (bf16[256,1152]{1,0:T(8,128)(2,1)S(1)}, bf16[256,1152]{1,0:T(8,128)(2,1)S(1)}, u32[]{:S(2)}, u32[]{:S(2)}) collective-permute-start(bf16[256,1152]{1,0:T(8,128)(2,1)S(1)} %get-tuple-element.68), channel_id=1, source_target_pairs={{0,4},{1,5},{2,6},{3,7},{4,8},{5,9},{6,10},{7,11},{8,12},{9,13},{1... | collective-permute-start | bytes 1769480 | tf_op jit(solution)/shard_map/ppermute | solution.py:300
  27.1 1.5 %collective-permute-start.12 = (bf16[256,1152]{1,0:T(8,128)(2,1)S(1)}, bf16[256,1152]{1,0:T(8,128)(2,1)S(1)}, u32[]{:S(2)}, u32[]{:S(2)}) collective-permute-start(bf16[256,1152]{1,0:T(8,128)(2,1)S(1)} %get-tuple-element.69), channel_id=1, source_target_pairs={{0,12},{1,13},{2,14},{3,15},{4,0},{5,1},{6,2},{7,3},{8,4},{9,5},{1... | collective-permute-start | bytes 1769480 | tf_op jit(solution)/shard_map/ppermute | solution.py:300
  28.6 3.8 %first_c.1 = (bf16[512,512]{1,0:T(8,128)(2,1)S(1)}, bf16[512,512]{1,0:T(8,128)(2,1)S(1)}, f32[512,1152]{1,0:T(8,128)S(1)}, f32[512,128]{1,0:T(8,128)S(1)}) custom-call(f32[3]{0:T(128)S(1)} %pad_maximum_fusion.refs_0_, bf16[512,1152]{1,0:T(8,128)(2,1)S(1)} %get-tuple-element.52.refs_1_.refs_5_, bf16[512,1152]{1,0:T(8,128)(2,1)S(1)} %norm_text.1.refs_1_.refs_2_, ...), custom_call_target="tpu_custom_call" | custom-call | flops 20000000000 | tf_op jit(solution)/shard_map/first_c/pallas_call | solution.py:30
  32.4 1.1 %prep_image.1 = (f32[512,1152]{1,0:T(8,128)S(1)}, f32[512,128]{1,0:T(8,128)S(1)}) custom-call(f32[3]{0:T(128)S(1)} %pad_maximum_fusion.refs_0_, bf16[512,1152]{1,0:T(8,128)(2,1)S(1)} %copy-done.4, f32[512,128]{1,0:T(8,128)S(1)} %get-tuple-element.53.refs_2_.refs_5_), custom_call_target="tpu_custom_call" | custom-call | flops 20000000000 | tf_op jit(solution)/shard_map/prep_image/pallas_call | solution.py:30
  33.6 0.1 hold_text.1.refs_2_.refs_4_
  33.7 0.6 copy-done
  34.3 0.7 copy-done.6
  34.9 1.1 %prep_text.1 = (f32[512,1152]{1,0:T(8,128)S(1)}, f32[512,128]{1,0:T(8,128)S(1)}) custom-call(f32[3]{0:T(128)S(1)} %pad_maximum_fusion.refs_0_, bf16[512,1152]{1,0:T(8,128)(2,1)S(1)} %copy-done.6, bf16[512,1152]{1,0:T(8,128)(2,1)S(1)} %hold_text.1.refs_2_.refs_4_), custom_call_target="tpu_custom_call" | custom-call | flops 20000000000 | tf_op jit(solution)/shard_map/prep_text/pallas_call | solution.py:30
  36.1 1.0 collective-permute-done.4.refs_3_.refs_5_
  37.1 4.4 %own_y.1 = (bf16[512,512]{1,0:T(8,128)(2,1)S(1)}, bf16[512,512]{1,0:T(8,128)(2,1)S(1)}, f32[512,1152]{1,0:T(8,128)S(1)}, f32[512,128]{1,0:T(8,128)S(1)}) custom-call(f32[3]{0:T(128)S(1)} %pad_maximum_fusion.refs_0_, bf16[512,1152]{1,0:T(8,128)(2,1)S(1)} %get-tuple-element.47.refs_1_.refs_4_, bf16[512,1152]{1,0:T(8,128)(2,1)S(1)} %hold_text.1.refs_2_.refs_4_, ...), custom_call_target="tpu_custom_call" | custom-call | flops 20000000000 | tf_op jit(solution)/shard_map/own_y/pallas_call | solution.py:30
  41.5 4.5 %first_y.1 = (bf16[512,512]{1,0:T(8,128)(2,1)S(1)}, bf16[512,512]{1,0:T(8,128)(2,1)S(1)}, bf16[272,1152]{1,0:T(8,128)(2,1)S(1)}, bf16[272,1152]{1,0:T(8,128)(2,1)S(1)}) custom-call(f32[3]{0:T(128)S(1)} %pad_maximum_fusion.refs_0_, bf16[512,1152]{1,0:T(8,128)(2,1)S(1)} %get-tuple-element.52.refs_1_.refs_5_, bf16[512,1152]{1,0:T(8,128)(2,1)S(1)} %hold_text.1.refs_2_.refs_4_, ...), custom_call_target="tpu_custom_call" | custom-call | flops 20000000000 | tf_op jit(solution)/shard_map/first_y/pallas_call | solution.py:30
  46.0 0.6 collective-permute-start.9
  46.6 2.7 %collective-permute-start.5 = (bf16[272,1152]{1,0:T(8,128)(2,1)S(1)}, bf16[272,1152]{1,0:T(8,128)(2,1)S(1)}, u32[]{:S(2)}, u32[]{:S(2)}) collective-permute-start(bf16[272,1152]{1,0:T(8,128)(2,1)S(1)} %get-tuple-element.60.refs_2_), channel_id=1, source_target_pairs={{0,12},{1,13},{2,14},{3,15},{4,0},{5,1},{6,2},{7,3},{8,4},{9,5},{1... | collective-permute-start | bytes 1880072 | tf_op jit(solution)/shard_map/ppermute | solution.py:300
  49.3 0.1 merge_last.1.refs_1_.refs_6_
  49.4 6.8 %last.1 = (bf16[512,512]{1,0:T(8,128)(2,1)S(1)}, bf16[512,512]{1,0:T(8,128)(2,1)S(1)}, bf16[512,512]{1,0:T(8,128)(2,1)S(1)}, bf16[512,512]{1,0:T(8,128)(2,1)S(1)...) custom-call(f32[3]{0:T(128)S(1)} %pad_maximum_fusion.refs_0_, ...), custom_call_target="tpu_custom_call" | custom-call | flops 20000000000 | tf_op jit(solution)/shard_map/last/pallas_call | solution.py:30
  56.2 0.1 collective-permute-start.8
  56.3 3.2 %collective-permute-start.10 = (bf16[272,1152]{1,0:T(8,128)(2,1)S(1)}, bf16[272,1152]{1,0:T(8,128)(2,1)S(1)}, u32[]{:S(2)}, u32[]{:S(2)}) collective-permute-start(bf16[272,1152]{1,0:T(8,128)(2,1)S(1)} %get-tuple-element.64.refs_2_), channel_id=1, source_target_pairs={{0,12},{1,13},{2,14},{3,15},{4,0},{5,1},{6,2},{7,3},{8,4},{9,5},{1... | collective-permute-start | bytes 1880072 | tf_op jit(solution)/shard_map/ppermute | solution.py:300
  59.5 0.1 merge_far.1.refs_1_.refs_7_
  59.6 6.8 %far.1 = (bf16[512,512]{1,0:T(8,128)(2,1)S(1)}, bf16[512,512]{1,0:T(8,128)(2,1)S(1)}, bf16[512,512]{1,0:T(8,128)(2,1)S(1)}, bf16[512,512]{1,0:T(8,128)(2,1)S(1)}, bf16[528,1152]{1,0:T(8,128)(2,1)S(1)}) custom-call(f32[3]{0:T(128)S(1)} %pad_maximum_fusion.refs_0_, bf16[512,1152]{1,0:T(8,128)(2,1)S(1)} %merge_far.1.refs_1_.refs_7_, ...), custom_call_target="tpu_custom_call" | custom-call | flops 20000000000 | tf_op jit(solution)/shard_map/far/pallas_call | solution.py:30
  66.4 0.1 collective-permute-start.14
  66.5 3.0 %cols_yc.1.refs_8_ = bf16[512,1152]{1,0:T(8,128)(2,1)S(1)} custom-call(bf16[512,512]{1,0:T(8,128)(2,1)S(1)} %get-tuple-element.79.refs_0_, bf16[512,512]{1,0:T(8,128)(2,1)S(1)} %get-tuple-element.80.refs_1_, bf16[512,512]{1,0:T(8,128)(2,1)S(1)} %get-tuple-element.81.refs_2_, bf16[512,512]{1,0:T(8,128)(2,1)S(1)} %get-tuple-element.82.refs_3_, ...), custom_call_target="tpu_custom_call" | custom-call | flops 20000000000 | tf_op jit(solution)/shard_map/cols_yc/pallas_call | solution.py:30
  69.5 0.1 collective-permute-start.13
  69.6 3.0 %cols_y.1.refs_0_ = f32[512,1152]{1,0:T(8,128)S(1)} custom-call(bf16[512,512]{1,0:T(8,128)(2,1)S(1)} %get-tuple-element.75.refs_0_, bf16[512,512]{1,0:T(8,128)(2,1)S(1)} %get-tuple-element.76.refs_1_, bf16[512,512]{1,0:T(8,128)(2,1)S(1)} %get-tuple-element.77.refs_2_, bf16[512,512]{1,0:T(8,128)(2,1)S(1)} %get-tuple-element.78.refs_3_, ...), custom_call_target="tpu_custom_call" | custom-call | flops 20000000000 | tf_op jit(solution)/shard_map/cols_y/pallas_call | solution.py:30
  72.6 0.2 add_y.1.refs_8_
  72.8 3.5 %collective-permute-start.16 = (bf16[512,1152]{1,0:T(8,128)(2,1)S(1)}, bf16[512,1152]{1,0:T(8,128)(2,1)S(1)}, u32[]{:S(2)}, u32[]{:S(2)}) collective-permute-start(bf16[512,1152]{1,0:T(8,128)(2,1)S(1)} %add_y.1.refs_8_), channel_id=1, source_target_pairs={{0,2},{1,3},{2,0},{3,1},{4,6},{5,7},{6,4},{7,5},{8,10},{9,11},{10,... | collective-permute-start | bytes 3538952 | tf_op jit(solution)/shard_map/ppermute | solution.py:300
  76.3 3.0 %cols_c.1.refs_8_ = bf16[512,1152]{1,0:T(8,128)(2,1)S(1)} custom-call(bf16[512,512]{1,0:T(8,128)(2,1)S(1)} %get-tuple-element.71.refs_0_, bf16[512,512]{1,0:T(8,128)(2,1)S(1)} %get-tuple-element.72.refs_1_, bf16[512,512]{1,0:T(8,128)(2,1)S(1)} %get-tuple-element.73.refs_2_, bf16[512,512]{1,0:T(8,128)(2,1)S(1)} %get-tuple-element.74.refs_3_, ...), custom_call_target="tpu_custom_call" | custom-call | flops 20000000000 | tf_op jit(solution)/shard_map/cols_c/pallas_call | solution.py:30
  79.2 0.3 collective-permute-start.15
  79.5 3.0 %cols_own.1.refs_6_.refs_0_ = f32[512,1152]{1,0:T(8,128)S(1)} custom-call(bf16[512,512]{1,0:T(8,128)(2,1)S(1)} %get-tuple-element.65.refs_0_, bf16[512,512]{1,0:T(8,128)(2,1)S(1)} %get-tuple-element.66.refs_1_, bf16[512,512]{1,0:T(8,128)(2,1)S(1)} %get-tuple-element.67.refs_2_, bf16[512,512]{1,0:T(8,128)(2,1)S(1)} %get-tuple-element.70.refs_3_, ...), custom_call_target="tpu_custom_call" | custom-call | flops 20000000000 | tf_op jit(solution)/shard_map/cols_own/pallas_call | solution.py:30
  82.5 19.7 %collective-permute-done.10.refs_5_ = bf16[272,1152]{1,0:T(8,128)(2,1)S(1)} collective-permute-done((bf16[272,1152]{1,0:T(8,128)(2,1)S(1)}, bf16[272,1152]{1,0:T(8,128)(2,1)S(1)}, u32[]{:S(2)}, u32[]{:S(2)}) %collective-permute-start.10) | collective-permute-done | bytes 626720 | tf_op jit(solution)/shard_map/ppermute | solution.py:300
  102.3 0.6 image_base.1
  102.9 0.3 text_base.1.ready.base
  103.2 0.7 collective-permute-done.14.late
  103.9 2.3 %image.1 = (bf16[512,1152]{1,0:T(8,128)(2,1)}, f32[1,512]{1,0:T(1,128)}, f32[8,128]{1,0:T(8,128)S(1)}) custom-call(f32[512,1152]{1,0:T(8,128)S(1)} %get-tuple-element.84.base, f32[8,512]{1,0:T(8,128)S(1)} %get-tuple-element.85.refs_2_.line, f32[512,1152]{1,0:T(8,128)S(1)} %get-tuple-element.86.unit, f32[512,128]{1,0:T(8,128)S(1)} %copy-done.1, ...), custom_call_target="tpu_custom_call" | custom-call | flops 1000 | tf_op jit(solution)/shard_map/image/pallas_call | solution.py:280
  106.2 1.7 %text.1 = bf16[512,1152]{1,0:T(8,128)(2,1)} custom-call(f32[512,1152]{1,0:T(8,128)S(1)} %text_base.1.ready.base, f32[512,1152]{1,0:T(8,128)S(1)} %get-tuple-element.89.unit, f32[512,128]{1,0:T(8,128)S(1)} %copy-done.3, bf16[512,1152]{1,0:T(8,128)(2,1)S(1)} %collective-permute-done.16.late, f32[8,128]{1,0:T(8,128)S(1)} %get-tuple-element.90.done), custom_call_target="tpu_custom_call" | custom-call | flops 1000 | tf_op jit(solution)/shard_map/text/pallas_call | solution.py:280
  (25 shorter events, 0.1 us)
Async XLA Ops:
  0.6 5.4 %copy-start.4 = (bf16[512,1152]{1,0:T(8,128)(2,1)S(1)}, bf16[512,1152]{1,0:T(8,128)(2,1)}, u32[]{:S(2)}) copy-start(bf16[512,1152]{1,0:T(8,128)(2,1)} %refs_1_.2) | copy-start | bytes 3538948
  0.6 1.4 %copy-start.5 = (bf16[512,1152]{1,0:T(8,128)(2,1)S(1)}, bf16[512,1152]{1,0:T(8,128)(2,1)}, u32[]{:S(2)}) copy-start(bf16[512,1152]{1,0:T(8,128)(2,1)} %refs_1_.3) | copy-start | bytes 3538948
  2.6 9.7 %collective-permute-start.3 = (bf16[512,1152]{1,0:T(8,128)(2,1)S(1)}, bf16[512,1152]{1,0:T(8,128)(2,1)S(1)}, u32[]{:S(2)}, u32[]{:S(2)}) collective-permute-start(bf16[512,1152]{1,0:T(8,128)(2,1)S(1)} %norm_text.1.refs_1_.refs_2_), channel_id=1, source_target_pairs={{0,1},{1,0},{2,3},{3,2},{4,5},{5,4},{6,7},{7,6},{8,9},{9,8},{10,11... | collective-permute-start | bytes 3538952 | tf_op jit(solution)/shard_map/ppermute | solution.py:300
  2.7 30.9 %collective-permute-start = (bf16[512,1152]{1,0:T(8,128)(2,1)S(1)}, bf16[512,1152]{1,0:T(8,128)(2,1)S(1)}, u32[]{:S(2)}, u32[]{:S(2)}) collective-permute-start(bf16[512,1152]{1,0:T(8,128)(2,1)S(1)} %norm_text.1.refs_1_.refs_2_), channel_id=1, source_target_pairs={{0,2},{1,3},{2,0},{3,1},{4,6},{5,7},{6,4},{7,5},{8,10},{9,11},{10,... | collective-permute-start | bytes 3538952 | tf_op jit(solution)/shard_map/ppermute | solution.py:300
  6.7 18.2 %collective-permute-start.1 = (bf16[256,1152]{1,0:T(8,128)(2,1)S(1)}, bf16[256,1152]{1,0:T(8,128)(2,1)S(1)}, u32[]{:S(2)}, u32[]{:S(2)}) collective-permute-start(bf16[256,1152]{1,0:T(8,128)(2,1)S(1)} %get-tuple-element.48.refs_0_), channel_id=1, source_target_pairs={{0,4},{1,5},{2,6},{3,7},{4,8},{5,9},{6,10},{7,11},{8,12},{9,13},{1... | collective-permute-start | bytes 1769480 | tf_op jit(solution)/shard_map/ppermute | solution.py:300
  8.7 16.2 %collective-permute-start.2 = (bf16[256,1152]{1,0:T(8,128)(2,1)S(1)}, bf16[256,1152]{1,0:T(8,128)(2,1)S(1)}, u32[]{:S(2)}, u32[]{:S(2)}) collective-permute-start(bf16[256,1152]{1,0:T(8,128)(2,1)S(1)} %get-tuple-element.49.refs_1_), channel_id=1, source_target_pairs={{0,12},{1,13},{2,14},{3,15},{4,0},{5,1},{6,2},{7,3},{8,4},{9,5},{1... | collective-permute-start | bytes 1769480 | tf_op jit(solution)/shard_map/ppermute | solution.py:300
  12.4 34.2 %collective-permute-start.6 = (bf16[256,1152]{1,0:T(8,128)(2,1)S(1)}, bf16[256,1152]{1,0:T(8,128)(2,1)S(1)}, u32[]{:S(2)}, u32[]{:S(2)}) collective-permute-start(bf16[256,1152]{1,0:T(8,128)(2,1)S(1)} %get-tuple-element.61), channel_id=1, source_target_pairs={{0,4},{1,5},{2,6},{3,7},{4,8},{5,9},{6,10},{7,11},{8,12},{9,13},{1... | collective-permute-start | bytes 1769480 | tf_op jit(solution)/shard_map/ppermute | solution.py:300
  12.5 36.8 %collective-permute-start.7 = (bf16[256,1152]{1,0:T(8,128)(2,1)S(1)}, bf16[256,1152]{1,0:T(8,128)(2,1)S(1)}, u32[]{:S(2)}, u32[]{:S(2)}) collective-permute-start(bf16[256,1152]{1,0:T(8,128)(2,1)S(1)} %get-tuple-element.50.refs_4_), channel_id=1, source_target_pairs={{0,12},{1,13},{2,14},{3,15},{4,0},{5,1},{6,2},{7,3},{8,4},{9,5},{1... | collective-permute-start | bytes 1769480 | tf_op jit(solution)/shard_map/ppermute | solution.py:300
  25.1 31.1 %collective-permute-start.11 = (bf16[256,1152]{1,0:T(8,128)(2,1)S(1)}, bf16[256,1152]{1,0:T(8,128)(2,1)S(1)}, u32[]{:S(2)}, u32[]{:S(2)}) collective-permute-start(bf16[256,1152]{1,0:T(8,128)(2,1)S(1)} %get-tuple-element.68), channel_id=1, source_target_pairs={{0,4},{1,5},{2,6},{3,7},{4,8},{5,9},{6,10},{7,11},{8,12},{9,13},{1... | collective-permute-start | bytes 1769480 | tf_op jit(solution)/shard_map/ppermute | solution.py:300
  27.1 32.4 %collective-permute-start.12 = (bf16[256,1152]{1,0:T(8,128)(2,1)S(1)}, bf16[256,1152]{1,0:T(8,128)(2,1)S(1)}, u32[]{:S(2)}, u32[]{:S(2)}) collective-permute-start(bf16[256,1152]{1,0:T(8,128)(2,1)S(1)} %get-tuple-element.69), channel_id=1, source_target_pairs={{0,12},{1,13},{2,14},{3,15},{4,0},{5,1},{6,2},{7,3},{8,4},{9,5},{1... | collective-permute-start | bytes 1769480 | tf_op jit(solution)/shard_map/ppermute | solution.py:300
  33.5 0.7 copy-start
  33.6 1.4 %copy-start.6 = (bf16[512,1152]{1,0:T(8,128)(2,1)S(1)}, bf16[512,1152]{1,0:T(8,128)(2,1)}, u32[]{:S(2)}) copy-start(bf16[512,1152]{1,0:T(8,128)(2,1)} %refs_1_.3) | copy-start | bytes 3538948
  34.2 2.8 %collective-permute-start.4 = (bf16[512,1152]{1,0:T(8,128)(2,1)S(1)}, bf16[512,1152]{1,0:T(8,128)(2,1)S(1)}, u32[]{:S(2)}, u32[]{:S(2)}) collective-permute-start(bf16[512,1152]{1,0:T(8,128)(2,1)S(1)} %hold_text.1.refs_2_.refs_4_), channel_id=1, source_target_pairs={{0,1},{1,0},{2,3},{3,2},{4,5},{5,4},{6,7},{7,6},{8,9},{9,8},{10,11... | collective-permute-start | bytes 3538952 | tf_op jit(solution)/shard_map/ppermute | solution.py:300
  36.1 5.4 %copy-start.2 = (f32[512,128]{1,0:T(8,128)}, f32[512,128]{1,0:T(8,128)S(1)}, u32[]{:S(2)}) copy-start(f32[512,128]{1,0:T(8,128)S(1)} %get-tuple-element.56.refs_6_.factor) | copy-start | bytes 786436
  46.0 20.5 %collective-permute-start.9 = (bf16[272,1152]{1,0:T(8,128)(2,1)S(1)}, bf16[272,1152]{1,0:T(8,128)(2,1)S(1)}, u32[]{:S(2)}, u32[]{:S(2)}) collective-permute-start(bf16[272,1152]{1,0:T(8,128)(2,1)S(1)} %get-tuple-element.63), channel_id=1, source_target_pairs={{0,4},{1,5},{2,6},{3,7},{4,8},{5,9},{6,10},{7,11},{8,12},{9,13},{1... | collective-permute-start | bytes 1880072 | tf_op jit(solution)/shard_map/ppermute | solution.py:300
  46.6 19.9 %collective-permute-start.5 = (bf16[272,1152]{1,0:T(8,128)(2,1)S(1)}, bf16[272,1152]{1,0:T(8,128)(2,1)S(1)}, u32[]{:S(2)}, u32[]{:S(2)}) collective-permute-start(bf16[272,1152]{1,0:T(8,128)(2,1)S(1)} %get-tuple-element.60.refs_2_), channel_id=1, source_target_pairs={{0,12},{1,13},{2,14},{3,15},{4,0},{5,1},{6,2},{7,3},{8,4},{9,5},{1... | collective-permute-start | bytes 1880072 | tf_op jit(solution)/shard_map/ppermute | solution.py:300
  56.2 26.3 %collective-permute-start.8 = (bf16[272,1152]{1,0:T(8,128)(2,1)S(1)}, bf16[272,1152]{1,0:T(8,128)(2,1)S(1)}, u32[]{:S(2)}, u32[]{:S(2)}) collective-permute-start(bf16[272,1152]{1,0:T(8,128)(2,1)S(1)} %get-tuple-element.62), channel_id=1, source_target_pairs={{0,4},{1,5},{2,6},{3,7},{4,8},{5,9},{6,10},{7,11},{8,12},{9,13},{1... | collective-permute-start | bytes 1880072 | tf_op jit(solution)/shard_map/ppermute | solution.py:300
  56.3 46.0 %collective-permute-start.10 = (bf16[272,1152]{1,0:T(8,128)(2,1)S(1)}, bf16[272,1152]{1,0:T(8,128)(2,1)S(1)}, u32[]{:S(2)}, u32[]{:S(2)}) collective-permute-start(bf16[272,1152]{1,0:T(8,128)(2,1)S(1)} %get-tuple-element.64.refs_2_), channel_id=1, source_target_pairs={{0,12},{1,13},{2,14},{3,15},{4,0},{5,1},{6,2},{7,3},{8,4},{9,5},{1... | collective-permute-start | bytes 1880072 | tf_op jit(solution)/shard_map/ppermute | solution.py:300
  66.4 37.5 %collective-permute-start.14 = (bf16[528,1152]{1,0:T(8,128)(2,1)S(1)}, bf16[528,1152]{1,0:T(8,128)(2,1)S(1)}, u32[]{:S(2)}, u32[]{:S(2)}) collective-permute-start(bf16[528,1152]{1,0:T(8,128)(2,1)S(1)} %get-tuple-element.83.refs_8_), channel_id=1, source_target_pairs={{0,8},{1,9},{2,10},{3,11},{4,12},{5,13},{6,14},{7,15},{8,0},{9,1},... | collective-permute-start | bytes 3649544 | tf_op jit(solution)/shard_map/ppermute | solution.py:300
  69.5 3.1 %collective-permute-start.13 = (bf16[512,1152]{1,0:T(8,128)(2,1)S(1)}, bf16[512,1152]{1,0:T(8,128)(2,1)S(1)}, u32[]{:S(2)}, u32[]{:S(2)}) collective-permute-start(bf16[512,1152]{1,0:T(8,128)(2,1)S(1)} %cols_yc.1.refs_8_), channel_id=1, source_target_pairs={{0,1},{1,0},{2,3},{3,2},{4,5},{5,4},{6,7},{7,6},{8,9},{9,8},{10,11... | collective-permute-start | bytes 3538952 | tf_op jit(solution)/shard_map/ppermute | solution.py:300
  72.8 33.4 %collective-permute-start.16 = (bf16[512,1152]{1,0:T(8,128)(2,1)S(1)}, bf16[512,1152]{1,0:T(8,128)(2,1)S(1)}, u32[]{:S(2)}, u32[]{:S(2)}) collective-permute-start(bf16[512,1152]{1,0:T(8,128)(2,1)S(1)} %add_y.1.refs_8_), channel_id=1, source_target_pairs={{0,2},{1,3},{2,0},{3,1},{4,6},{5,7},{6,4},{7,5},{8,10},{9,11},{10,... | collective-permute-start | bytes 3538952 | tf_op jit(solution)/shard_map/ppermute | solution.py:300
  79.2 23.7 %collective-permute-start.15 = (bf16[512,1152]{1,0:T(8,128)(2,1)S(1)}, bf16[512,1152]{1,0:T(8,128)(2,1)S(1)}, u32[]{:S(2)}, u32[]{:S(2)}) collective-permute-start(bf16[512,1152]{1,0:T(8,128)(2,1)S(1)} %cols_c.1.refs_8_), channel_id=1, source_target_pairs={{0,1},{1,0},{2,3},{3,2},{4,5},{5,4},{6,7},{7,6},{8,9},{9,8},{10,11... | collective-permute-start | bytes 3538952 | tf_op jit(solution)/shard_map/ppermute | solution.py:300
  102.9 1.0 copy-start.1
  103.9 2.3 %copy-start.3 = (f32[512,128]{1,0:T(8,128)S(1)}, f32[512,128]{1,0:T(8,128)}, u32[]{:S(2)}) copy-start(f32[512,128]{1,0:T(8,128)} %copy-done.2) | copy-start | bytes 786436

commit v4 on v3

--- a/solution.py
+++ b/solution.py
@@ -237,14 +237,27 @@
     return call(add_kernel, name, [a, b], [pltpu.VMEM(a.shape, BF)], after)[0]
 
 
-def image_base_kernel(own, lanes, a_0, a_1, b_0, b_1, base, line):
+def sums_kernel(own, lanes, *refs):
+    given, outs = refs[:2], refs[2:]
+    half = own.shape[0] // 2
+    for k in range(2):
+        mine = slice(k * half, (k + 1) * half)
+        outs[k][:half, :] = (own[mine, :] + given[k][:half, :].astype(F32)).astype(BF)
+        tail = jnp.sum(given[k][half:, :half].astype(F32), axis=0, keepdims=True)
+        outs[k][half:, :] = loss_rows_of(line_of(lanes[mine, :]) + tail, own.shape[1])
+
+
+def sums(name, state, given, after):
+    return call(sums_kernel, name, [*state, *given], [pltpu.VMEM(g.shape, BF) for g in given], after)
+
+
+def image_base_kernel(own, lanes, near_a, near_b, base, line):
     half = own.shape[0] // 2
     lines = []
-    for k, (p, q) in enumerate(((a_0, a_1), (b_0, b_1))):
+    for k, near in enumerate((near_a, near_b)):
         mine = slice(k * half, (k + 1) * half)
-        base[mine, :] = own[mine, :] + p[:half, :].astype(F32) + q[:half, :].astype(F32)
-        tail = p[half:, :half].astype(F32) + q[half:, :half].astype(F32)
-        lines.append(jnp.sum(tail, axis=0, keepdims=True))
+        base[mine, :] = own[mine, :] + near[:half, :].astype(F32)
+        lines.append(jnp.sum(near[half:, :half].astype(F32), axis=0, keepdims=True))
     line[...] = jnp.broadcast_to(line_of(lanes[...]) + jnp.concatenate(lines, axis=1), line.shape)
 
 
@@ -253,27 +266,32 @@
 
 
 def tangent_rows(base, late, unit, factor, out, buf, sem):
-    def body(at):
-        total = base[at, :] + late[at, :].astype(F32)
-        u = unit[at, :]
-        along = jnp.sum(u * total, axis=1, keepdims=True)
-        buf[at, :] = ((total - u * along) * factor[at, :][:, :1]).astype(BF)
-        pltpu.make_async_copy(buf.at[at, :], out.at[at, :], sem).start()
-
-    in_chunks(base.shape[0], body)
+    first, size = 0, base.shape[0] // len(late)
+    for more in late:
+
+        def body(at, first=first, more=more):
+            rows = pl.ds(pl.multiple_of(at.start + first, CHUNK), CHUNK)
+            total = base[rows, :] + more[at, :].astype(F32)
+            u = unit[rows, :]
+            along = jnp.sum(u * total, axis=1, keepdims=True)
+            buf[rows, :] = ((total - u * along) * factor[rows, :][:, :1]).astype(BF)
+            pltpu.make_async_copy(buf.at[rows, :], out.at[rows, :], sem).start()
+
+        in_chunks(size, body)
+        first += size
     pltpu.make_async_copy(buf, out, sem).wait()
 
 
-def image_kernel(count, base, line, unit, factor, late, ready, grad_ref, loss_ref, done, buf, sem):
-    rows = base.shape[0]
+def image_kernel(count, base, line, unit, factor, sum_a, sum_b, ready, grad_ref, loss_ref, done, buf, sem):
+    half = base.shape[0] // 2
     done[...] = jnp.zeros(done.shape, F32)
-    tail = jnp.sum(late[rows:, :rows].astype(F32), axis=0, keepdims=True)
-    loss_ref[...] = (line[:1, :] + tail) * (1.0 / count)
-    tangent_rows(base, late, unit, factor, grad_ref, buf, sem)
+    lines = [jnp.sum(s[half:, :half].astype(F32), axis=0, keepdims=True) for s in (sum_a, sum_b)]
+    loss_ref[...] = (line[:1, :] + jnp.concatenate(lines, axis=1)) * (1.0 / count)
+    tangent_rows(base, [sum_a, sum_b], unit, factor, grad_ref, buf, sem)
 
 
 def text_kernel(base, unit, factor, late, done, grad_ref, buf, sem):
-    tangent_rows(base, late, unit, factor, grad_ref, buf, sem)
+    tangent_rows(base, [late], unit, factor, grad_ref, buf, sem)
 
 
 def final(kernel, name, inputs, shape, more):
@@ -318,35 +336,34 @@
     far_t = [txt_y, move(txt_y, dc=1)]
     t_unit, t_factor = prepare(scal, text_embeds, "prep_text", [txt_y])
     (own_y, own_yc), s_own = rows_step("own_y", scal, own, far_t, s_own, after=[t_factor])
-    (first_y, first_yc), (g_prev_a, g_next_b) = rows_step(
-        "first_y", scal, first, far_t, s_first, finish=2, after=s_own[1:]
-    )
-    home_a0, home_b0 = move(g_prev_a, dz=-1), move(g_next_b, dz=1)
-    (last,) = merge("merge_last", prev_b, next_a, [g_prev_a])
+    (last,) = merge("merge_last", prev_b, next_a, s_own[1:])
     (last_0, last_c, last_y, last_yc), (g_prev_b, g_next_a) = rows_step(
         "last", scal, last, near_t + far_t, finish=2
     )
-    home_b1, home_a1 = move(g_prev_b, dz=-1), move(g_next_a, dz=1)
+    near_b, near_a = move(g_prev_b, dz=-1), move(g_next_a, dz=1)
     (far,) = merge("merge_far", far_a, far_b, [g_prev_b])
-    (far_0, far_c, far_y, far_yc), (g_far,) = rows_step("far", scal, far, near_t + far_t, finish=1)
-    home_far = move(g_far, dz=2)
+    (far_0, far_c, far_y, far_yc), (g_far_a, g_far_b) = rows_step("far", scal, far, near_t + far_t, finish=2)
+    through_a, through_b = move(g_far_a, dz=-1), move(g_far_b, dz=1)
+    (first_y, first_yc), s_first = rows_step("first_y", scal, first, far_t, s_first, after=[g_far_a])
     images = [own, first, last, far]
-    (gt_yc,) = cols_step(
-        "cols_yc", [[own_yc], [first_yc], [last_yc], [far_yc]], images, (BF,), after=[g_far, home_a0, home_b0]
-    )
+    (gt_yc,) = cols_step("cols_yc", [[own_yc], [first_yc], [last_yc], [far_yc]], images, (BF,))
     through_y = move(gt_yc, dc=1)
     (gt_y,) = cols_step("cols_y", [[own_y], [first_y], [last_y], [far_y]], images, (F32,), after=[gt_yc])
     sum_y = add("add_y", gt_y, through_y)
     text_y = move(sum_y, dy=1)
-    (gt_c,) = cols_step("cols_c", [[own_c], [first_c], [last_c], [far_c]], images, (BF,), after=[sum_y])
+    (gt_c,) = cols_step(
+        "cols_c", [[own_c], [first_c], [last_c], [far_c]], images, (BF,), after=[sum_y, near_a, near_b]
+    )
     text_c = move(gt_c, dc=1)
+    to_prev, to_next = sums("sums", s_first, [through_a, through_b], [gt_c])
+    sum_a, sum_b = move(to_prev, dz=-1), move(to_next, dz=1)
     (gt_own,) = cols_step(
-        "cols_own", [[own_0], [first_0], [last_0], [far_0]], images, (F32,), after=[gt_c]
+        "cols_own", [[own_0], [first_0], [last_0], [far_0]], images, (F32,), after=[to_prev]
     )
     i_base, line = call(
         image_base_kernel,
         "image_base",
-        [*s_own, home_a0, home_a1, home_b0, home_b1],
+        [*s_own, near_a, near_b],
         [pltpu.VMEM((rows, width), F32), pltpu.VMEM((8, rows), F32)],
         [gt_own],
         cost=1000,
@@ -357,7 +374,7 @@
     grad_image, loss, done = final(
         functools.partial(image_kernel, total),
         "image",
-        [i_base, line, i_unit, i_factor, home_far, t_base],
+        [i_base, line, i_unit, i_factor, sum_a, sum_b, t_base],
         (rows, width),
         [jax.ShapeDtypeStruct((1, rows), F32), pltpu.VMEM((8, 128), F32)],
     )

time: 109 us -> 106 us (0.972)
  waiting for transfers between devices: 26.6 us -> 20.2 us
  starting transfers between devices: 25 us -> 27.9 us
    ppermute x17 -> x18, waiting for transfers between devices: 26.6 us -> 20.2 us  [move(): return lax.ppermute(value, 'loss', pairs)]
    ppermute x17 -> x18, starting transfers between devices: 25 us -> 27.9 us  [move(): return lax.ppermute(value, 'loss', pairs)]
    unnamed x14 -> x18, local copies, waits for them, and re-layouts: 2.64 us -> 3.34 us
    pallas_call x22 -> x23, Pallas kernels: 47.2 us -> 47.3 us  [call(): pl.pallas_call(body, name=name, in_specs=specs, out_specs=[VMEM] * len(ou...]
  transfers between devices with their start and end apart: 17 -> 18, of which waited for: 4 -> 5; matrix products, arithmetic and copies ran while one was open for 0% -> 0% of each run, Pallas kernels for 45% -> 47%
where the time goes in v4:
time: 106 us; the launch traced here: 105 us
  Pallas kernels  51.4 us (48%)
  starting transfers between devices  27.9 us (26%)
  waiting for transfers between devices  20.2 us (19%)
  local copies, waits for them, and re-layouts  3.34 us (3%)
  between operations  2.46 us (2%)
    pallas_call x23, Pallas kernels, call(): pl.pallas_call(body, name=name, in_specs=specs, out_specs=[VMEM] * len(ou...  47.3 us
    ppermute x18, starting transfers between devices, move(): return lax.ppermute(value, 'loss', pairs)  27.9 us
    ppermute x18, waiting for transfers between devices, move(): return lax.ppermute(value, 'loss', pairs)  20.2 us
    pallas_call x2, Pallas kernels, final(): pl.pallas_call(kernel, name=name, in_specs=[VMEM] * len(inputs), out_spec...  4.14 us
    unnamed x18, local copies, waits for them, and re-layouts  3.34 us
  transfers between devices with their start and end apart: 18, of which 5 were waited for; matrix products, arithmetic and copies ran while one was open for 0% of the time, Pallas kernels for 47%

profile of v4, /device:TPU:0, one launch (start us, length us, event | category | flops | bytes accessed | tf_op | source)
XLA Modules:
  0.0 105.4 jit_solution(18057235148438288330)
XLA Ops:
  0.7 1.4 %copy-done.7 = bf16[512,1152]{1,0:T(8,128)(2,1)S(1)} copy-done((bf16[512,1152]{1,0:T(8,128)(2,1)S(1)}, bf16[512,1152]{1,0:T(8,128)(2,1)}, u32[]{:S(2)}) %copy-start.7) | copy-done | bytes 1179672
  2.0 0.6 norm_text.1.refs_1_.refs_2_
  2.6 0.1 collective-permute-start.3
  2.7 3.4 %collective-permute-start = (bf16[512,1152]{1,0:T(8,128)(2,1)S(1)}, bf16[512,1152]{1,0:T(8,128)(2,1)S(1)}, u32[]{:S(2)}, u32[]{:S(2)}) collective-permute-start(bf16[512,1152]{1,0:T(8,128)(2,1)S(1)} %norm_text.1.refs_1_.refs_2_), channel_id=1, source_target_pairs={{0,2},{1,3},{2,0},{3,1},{4,6},{5,7},{6,4},{7,5},{8,10},{9,11},{10,... | collective-permute-start | bytes 3538952 | tf_op jit(solution)/shard_map/ppermute | solution.py:318
  6.1 0.7 norm_image.1
  6.7 2.0 %collective-permute-start.1 = (bf16[256,1152]{1,0:T(8,128)(2,1)S(1)}, bf16[256,1152]{1,0:T(8,128)(2,1)S(1)}, u32[]{:S(2)}, u32[]{:S(2)}) collective-permute-start(bf16[256,1152]{1,0:T(8,128)(2,1)S(1)} %get-tuple-element.51.refs_0_), channel_id=1, source_target_pairs={{0,4},{1,5},{2,6},{3,7},{4,8},{5,9},{6,10},{7,11},{8,12},{9,13},{1... | collective-permute-start | bytes 1769480 | tf_op jit(solution)/shard_map/ppermute | solution.py:318
  8.7 2.2 %collective-permute-start.2 = (bf16[256,1152]{1,0:T(8,128)(2,1)S(1)}, bf16[256,1152]{1,0:T(8,128)(2,1)S(1)}, u32[]{:S(2)}, u32[]{:S(2)}) collective-permute-start(bf16[256,1152]{1,0:T(8,128)(2,1)S(1)} %get-tuple-element.52.refs_1_), channel_id=1, source_target_pairs={{0,12},{1,13},{2,14},{3,15},{4,0},{5,1},{6,2},{7,3},{8,4},{9,5},{1... | collective-permute-start | bytes 1769480 | tf_op jit(solution)/shard_map/ppermute | solution.py:318
  12.3 0.1 hold_last.1
  12.5 3.2 %collective-permute-start.6 = (bf16[256,1152]{1,0:T(8,128)(2,1)S(1)}, bf16[256,1152]{1,0:T(8,128)(2,1)S(1)}, u32[]{:S(2)}, u32[]{:S(2)}) collective-permute-start(bf16[256,1152]{1,0:T(8,128)(2,1)S(1)} %get-tuple-element.53.refs_4_), channel_id=1, source_target_pairs={{0,12},{1,13},{2,14},{3,15},{4,0},{5,1},{6,2},{7,3},{8,4},{9,5},{1... | collective-permute-start | bytes 1769480 | tf_op jit(solution)/shard_map/ppermute | solution.py:318
  15.7 4.1 %own_c.1 = (bf16[512,512]{1,0:T(8,128)(2,1)S(1)}, bf16[512,512]{1,0:T(8,128)(2,1)S(1)}, f32[512,1152]{1,0:T(8,128)S(1)}, f32[512,128]{1,0:T(8,128)S(1)}) custom-call(f32[3]{0:T(128)S(1)} %pad_maximum_fusion.refs_0_, bf16[512,1152]{1,0:T(8,128)(2,1)S(1)} %get-tuple-element.50.refs_1_.refs_4_, bf16[512,1152]{1,0:T(8,128)(2,1)S(1)} %norm_text.1.refs_1_.refs_2_, ...), custom_call_target="tpu_custom_call" | custom-call | flops 20000000000 | tf_op jit(solution)/shard_map/own_c/pallas_call | solution.py:30
  19.8 5.2 %collective-permute-done.1.refs_0_ = bf16[256,1152]{1,0:T(8,128)(2,1)S(1)} collective-permute-done((bf16[256,1152]{1,0:T(8,128)(2,1)S(1)}, bf16[256,1152]{1,0:T(8,128)(2,1)S(1)}, u32[]{:S(2)}, u32[]{:S(2)}) %collective-permute-start.1) | collective-permute-done | bytes 589856 | tf_op jit(solution)/shard_map/ppermute | solution.py:318
  25.0 0.2 merge_first.1
  25.1 2.0 %collective-permute-start.9 = (bf16[256,1152]{1,0:T(8,128)(2,1)S(1)}, bf16[256,1152]{1,0:T(8,128)(2,1)S(1)}, u32[]{:S(2)}, u32[]{:S(2)}) collective-permute-start(bf16[256,1152]{1,0:T(8,128)(2,1)S(1)} %get-tuple-element.68), channel_id=1, source_target_pairs={{0,4},{1,5},{2,6},{3,7},{4,8},{5,9},{6,10},{7,11},{8,12},{9,13},{1... | collective-permute-start | bytes 1769480 | tf_op jit(solution)/shard_map/ppermute | solution.py:318
  27.1 1.5 %collective-permute-start.10 = (bf16[256,1152]{1,0:T(8,128)(2,1)S(1)}, bf16[256,1152]{1,0:T(8,128)(2,1)S(1)}, u32[]{:S(2)}, u32[]{:S(2)}) collective-permute-start(bf16[256,1152]{1,0:T(8,128)(2,1)S(1)} %get-tuple-element.69), channel_id=1, source_target_pairs={{0,12},{1,13},{2,14},{3,15},{4,0},{5,1},{6,2},{7,3},{8,4},{9,5},{1... | collective-permute-start | bytes 1769480 | tf_op jit(solution)/shard_map/ppermute | solution.py:318
  28.6 3.8 %first_c.1 = (bf16[512,512]{1,0:T(8,128)(2,1)S(1)}, bf16[512,512]{1,0:T(8,128)(2,1)S(1)}, f32[512,1152]{1,0:T(8,128)S(1)}, f32[512,128]{1,0:T(8,128)S(1)}) custom-call(f32[3]{0:T(128)S(1)} %pad_maximum_fusion.refs_0_, bf16[512,1152]{1,0:T(8,128)(2,1)S(1)} %get-tuple-element.55.refs_1_.refs_5_, bf16[512,1152]{1,0:T(8,128)(2,1)S(1)} %norm_text.1.refs_1_.refs_2_, ...), custom_call_target="tpu_custom_call" | custom-call | flops 20000000000 | tf_op jit(solution)/shard_map/first_c/pallas_call | solution.py:30
  32.4 1.1 %prep_image.1 = (f32[512,1152]{1,0:T(8,128)S(1)}, f32[512,128]{1,0:T(8,128)S(1)}) custom-call(f32[3]{0:T(128)S(1)} %pad_maximum_fusion.refs_0_, bf16[512,1152]{1,0:T(8,128)(2,1)S(1)} %copy-done.6, f32[512,128]{1,0:T(8,128)S(1)} %get-tuple-element.56.refs_2_.refs_5_), custom_call_target="tpu_custom_call" | custom-call | flops 20000000000 | tf_op jit(solution)/shard_map/prep_image/pallas_call | solution.py:30
  33.6 0.1 hold_text.1.refs_2_.refs_4_
  33.7 0.6 copy-done
  34.3 0.7 copy-done.8
  34.9 1.1 %prep_text.1 = (f32[512,1152]{1,0:T(8,128)S(1)}, f32[512,128]{1,0:T(8,128)S(1)}) custom-call(f32[3]{0:T(128)S(1)} %pad_maximum_fusion.refs_0_, bf16[512,1152]{1,0:T(8,128)(2,1)S(1)} %copy-done.8, bf16[512,1152]{1,0:T(8,128)(2,1)S(1)} %hold_text.1.refs_2_.refs_4_), custom_call_target="tpu_custom_call" | custom-call | flops 20000000000 | tf_op jit(solution)/shard_map/prep_text/pallas_call | solution.py:30
  36.1 1.0 collective-permute-done.4.refs_3_.refs_5_
  37.1 4.3 %own_y.1 = (bf16[512,512]{1,0:T(8,128)(2,1)S(1)}, bf16[512,512]{1,0:T(8,128)(2,1)S(1)}, f32[512,1152]{1,0:T(8,128)S(1)}, f32[512,128]{1,0:T(8,128)S(1)}) custom-call(f32[3]{0:T(128)S(1)} %pad_maximum_fusion.refs_0_, bf16[512,1152]{1,0:T(8,128)(2,1)S(1)} %get-tuple-element.50.refs_1_.refs_4_, bf16[512,1152]{1,0:T(8,128)(2,1)S(1)} %hold_text.1.refs_2_.refs_4_, ...), custom_call_target="tpu_custom_call" | custom-call | flops 20000000000 | tf_op jit(solution)/shard_map/own_y/pallas_call | solution.py:30
  41.5 0.1 merge_last.1.refs_1_.refs_6_
  41.6 0.7 copy-done.2
  42.3 6.8 %last.1 = (bf16[512,512]{1,0:T(8,128)(2,1)S(1)}, bf16[512,512]{1,0:T(8,128)(2,1)S(1)}, bf16[512,512]{1,0:T(8,128)(2,1)S(1)}, bf16[512,512]{1,0:T(8,128)(2,1)S(1)...) custom-call(f32[3]{0:T(128)S(1)} %pad_maximum_fusion.refs_0_, ...), custom_call_target="tpu_custom_call" | custom-call | flops 20000000000 | tf_op jit(solution)/shard_map/last/pallas_call | solution.py:30
  49.1 0.6 collective-permute-start.7
  49.7 2.7 %collective-permute-start.8 = (bf16[272,1152]{1,0:T(8,128)(2,1)S(1)}, bf16[272,1152]{1,0:T(8,128)(2,1)S(1)}, u32[]{:S(2)}, u32[]{:S(2)}) collective-permute-start(bf16[272,1152]{1,0:T(8,128)(2,1)S(1)} %get-tuple-element.64.refs_2_), channel_id=1, source_target_pairs={{0,12},{1,13},{2,14},{3,15},{4,0},{5,1},{6,2},{7,3},{8,4},{9,5},{1... | collective-permute-start | bytes 1880072 | tf_op jit(solution)/shard_map/ppermute | solution.py:318
  52.4 0.1 merge_far.1.refs_1_.refs_7_
  52.5 6.8 %far.1 = (bf16[512,512]{1,0:T(8,128)(2,1)S(1)}, bf16[512,512]{1,0:T(8,128)(2,1)S(1)}, bf16[512,512]{1,0:T(8,128)(2,1)S(1)}, bf16[512,512]{1,0:T(8,128)(2,1)S(1)}...) custom-call(f32[3]{0:T(128)S(1)} %pad_maximum_fusion.refs_0_, ...), custom_call_target="tpu_custom_call" | custom-call | flops 20000000000 | tf_op jit(solution)/shard_map/far/pallas_call | solution.py:30
  59.4 3.2 %collective-permute-start.11 = (bf16[272,1152]{1,0:T(8,128)(2,1)S(1)}, bf16[272,1152]{1,0:T(8,128)(2,1)S(1)}, u32[]{:S(2)}, u32[]{:S(2)}) collective-permute-start(bf16[272,1152]{1,0:T(8,128)(2,1)S(1)} %get-tuple-element.72.refs_6_), channel_id=1, source_target_pairs={{0,12},{1,13},{2,14},{3,15},{4,0},{5,1},{6,2},{7,3},{8,4},{9,5},{1... | collective-permute-start | bytes 1880072 | tf_op jit(solution)/shard_map/ppermute | solution.py:318
  62.6 4.3 %first_y.1 = (bf16[512,512]{1,0:T(8,128)(2,1)S(1)}, bf16[512,512]{1,0:T(8,128)(2,1)S(1)}, f32[512,1152]{1,0:T(8,128)S(1)}, f32[512,128]{1,0:T(8,128)S(1)}) custom-call(f32[3]{0:T(128)S(1)} %pad_maximum_fusion.refs_0_, bf16[512,1152]{1,0:T(8,128)(2,1)S(1)} %get-tuple-element.55.refs_1_.refs_5_, bf16[512,1152]{1,0:T(8,128)(2,1)S(1)} %hold_text.1.refs_2_.refs_4_, ...), custom_call_target="tpu_custom_call" | custom-call | flops 20000000000 | tf_op jit(solution)/shard_map/first_y/pallas_call | solution.py:30
  67.0 3.0 %cols_yc.1.refs_8_ = bf16[512,1152]{1,0:T(8,128)(2,1)S(1)} custom-call(bf16[512,512]{1,0:T(8,128)(2,1)S(1)} %get-tuple-element.84.refs_0_, bf16[512,512]{1,0:T(8,128)(2,1)S(1)} %get-tuple-element.85.refs_1_, bf16[512,512]{1,0:T(8,128)(2,1)S(1)} %get-tuple-element.86.refs_2_, bf16[512,512]{1,0:T(8,128)(2,1)S(1)} %get-tuple-element.87.refs_3_, ...), custom_call_target="tpu_custom_call" | custom-call | flops 20000000000 | tf_op jit(solution)/shard_map/cols_yc/pallas_call | solution.py:30
  70.1 3.0 %cols_y.1.refs_0_ = f32[512,1152]{1,0:T(8,128)S(1)} custom-call(bf16[512,512]{1,0:T(8,128)(2,1)S(1)} %get-tuple-element.80.refs_0_, bf16[512,512]{1,0:T(8,128)(2,1)S(1)} %get-tuple-element.81.refs_1_, bf16[512,512]{1,0:T(8,128)(2,1)S(1)} %get-tuple-element.82.refs_2_, bf16[512,512]{1,0:T(8,128)(2,1)S(1)} %get-tuple-element.83.refs_3_, ...), custom_call_target="tpu_custom_call" | custom-call | flops 20000000000 | tf_op jit(solution)/shard_map/cols_y/pallas_call | solution.py:30
  73.0 0.2 add_y.1.refs_8_
  73.2 3.1 %collective-permute-start.17 = (bf16[512,1152]{1,0:T(8,128)(2,1)S(1)}, bf16[512,1152]{1,0:T(8,128)(2,1)S(1)}, u32[]{:S(2)}, u32[]{:S(2)}) collective-permute-start(bf16[512,1152]{1,0:T(8,128)(2,1)S(1)} %add_y.1.refs_8_), channel_id=1, source_target_pairs={{0,2},{1,3},{2,0},{3,1},{4,6},{5,7},{6,4},{7,5},{8,10},{9,11},{10,... | collective-permute-start | bytes 3538952 | tf_op jit(solution)/shard_map/ppermute | solution.py:318
  76.4 3.0 %cols_c.1.refs_4_ = bf16[512,1152]{1,0:T(8,128)(2,1)S(1)} custom-call(bf16[512,512]{1,0:T(8,128)(2,1)S(1)} %get-tuple-element.76.refs_0_, bf16[512,512]{1,0:T(8,128)(2,1)S(1)} %get-tuple-element.77.refs_1_, bf16[512,512]{1,0:T(8,128)(2,1)S(1)} %get-tuple-element.78.refs_2_, bf16[512,512]{1,0:T(8,128)(2,1)S(1)} %get-tuple-element.79.refs_3_, ...), custom_call_target="tpu_custom_call" | custom-call | flops 20000000000 | tf_op jit(solution)/shard_map/cols_c/pallas_call | solution.py:30
  79.4 0.3 collective-permute-start.16
  79.6 0.3 collective-permute-done.12.refs_3_
  80.0 0.5 sums.1
  80.5 1.0 collective-permute-start.15
  81.5 2.3 %collective-permute-start.14 = (bf16[272,1152]{1,0:T(8,128)(2,1)S(1)}, bf16[272,1152]{1,0:T(8,128)(2,1)S(1)}, u32[]{:S(2)}, u32[]{:S(2)}) collective-permute-start(bf16[272,1152]{1,0:T(8,128)(2,1)S(1)} %get-tuple-element.88.refs_8_), channel_id=1, source_target_pairs={{0,12},{1,13},{2,14},{3,15},{4,0},{5,1},{6,2},{7,3},{8,4},{9,5},{1... | collective-permute-start | bytes 1880072 | tf_op jit(solution)/shard_map/ppermute | solution.py:318
  83.8 3.0 %cols_own.1.refs_4_.refs_0_ = f32[512,1152]{1,0:T(8,128)S(1)} custom-call(bf16[512,512]{1,0:T(8,128)(2,1)S(1)} %get-tuple-element.65.refs_0_, bf16[512,512]{1,0:T(8,128)(2,1)S(1)} %get-tuple-element.66.refs_1_, bf16[512,512]{1,0:T(8,128)(2,1)S(1)} %get-tuple-element.67.refs_2_, bf16[512,512]{1,0:T(8,128)(2,1)S(1)} %get-tuple-element.70.refs_3_, ...), custom_call_target="tpu_custom_call" | custom-call | flops 20000000000 | tf_op jit(solution)/shard_map/cols_own/pallas_call | solution.py:30
  86.8 0.4 image_base.1
  87.2 0.2 text_base.1.ready.base
  87.4 10.4 %collective-permute-done.15.sum_b = bf16[272,1152]{1,0:T(8,128)(2,1)S(1)} collective-permute-done((bf16[272,1152]{1,0:T(8,128)(2,1)S(1)}, bf16[272,1152]{1,0:T(8,128)(2,1)S(1)}, u32[]{:S(2)}, u32[]{:S(2)}) %collective-permute-start.15) | collective-permute-done | bytes 626720 | tf_op jit(solution)/shard_map/ppermute | solution.py:318
  97.8 2.4 %image.1 = (bf16[512,1152]{1,0:T(8,128)(2,1)}, f32[1,512]{1,0:T(1,128)}, f32[8,128]{1,0:T(8,128)S(1)}) custom-call(f32[512,1152]{1,0:T(8,128)S(1)} %get-tuple-element.89.base, f32[8,512]{1,0:T(8,128)S(1)} %get-tuple-element.90.refs_2_.line, f32[512,1152]{1,0:T(8,128)S(1)} %get-tuple-element.91.unit, f32[512,128]{1,0:T(8,128)S(1)} %copy-done.1, ...), custom_call_target="tpu_custom_call" | custom-call | flops 1000 | tf_op jit(solution)/shard_map/image/pallas_call | solution.py:298
  100.2 3.2 %collective-permute-done.17.late = bf16[512,1152]{1,0:T(8,128)(2,1)S(1)} collective-permute-done((bf16[512,1152]{1,0:T(8,128)(2,1)S(1)}, bf16[512,1152]{1,0:T(8,128)(2,1)S(1)}, u32[]{:S(2)}, u32[]{:S(2)}) %collective-permute-start.17) | collective-permute-done | bytes 1179680 | tf_op jit(solution)/shard_map/ppermute | solution.py:318
  103.4 1.8 %text.1 = bf16[512,1152]{1,0:T(8,128)(2,1)} custom-call(f32[512,1152]{1,0:T(8,128)S(1)} %text_base.1.ready.base, f32[512,1152]{1,0:T(8,128)S(1)} %get-tuple-element.95.unit, f32[512,128]{1,0:T(8,128)S(1)} %copy-done.5, bf16[512,1152]{1,0:T(8,128)(2,1)S(1)} %collective-permute-done.17.late, f32[8,128]{1,0:T(8,128)S(1)} %get-tuple-element.96.done), custom_call_target="tpu_custom_call" | custom-call | flops 1000 | tf_op jit(solution)/shard_map/text/pallas_call | solution.py:298
  (32 shorter events, 0.4 us)
Async XLA Ops:
  0.6 5.4 %copy-start.6 = (bf16[512,1152]{1,0:T(8,128)(2,1)S(1)}, bf16[512,1152]{1,0:T(8,128)(2,1)}, u32[]{:S(2)}) copy-start(bf16[512,1152]{1,0:T(8,128)(2,1)} %refs_1_.2) | copy-start | bytes 3538948
  0.6 1.4 %copy-start.7 = (bf16[512,1152]{1,0:T(8,128)(2,1)S(1)}, bf16[512,1152]{1,0:T(8,128)(2,1)}, u32[]{:S(2)}) copy-start(bf16[512,1152]{1,0:T(8,128)(2,1)} %refs_1_.3) | copy-start | bytes 3538948
  2.6 9.7 %collective-permute-start.3 = (bf16[512,1152]{1,0:T(8,128)(2,1)S(1)}, bf16[512,1152]{1,0:T(8,128)(2,1)S(1)}, u32[]{:S(2)}, u32[]{:S(2)}) collective-permute-start(bf16[512,1152]{1,0:T(8,128)(2,1)S(1)} %norm_text.1.refs_1_.refs_2_), channel_id=1, source_target_pairs={{0,1},{1,0},{2,3},{3,2},{4,5},{5,4},{6,7},{7,6},{8,9},{9,8},{10,11... | collective-permute-start | bytes 3538952 | tf_op jit(solution)/shard_map/ppermute | solution.py:318
  2.7 30.9 %collective-permute-start = (bf16[512,1152]{1,0:T(8,128)(2,1)S(1)}, bf16[512,1152]{1,0:T(8,128)(2,1)S(1)}, u32[]{:S(2)}, u32[]{:S(2)}) collective-permute-start(bf16[512,1152]{1,0:T(8,128)(2,1)S(1)} %norm_text.1.refs_1_.refs_2_), channel_id=1, source_target_pairs={{0,2},{1,3},{2,0},{3,1},{4,6},{5,7},{6,4},{7,5},{8,10},{9,11},{10,... | collective-permute-start | bytes 3538952 | tf_op jit(solution)/shard_map/ppermute | solution.py:318
  6.7 18.2 %collective-permute-start.1 = (bf16[256,1152]{1,0:T(8,128)(2,1)S(1)}, bf16[256,1152]{1,0:T(8,128)(2,1)S(1)}, u32[]{:S(2)}, u32[]{:S(2)}) collective-permute-start(bf16[256,1152]{1,0:T(8,128)(2,1)S(1)} %get-tuple-element.51.refs_0_), channel_id=1, source_target_pairs={{0,4},{1,5},{2,6},{3,7},{4,8},{5,9},{6,10},{7,11},{8,12},{9,13},{1... | collective-permute-start | bytes 1769480 | tf_op jit(solution)/shard_map/ppermute | solution.py:318
  8.7 16.2 %collective-permute-start.2 = (bf16[256,1152]{1,0:T(8,128)(2,1)S(1)}, bf16[256,1152]{1,0:T(8,128)(2,1)S(1)}, u32[]{:S(2)}, u32[]{:S(2)}) collective-permute-start(bf16[256,1152]{1,0:T(8,128)(2,1)S(1)} %get-tuple-element.52.refs_1_), channel_id=1, source_target_pairs={{0,12},{1,13},{2,14},{3,15},{4,0},{5,1},{6,2},{7,3},{8,4},{9,5},{1... | collective-permute-start | bytes 1769480 | tf_op jit(solution)/shard_map/ppermute | solution.py:318
  12.4 29.0 %collective-permute-start.5 = (bf16[256,1152]{1,0:T(8,128)(2,1)S(1)}, bf16[256,1152]{1,0:T(8,128)(2,1)S(1)}, u32[]{:S(2)}, u32[]{:S(2)}) collective-permute-start(bf16[256,1152]{1,0:T(8,128)(2,1)S(1)} %get-tuple-element.62), channel_id=1, source_target_pairs={{0,4},{1,5},{2,6},{3,7},{4,8},{5,9},{6,10},{7,11},{8,12},{9,13},{1... | collective-permute-start | bytes 1769480 | tf_op jit(solution)/shard_map/ppermute | solution.py:318
  12.5 29.0 %collective-permute-start.6 = (bf16[256,1152]{1,0:T(8,128)(2,1)S(1)}, bf16[256,1152]{1,0:T(8,128)(2,1)S(1)}, u32[]{:S(2)}, u32[]{:S(2)}) collective-permute-start(bf16[256,1152]{1,0:T(8,128)(2,1)S(1)} %get-tuple-element.53.refs_4_), channel_id=1, source_target_pairs={{0,12},{1,13},{2,14},{3,15},{4,0},{5,1},{6,2},{7,3},{8,4},{9,5},{1... | collective-permute-start | bytes 1769480 | tf_op jit(solution)/shard_map/ppermute | solution.py:318
  25.1 27.3 %collective-permute-start.9 = (bf16[256,1152]{1,0:T(8,128)(2,1)S(1)}, bf16[256,1152]{1,0:T(8,128)(2,1)S(1)}, u32[]{:S(2)}, u32[]{:S(2)}) collective-permute-start(bf16[256,1152]{1,0:T(8,128)(2,1)S(1)} %get-tuple-element.68), channel_id=1, source_target_pairs={{0,4},{1,5},{2,6},{3,7},{4,8},{5,9},{6,10},{7,11},{8,12},{9,13},{1... | collective-permute-start | bytes 1769480 | tf_op jit(solution)/shard_map/ppermute | solution.py:318
  27.1 25.3 %collective-permute-start.10 = (bf16[256,1152]{1,0:T(8,128)(2,1)S(1)}, bf16[256,1152]{1,0:T(8,128)(2,1)S(1)}, u32[]{:S(2)}, u32[]{:S(2)}) collective-permute-start(bf16[256,1152]{1,0:T(8,128)(2,1)S(1)} %get-tuple-element.69), channel_id=1, source_target_pairs={{0,12},{1,13},{2,14},{3,15},{4,0},{5,1},{6,2},{7,3},{8,4},{9,5},{1... | collective-permute-start | bytes 1769480 | tf_op jit(solution)/shard_map/ppermute | solution.py:318
  33.6 0.7 copy-start
  33.6 1.4 %copy-start.8 = (bf16[512,1152]{1,0:T(8,128)(2,1)S(1)}, bf16[512,1152]{1,0:T(8,128)(2,1)}, u32[]{:S(2)}) copy-start(bf16[512,1152]{1,0:T(8,128)(2,1)} %refs_1_.3) | copy-start | bytes 3538948
  34.3 2.8 %collective-permute-start.4 = (bf16[512,1152]{1,0:T(8,128)(2,1)S(1)}, bf16[512,1152]{1,0:T(8,128)(2,1)S(1)}, u32[]{:S(2)}, u32[]{:S(2)}) collective-permute-start(bf16[512,1152]{1,0:T(8,128)(2,1)S(1)} %hold_text.1.refs_2_.refs_4_), channel_id=1, source_target_pairs={{0,1},{1,0},{2,3},{3,2},{4,5},{5,4},{6,7},{7,6},{8,9},{9,8},{10,11... | collective-permute-start | bytes 3538952 | tf_op jit(solution)/shard_map/ppermute | solution.py:318
  36.1 5.4 %copy-start.4 = (f32[512,128]{1,0:T(8,128)}, f32[512,128]{1,0:T(8,128)S(1)}, u32[]{:S(2)}) copy-start(f32[512,128]{1,0:T(8,128)S(1)} %get-tuple-element.59.refs_6_.factor) | copy-start | bytes 786436
  41.6 0.7 copy-start.2
  49.1 27.3 %collective-permute-start.7 = (bf16[272,1152]{1,0:T(8,128)(2,1)S(1)}, bf16[272,1152]{1,0:T(8,128)(2,1)S(1)}, u32[]{:S(2)}, u32[]{:S(2)}) collective-permute-start(bf16[272,1152]{1,0:T(8,128)(2,1)S(1)} %get-tuple-element.63), channel_id=1, source_target_pairs={{0,4},{1,5},{2,6},{3,7},{4,8},{5,9},{6,10},{7,11},{8,12},{9,13},{1... | collective-permute-start | bytes 1880072 | tf_op jit(solution)/shard_map/ppermute | solution.py:318
  49.7 26.7 %collective-permute-start.8 = (bf16[272,1152]{1,0:T(8,128)(2,1)S(1)}, bf16[272,1152]{1,0:T(8,128)(2,1)S(1)}, u32[]{:S(2)}, u32[]{:S(2)}) collective-permute-start(bf16[272,1152]{1,0:T(8,128)(2,1)S(1)} %get-tuple-element.64.refs_2_), channel_id=1, source_target_pairs={{0,12},{1,13},{2,14},{3,15},{4,0},{5,1},{6,2},{7,3},{8,4},{9,5},{1... | collective-permute-start | bytes 1880072 | tf_op jit(solution)/shard_map/ppermute | solution.py:318
  59.3 20.7 %collective-permute-start.12 = (bf16[272,1152]{1,0:T(8,128)(2,1)S(1)}, bf16[272,1152]{1,0:T(8,128)(2,1)S(1)}, u32[]{:S(2)}, u32[]{:S(2)}) collective-permute-start(bf16[272,1152]{1,0:T(8,128)(2,1)S(1)} %get-tuple-element.75), channel_id=1, source_target_pairs={{0,4},{1,5},{2,6},{3,7},{4,8},{5,9},{6,10},{7,11},{8,12},{9,13},{1... | collective-permute-start | bytes 1880072 | tf_op jit(solution)/shard_map/ppermute | solution.py:318
  59.4 20.6 %collective-permute-start.11 = (bf16[272,1152]{1,0:T(8,128)(2,1)S(1)}, bf16[272,1152]{1,0:T(8,128)(2,1)S(1)}, u32[]{:S(2)}, u32[]{:S(2)}) collective-permute-start(bf16[272,1152]{1,0:T(8,128)(2,1)S(1)} %get-tuple-element.72.refs_6_), channel_id=1, source_target_pairs={{0,12},{1,13},{2,14},{3,15},{4,0},{5,1},{6,2},{7,3},{8,4},{9,5},{1... | collective-permute-start | bytes 1880072 | tf_op jit(solution)/shard_map/ppermute | solution.py:318
  70.0 3.1 %collective-permute-start.13 = (bf16[512,1152]{1,0:T(8,128)(2,1)S(1)}, bf16[512,1152]{1,0:T(8,128)(2,1)S(1)}, u32[]{:S(2)}, u32[]{:S(2)}) collective-permute-start(bf16[512,1152]{1,0:T(8,128)(2,1)S(1)} %cols_yc.1.refs_8_), channel_id=1, source_target_pairs={{0,1},{1,0},{2,3},{3,2},{4,5},{5,4},{6,7},{7,6},{8,9},{9,8},{10,11... | collective-permute-start | bytes 3538952 | tf_op jit(solution)/shard_map/ppermute | solution.py:318
  73.2 30.2 %collective-permute-start.17 = (bf16[512,1152]{1,0:T(8,128)(2,1)S(1)}, bf16[512,1152]{1,0:T(8,128)(2,1)S(1)}, u32[]{:S(2)}, u32[]{:S(2)}) collective-permute-start(bf16[512,1152]{1,0:T(8,128)(2,1)S(1)} %add_y.1.refs_8_), channel_id=1, source_target_pairs={{0,2},{1,3},{2,0},{3,1},{4,6},{5,7},{6,4},{7,5},{8,10},{9,11},{10,... | collective-permute-start | bytes 3538952 | tf_op jit(solution)/shard_map/ppermute | solution.py:318
  79.4 7.8 %collective-permute-start.16 = (bf16[512,1152]{1,0:T(8,128)(2,1)S(1)}, bf16[512,1152]{1,0:T(8,128)(2,1)S(1)}, u32[]{:S(2)}, u32[]{:S(2)}) collective-permute-start(bf16[512,1152]{1,0:T(8,128)(2,1)S(1)} %cols_c.1.refs_4_), channel_id=1, source_target_pairs={{0,1},{1,0},{2,3},{3,2},{4,5},{5,4},{6,7},{7,6},{8,9},{9,8},{10,11... | collective-permute-start | bytes 3538952 | tf_op jit(solution)/shard_map/ppermute | solution.py:318
  80.5 17.3 %collective-permute-start.15 = (bf16[272,1152]{1,0:T(8,128)(2,1)S(1)}, bf16[272,1152]{1,0:T(8,128)(2,1)S(1)}, u32[]{:S(2)}, u32[]{:S(2)}) collective-permute-start(bf16[272,1152]{1,0:T(8,128)(2,1)S(1)} %get-tuple-element.92), channel_id=1, source_target_pairs={{0,4},{1,5},{2,6},{3,7},{4,8},{5,9},{6,10},{7,11},{8,12},{9,13},{1... | collective-permute-start | bytes 1880072 | tf_op jit(solution)/shard_map/ppermute | solution.py:318
  81.5 16.3 %collective-permute-start.14 = (bf16[272,1152]{1,0:T(8,128)(2,1)S(1)}, bf16[272,1152]{1,0:T(8,128)(2,1)S(1)}, u32[]{:S(2)}, u32[]{:S(2)}) collective-permute-start(bf16[272,1152]{1,0:T(8,128)(2,1)S(1)} %get-tuple-element.88.refs_8_), channel_id=1, source_target_pairs={{0,12},{1,13},{2,14},{3,15},{4,0},{5,1},{6,2},{7,3},{8,4},{9,5},{1... | collective-permute-start | bytes 1880072 | tf_op jit(solution)/shard_map/ppermute | solution.py:318
  83.8 3.0 %copy-start.3 = (f32[512,128]{1,0:T(8,128)S(1)}, f32[512,128]{1,0:T(8,128)}, u32[]{:S(2)}) copy-start(f32[512,128]{1,0:T(8,128)} %copy-done.2) | copy-start | bytes 786436
  87.2 10.6 %copy-start.1 = (f32[512,128]{1,0:T(8,128)S(1)}, f32[512,128]{1,0:T(8,128)}, u32[]{:S(2)}) copy-start(f32[512,128]{1,0:T(8,128)} %copy-done) | copy-start | bytes 786436
  97.8 5.6 %copy-start.5 = (f32[512,128]{1,0:T(8,128)S(1)}, f32[512,128]{1,0:T(8,128)}, u32[]{:S(2)}) copy-start(f32[512,128]{1,0:T(8,128)} %copy-done.4) | copy-start | bytes 786436

commit v5 on v4

--- a/solution.py
+++ b/solution.py
@@ -63,6 +63,31 @@
     rows, width = raw.shape
     outs = [pltpu.VMEM((rows // p, width), BF) for p in ((1, 2, 2) if halves else (1,))]
     return call(normalize_kernel, name, [raw], outs, after)
+
+
+def normalize_hbm_kernel(raw, whole, buf, sems):
+    chunks = [pl.ds(k * CHUNK, CHUNK) for k in range(raw.shape[0] // CHUNK)]
+    copies = [pltpu.make_async_copy(raw.at[at, :], buf.at[at, :], sems.at[k]) for k, at in enumerate(chunks)]
+    for copy in copies:
+        copy.start()
+    for at, copy in zip(chunks, copies, strict=True):
+        copy.wait()
+        wide = buf[at, :].astype(F32)
+        whole[at, :] = (wide * recip_of(wide)).astype(BF)
+
+
+def normalize_hbm(raw, name):
+    rows, width = raw.shape
+    return pl.pallas_call(
+        normalize_hbm_kernel,
+        name=name,
+        in_specs=[pl.BlockSpec(memory_space=pl.ANY)],
+        out_specs=VMEM,
+        out_shape=pltpu.VMEM((rows, width), BF),
+        scratch_shapes=[pltpu.VMEM((rows, width), BF), pltpu.SemaphoreType.DMA((rows // CHUNK,))],
+        cost_estimate=pl.CostEstimate(flops=COST, bytes_accessed=0, transcendentals=0),
+        compiler_params=pltpu.CompilerParams(vmem_limit_bytes=8 * 2**20),
+    )(pltpu.with_memory_space_constraint(raw, pltpu.HBM))
 
 
 def prepare_kernel(scal, raw, unit, factor):
@@ -320,7 +345,7 @@
     rows, width = image_embeds.shape
     scale = jnp.exp(log_scale[0])
     scal = jnp.stack([scale * (1.0 / math.log(2.0)), bias[0] * (1.0 / math.log(2.0)), scale])
-    (txt,) = normalize(text_embeds, "norm_text", False)
+    txt = normalize_hbm(text_embeds, "norm_text")
     txt_y, txt_c = move(txt, dy=1), move(txt, dc=1)
     own, a, b = normalize(image_embeds, "norm_image", True, after=[txt])
     prev_a, next_b = move(a, dz=1), move(b, dz=-1)
@@ -335,30 +360,33 @@
     (txt_y,) = hold("hold_text", [txt_y], [i_factor])
     far_t = [txt_y, move(txt_y, dc=1)]
     t_unit, t_factor = prepare(scal, text_embeds, "prep_text", [txt_y])
-    (own_y, own_yc), s_own = rows_step("own_y", scal, own, far_t, s_own, after=[t_factor])
+    (own_y, own_yc), s_own = rows_step("own_y", scal, own, far_t, s_own, after=[t_factor, i_factor])
+    kept = [i_factor, t_factor, s_own[1]]
     (last,) = merge("merge_last", prev_b, next_a, s_own[1:])
     (last_0, last_c, last_y, last_yc), (g_prev_b, g_next_a) = rows_step(
-        "last", scal, last, near_t + far_t, finish=2
+        "last", scal, last, near_t + far_t, finish=2, after=kept
     )
     near_b, near_a = move(g_prev_b, dz=-1), move(g_next_a, dz=1)
     (far,) = merge("merge_far", far_a, far_b, [g_prev_b])
-    (far_0, far_c, far_y, far_yc), (g_far_a, g_far_b) = rows_step("far", scal, far, near_t + far_t, finish=2)
+    (far_0, far_c, far_y, far_yc), (g_far_a, g_far_b) = rows_step(
+        "far", scal, far, near_t + far_t, finish=2, after=kept
+    )
     through_a, through_b = move(g_far_a, dz=-1), move(g_far_b, dz=1)
-    (first_y, first_yc), s_first = rows_step("first_y", scal, first, far_t, s_first, after=[g_far_a])
+    (first_y, first_yc), s_first = rows_step("first_y", scal, first, far_t, s_first, after=[g_far_a, *kept])
     images = [own, first, last, far]
-    (gt_yc,) = cols_step("cols_yc", [[own_yc], [first_yc], [last_yc], [far_yc]], images, (BF,))
+    (gt_yc,) = cols_step("cols_yc", [[own_yc], [first_yc], [last_yc], [far_yc]], images, (BF,), after=kept)
     through_y = move(gt_yc, dc=1)
-    (gt_y,) = cols_step("cols_y", [[own_y], [first_y], [last_y], [far_y]], images, (F32,), after=[gt_yc])
+    (gt_y,) = cols_step("cols_y", [[own_y], [first_y], [last_y], [far_y]], images, (F32,), after=[gt_yc, *kept])
     sum_y = add("add_y", gt_y, through_y)
     text_y = move(sum_y, dy=1)
     (gt_c,) = cols_step(
-        "cols_c", [[own_c], [first_c], [last_c], [far_c]], images, (BF,), after=[sum_y, near_a, near_b]
+        "cols_c", [[own_c], [first_c], [last_c], [far_c]], images, (BF,), after=[sum_y, near_a, near_b, *kept]
     )
     text_c = move(gt_c, dc=1)
     to_prev, to_next = sums("sums", s_first, [through_a, through_b], [gt_c])
     sum_a, sum_b = move(to_prev, dz=-1), move(to_next, dz=1)
     (gt_own,) = cols_step(
-        "cols_own", [[own_0], [first_0], [last_0], [far_0]], images, (F32,), after=[to_prev]
+        "cols_own", [[own_0], [first_0], [last_0], [far_0]], images, (F32,), after=[to_prev, *kept]
     )
     i_base, line = call(
         image_base_kernel,

time: 106 us -> 105 us (level)
  local copies, waits for them, and re-layouts: 3.34 us -> 1.08 us
  Pallas kernels: 51.4 us -> 52.5 us
    unnamed x18 -> x4, local copies, waits for them, and re-layouts: 3.34 us -> 1.08 us
    pallas_call x0 -> x1, Pallas kernels: none -> 1.68 us  [normalize_hbm(): pl.pallas_call(normalize_hbm_kernel, name=name, in_specs=[pl.BlockSpec(me...]
    pallas_call x23 -> x22, Pallas kernels: 47.3 us -> 46.7 us  [call(): pl.pallas_call(body, name=name, in_specs=specs, out_specs=[VMEM] * len(ou...]
where the time goes in v5:
time: 105 us; the launch traced here: 104 us
  Pallas kernels  52.5 us (50%)
  starting transfers between devices  28.4 us (27%)
  waiting for transfers between devices  19.5 us (19%)
  between operations  2.41 us (2%)
  local copies, waits for them, and re-layouts  1.08 us (1%)
    pallas_call x22, Pallas kernels, call(): pl.pallas_call(body, name=name, in_specs=specs, out_specs=[VMEM] * len(ou...  46.7 us
    ppermute x18, starting transfers between devices, move(): return lax.ppermute(value, 'loss', pairs)  28.4 us
    ppermute x18, waiting for transfers between devices, move(): return lax.ppermute(value, 'loss', pairs)  19.5 us
    pallas_call x2, Pallas kernels, final(): pl.pallas_call(kernel, name=name, in_specs=[VMEM] * len(inputs), out_spec...  4.13 us
  transfers between devices with their start and end apart: 18, of which 5 were waited for; matrix products, arithmetic and copies ran while one was open for 0% of the time, Pallas kernels for 47%

profile of v5, /device:TPU:0, one launch (start us, length us, event | category | flops | bytes accessed | tf_op | source)
XLA Modules:
  0.0 104.0 jit_solution(8582467394174728639)
XLA Ops:
  0.6 1.7 %norm_text.1.refs_1_.refs_2_ = bf16[512,1152]{1,0:T(8,128)(2,1)S(1)} custom-call(bf16[512,1152]{1,0:T(8,128)(2,1)} %refs_1_.3), custom_call_target="tpu_custom_call" | custom-call | flops 20000000000 | tf_op jit(solution)/shard_map/norm_text/pallas_call | solution.py:81
  2.3 0.1 collective-permute-start.3
  2.4 3.4 %collective-permute-start = (bf16[512,1152]{1,0:T(8,128)(2,1)S(1)}, bf16[512,1152]{1,0:T(8,128)(2,1)S(1)}, u32[]{:S(2)}, u32[]{:S(2)}) collective-permute-start(bf16[512,1152]{1,0:T(8,128)(2,1)S(1)} %norm_text.1.refs_1_.refs_2_), channel_id=1, source_target_pairs={{0,2},{1,3},{2,0},{3,1},{4,6},{5,7},{6,4},{7,5},{8,10},{9,11},{10,... | collective-permute-start | bytes 3538952 | tf_op jit(solution)/shard_map/ppermute | solution.py:343
  5.8 0.7 norm_image.1
  6.5 2.0 %collective-permute-start.1 = (bf16[256,1152]{1,0:T(8,128)(2,1)S(1)}, bf16[256,1152]{1,0:T(8,128)(2,1)S(1)}, u32[]{:S(2)}, u32[]{:S(2)}) collective-permute-start(bf16[256,1152]{1,0:T(8,128)(2,1)S(1)} %get-tuple-element.51.refs_0_), channel_id=1, source_target_pairs={{0,4},{1,5},{2,6},{3,7},{4,8},{5,9},{6,10},{7,11},{8,12},{9,13},{1... | collective-permute-start | bytes 1769480 | tf_op jit(solution)/shard_map/ppermute | solution.py:343
  8.4 2.2 %collective-permute-start.2 = (bf16[256,1152]{1,0:T(8,128)(2,1)S(1)}, bf16[256,1152]{1,0:T(8,128)(2,1)S(1)}, u32[]{:S(2)}, u32[]{:S(2)}) collective-permute-start(bf16[256,1152]{1,0:T(8,128)(2,1)S(1)} %get-tuple-element.52.refs_1_), channel_id=1, source_target_pairs={{0,12},{1,13},{2,14},{3,15},{4,0},{5,1},{6,2},{7,3},{8,4},{9,5},{1... | collective-permute-start | bytes 1769480 | tf_op jit(solution)/shard_map/ppermute | solution.py:343
  12.0 0.1 pad_maximum_fusion.refs_0_
  12.1 0.1 hold_last.1
  12.2 3.2 %collective-permute-start.6 = (bf16[256,1152]{1,0:T(8,128)(2,1)S(1)}, bf16[256,1152]{1,0:T(8,128)(2,1)S(1)}, u32[]{:S(2)}, u32[]{:S(2)}) collective-permute-start(bf16[256,1152]{1,0:T(8,128)(2,1)S(1)} %get-tuple-element.53.refs_4_), channel_id=1, source_target_pairs={{0,12},{1,13},{2,14},{3,15},{4,0},{5,1},{6,2},{7,3},{8,4},{9,5},{1... | collective-permute-start | bytes 1769480 | tf_op jit(solution)/shard_map/ppermute | solution.py:343
  15.5 4.0 %own_c.1 = (bf16[512,512]{1,0:T(8,128)(2,1)S(1)}, bf16[512,512]{1,0:T(8,128)(2,1)S(1)}, f32[512,1152]{1,0:T(8,128)S(1)}, f32[512,128]{1,0:T(8,128)S(1)}) custom-call(f32[3]{0:T(128)S(1)} %pad_maximum_fusion.refs_0_, bf16[512,1152]{1,0:T(8,128)(2,1)S(1)} %get-tuple-element.50.refs_1_.refs_4_, bf16[512,1152]{1,0:T(8,128)(2,1)S(1)} %norm_text.1.refs_1_.refs_2_, ...), custom_call_target="tpu_custom_call" | custom-call | flops 20000000000 | tf_op jit(solution)/shard_map/own_c/pallas_call | solution.py:30
  19.5 5.2 %collective-permute-done.1.refs_0_ = bf16[256,1152]{1,0:T(8,128)(2,1)S(1)} collective-permute-done((bf16[256,1152]{1,0:T(8,128)(2,1)S(1)}, bf16[256,1152]{1,0:T(8,128)(2,1)S(1)}, u32[]{:S(2)}, u32[]{:S(2)}) %collective-permute-start.1) | collective-permute-done | bytes 589856 | tf_op jit(solution)/shard_map/ppermute | solution.py:343
  24.7 0.2 merge_first.1
  24.9 2.0 %collective-permute-start.9 = (bf16[256,1152]{1,0:T(8,128)(2,1)S(1)}, bf16[256,1152]{1,0:T(8,128)(2,1)S(1)}, u32[]{:S(2)}, u32[]{:S(2)}) collective-permute-start(bf16[256,1152]{1,0:T(8,128)(2,1)S(1)} %get-tuple-element.68), channel_id=1, source_target_pairs={{0,4},{1,5},{2,6},{3,7},{4,8},{5,9},{6,10},{7,11},{8,12},{9,13},{1... | collective-permute-start | bytes 1769480 | tf_op jit(solution)/shard_map/ppermute | solution.py:343
  26.8 1.5 %collective-permute-start.10 = (bf16[256,1152]{1,0:T(8,128)(2,1)S(1)}, bf16[256,1152]{1,0:T(8,128)(2,1)S(1)}, u32[]{:S(2)}, u32[]{:S(2)}) collective-permute-start(bf16[256,1152]{1,0:T(8,128)(2,1)S(1)} %get-tuple-element.69), channel_id=1, source_target_pairs={{0,12},{1,13},{2,14},{3,15},{4,0},{5,1},{6,2},{7,3},{8,4},{9,5},{1... | collective-permute-start | bytes 1769480 | tf_op jit(solution)/shard_map/ppermute | solution.py:343
  28.4 3.8 %first_c.1 = (bf16[512,512]{1,0:T(8,128)(2,1)S(1)}, bf16[512,512]{1,0:T(8,128)(2,1)S(1)}, f32[512,1152]{1,0:T(8,128)S(1)}, f32[512,128]{1,0:T(8,128)S(1)}) custom-call(f32[3]{0:T(128)S(1)} %pad_maximum_fusion.refs_0_, bf16[512,1152]{1,0:T(8,128)(2,1)S(1)} %get-tuple-element.55.refs_1_.refs_5_, bf16[512,1152]{1,0:T(8,128)(2,1)S(1)} %norm_text.1.refs_1_.refs_2_, ...), custom_call_target="tpu_custom_call" | custom-call | flops 20000000000 | tf_op jit(solution)/shard_map/first_c/pallas_call | solution.py:30
  32.1 1.1 %prep_image.1 = (f32[512,1152]{1,0:T(8,128)S(1)}, f32[512,128]{1,0:T(8,128)S(1)}) custom-call(f32[3]{0:T(128)S(1)} %pad_maximum_fusion.refs_0_, bf16[512,1152]{1,0:T(8,128)(2,1)S(1)} %copy-done, f32[512,128]{1,0:T(8,128)S(1)} %get-tuple-element.56.refs_2_.refs_5_), custom_call_target="tpu_custom_call" | custom-call | flops 20000000000 | tf_op jit(solution)/shard_map/prep_image/pallas_call | solution.py:30
  33.3 0.1 hold_text.1.refs_2_.refs_4_
  33.4 0.1 collective-permute-start.4
  33.5 1.1 %copy-done.1 = bf16[512,1152]{1,0:T(8,128)(2,1)S(1)} copy-done((bf16[512,1152]{1,0:T(8,128)(2,1)S(1)}, bf16[512,1152]{1,0:T(8,128)(2,1)}, u32[]{:S(2)}) %copy-start.1) | copy-done | bytes 1179672
  34.6 1.1 %prep_text.1 = (f32[512,1152]{1,0:T(8,128)S(1)}, f32[512,128]{1,0:T(8,128)S(1)}) custom-call(f32[3]{0:T(128)S(1)} %pad_maximum_fusion.refs_0_, bf16[512,1152]{1,0:T(8,128)(2,1)S(1)} %copy-done.1, bf16[512,1152]{1,0:T(8,128)(2,1)S(1)} %hold_text.1.refs_2_.refs_4_), custom_call_target="tpu_custom_call" | custom-call | flops 20000000000 | tf_op jit(solution)/shard_map/prep_text/pallas_call | solution.py:30
  35.7 0.6 collective-permute-done.4.refs_3_.refs_5_
  36.3 4.3 %own_y.1 = (bf16[512,512]{1,0:T(8,128)(2,1)S(1)}, bf16[512,512]{1,0:T(8,128)(2,1)S(1)}, f32[512,1152]{1,0:T(8,128)S(1)}, f32[512,128]{1,0:T(8,128)S(1)}) custom-call(f32[3]{0:T(128)S(1)} %pad_maximum_fusion.refs_0_, bf16[512,1152]{1,0:T(8,128)(2,1)S(1)} %get-tuple-element.50.refs_1_.refs_4_, bf16[512,1152]{1,0:T(8,128)(2,1)S(1)} %hold_text.1.refs_2_.refs_4_, ...), custom_call_target="tpu_custom_call" | custom-call | flops 20000000000 | tf_op jit(solution)/shard_map/own_y/pallas_call | solution.py:30
  40.7 0.1 merge_last.1.refs_1_.refs_6_
  40.8 6.8 %last.1 = (bf16[512,512]{1,0:T(8,128)(2,1)S(1)}, bf16[512,512]{1,0:T(8,128)(2,1)S(1)}, bf16[512,512]{1,0:T(8,128)(2,1)S(1)}, bf16[512,512]{1,0:T(8,128)(2,1)S(1)...) custom-call(f32[3]{0:T(128)S(1)} %pad_maximum_fusion.refs_0_, ...), custom_call_target="tpu_custom_call" | custom-call | flops 20000000000 | tf_op jit(solution)/shard_map/last/pallas_call | solution.py:30
  47.6 1.3 %collective-permute-start.7 = (bf16[272,1152]{1,0:T(8,128)(2,1)S(1)}, bf16[272,1152]{1,0:T(8,128)(2,1)S(1)}, u32[]{:S(2)}, u32[]{:S(2)}) collective-permute-start(bf16[272,1152]{1,0:T(8,128)(2,1)S(1)} %get-tuple-element.63), channel_id=1, source_target_pairs={{0,4},{1,5},{2,6},{3,7},{4,8},{5,9},{6,10},{7,11},{8,12},{9,13},{1... | collective-permute-start | bytes 1880072 | tf_op jit(solution)/shard_map/ppermute | solution.py:343
  48.9 2.2 %collective-permute-start.8 = (bf16[272,1152]{1,0:T(8,128)(2,1)S(1)}, bf16[272,1152]{1,0:T(8,128)(2,1)S(1)}, u32[]{:S(2)}, u32[]{:S(2)}) collective-permute-start(bf16[272,1152]{1,0:T(8,128)(2,1)S(1)} %get-tuple-element.64.refs_2_), channel_id=1, source_target_pairs={{0,12},{1,13},{2,14},{3,15},{4,0},{5,1},{6,2},{7,3},{8,4},{9,5},{1... | collective-permute-start | bytes 1880072 | tf_op jit(solution)/shard_map/ppermute | solution.py:343
  51.1 0.1 merge_far.1.refs_1_.refs_7_
  51.2 6.8 %far.1 = (bf16[512,512]{1,0:T(8,128)(2,1)S(1)}, bf16[512,512]{1,0:T(8,128)(2,1)S(1)}, bf16[512,512]{1,0:T(8,128)(2,1)S(1)}, bf16[512,512]{1,0:T(8,128)(2,1)S(1)}...) custom-call(f32[3]{0:T(128)S(1)} %pad_maximum_fusion.refs_0_, ...), custom_call_target="tpu_custom_call" | custom-call | flops 20000000000 | tf_op jit(solution)/shard_map/far/pallas_call | solution.py:30
  58.1 3.2 %collective-permute-start.11 = (bf16[272,1152]{1,0:T(8,128)(2,1)S(1)}, bf16[272,1152]{1,0:T(8,128)(2,1)S(1)}, u32[]{:S(2)}, u32[]{:S(2)}) collective-permute-start(bf16[272,1152]{1,0:T(8,128)(2,1)S(1)} %get-tuple-element.72.refs_6_), channel_id=1, source_target_pairs={{0,12},{1,13},{2,14},{3,15},{4,0},{5,1},{6,2},{7,3},{8,4},{9,5},{1... | collective-permute-start | bytes 1880072 | tf_op jit(solution)/shard_map/ppermute | solution.py:343
  61.3 4.3 %first_y.1 = (bf16[512,512]{1,0:T(8,128)(2,1)S(1)}, bf16[512,512]{1,0:T(8,128)(2,1)S(1)}, f32[512,1152]{1,0:T(8,128)S(1)}, f32[512,128]{1,0:T(8,128)S(1)}) custom-call(f32[3]{0:T(128)S(1)} %pad_maximum_fusion.refs_0_, bf16[512,1152]{1,0:T(8,128)(2,1)S(1)} %get-tuple-element.55.refs_1_.refs_5_, bf16[512,1152]{1,0:T(8,128)(2,1)S(1)} %hold_text.1.refs_2_.refs_4_, ...), custom_call_target="tpu_custom_call" | custom-call | flops 20000000000 | tf_op jit(solution)/shard_map/first_y/pallas_call | solution.py:30
  65.7 3.0 %cols_yc.1.refs_8_ = bf16[512,1152]{1,0:T(8,128)(2,1)S(1)} custom-call(bf16[512,512]{1,0:T(8,128)(2,1)S(1)} %get-tuple-element.84.refs_0_, bf16[512,512]{1,0:T(8,128)(2,1)S(1)} %get-tuple-element.85.refs_1_, bf16[512,512]{1,0:T(8,128)(2,1)S(1)} %get-tuple-element.86.refs_2_, bf16[512,512]{1,0:T(8,128)(2,1)S(1)} %get-tuple-element.87.refs_3_, ...), custom_call_target="tpu_custom_call" | custom-call | flops 20000000000 | tf_op jit(solution)/shard_map/cols_yc/pallas_call | solution.py:30
  68.6 0.1 collective-permute-start.13
  68.7 3.0 %cols_y.1.refs_0_ = f32[512,1152]{1,0:T(8,128)S(1)} custom-call(bf16[512,512]{1,0:T(8,128)(2,1)S(1)} %get-tuple-element.80.refs_0_, bf16[512,512]{1,0:T(8,128)(2,1)S(1)} %get-tuple-element.81.refs_1_, bf16[512,512]{1,0:T(8,128)(2,1)S(1)} %get-tuple-element.82.refs_2_, bf16[512,512]{1,0:T(8,128)(2,1)S(1)} %get-tuple-element.83.refs_3_, ...), custom_call_target="tpu_custom_call" | custom-call | flops 20000000000 | tf_op jit(solution)/shard_map/cols_y/pallas_call | solution.py:30
  71.7 0.2 add_y.1.refs_8_
  71.9 3.5 %collective-permute-start.17 = (bf16[512,1152]{1,0:T(8,128)(2,1)S(1)}, bf16[512,1152]{1,0:T(8,128)(2,1)S(1)}, u32[]{:S(2)}, u32[]{:S(2)}) collective-permute-start(bf16[512,1152]{1,0:T(8,128)(2,1)S(1)} %add_y.1.refs_8_), channel_id=1, source_target_pairs={{0,2},{1,3},{2,0},{3,1},{4,6},{5,7},{6,4},{7,5},{8,10},{9,11},{10,... | collective-permute-start | bytes 3538952 | tf_op jit(solution)/shard_map/ppermute | solution.py:343
  75.4 3.0 %cols_c.1.refs_4_ = bf16[512,1152]{1,0:T(8,128)(2,1)S(1)} custom-call(bf16[512,512]{1,0:T(8,128)(2,1)S(1)} %get-tuple-element.76.refs_0_, bf16[512,512]{1,0:T(8,128)(2,1)S(1)} %get-tuple-element.77.refs_1_, bf16[512,512]{1,0:T(8,128)(2,1)S(1)} %get-tuple-element.78.refs_2_, bf16[512,512]{1,0:T(8,128)(2,1)S(1)} %get-tuple-element.79.refs_3_, ...), custom_call_target="tpu_custom_call" | custom-call | flops 20000000000 | tf_op jit(solution)/shard_map/cols_c/pallas_call | solution.py:30
  78.3 0.3 collective-permute-start.16
  78.6 0.2 collective-permute-done.12.refs_3_
  78.8 0.5 sums.1
  79.4 1.3 %collective-permute-start.15 = (bf16[272,1152]{1,0:T(8,128)(2,1)S(1)}, bf16[272,1152]{1,0:T(8,128)(2,1)S(1)}, u32[]{:S(2)}, u32[]{:S(2)}) collective-permute-start(bf16[272,1152]{1,0:T(8,128)(2,1)S(1)} %get-tuple-element.92), channel_id=1, source_target_pairs={{0,4},{1,5},{2,6},{3,7},{4,8},{5,9},{6,10},{7,11},{8,12},{9,13},{1... | collective-permute-start | bytes 1880072 | tf_op jit(solution)/shard_map/ppermute | solution.py:343
  80.7 2.0 %collective-permute-start.14 = (bf16[272,1152]{1,0:T(8,128)(2,1)S(1)}, bf16[272,1152]{1,0:T(8,128)(2,1)S(1)}, u32[]{:S(2)}, u32[]{:S(2)}) collective-permute-start(bf16[272,1152]{1,0:T(8,128)(2,1)S(1)} %get-tuple-element.88.refs_8_), channel_id=1, source_target_pairs={{0,12},{1,13},{2,14},{3,15},{4,0},{5,1},{6,2},{7,3},{8,4},{9,5},{1... | collective-permute-start | bytes 1880072 | tf_op jit(solution)/shard_map/ppermute | solution.py:343
  82.7 3.0 %cols_own.1.refs_4_.refs_0_ = f32[512,1152]{1,0:T(8,128)S(1)} custom-call(bf16[512,512]{1,0:T(8,128)(2,1)S(1)} %get-tuple-element.65.refs_0_, bf16[512,512]{1,0:T(8,128)(2,1)S(1)} %get-tuple-element.66.refs_1_, bf16[512,512]{1,0:T(8,128)(2,1)S(1)} %get-tuple-element.67.refs_2_, bf16[512,512]{1,0:T(8,128)(2,1)S(1)} %get-tuple-element.70.refs_3_, ...), custom_call_target="tpu_custom_call" | custom-call | flops 20000000000 | tf_op jit(solution)/shard_map/cols_own/pallas_call | solution.py:30
  85.6 0.3 image_base.1
  86.0 0.2 text_base.1.ready.base
  86.2 10.6 %collective-permute-done.15.sum_b = bf16[272,1152]{1,0:T(8,128)(2,1)S(1)} collective-permute-done((bf16[272,1152]{1,0:T(8,128)(2,1)S(1)}, bf16[272,1152]{1,0:T(8,128)(2,1)S(1)}, u32[]{:S(2)}, u32[]{:S(2)}) %collective-permute-start.15) | collective-permute-done | bytes 626720 | tf_op jit(solution)/shard_map/ppermute | solution.py:343
  96.8 2.4 %image.1 = (bf16[512,1152]{1,0:T(8,128)(2,1)}, f32[1,512]{1,0:T(1,128)}, f32[8,128]{1,0:T(8,128)S(1)}) custom-call(f32[512,1152]{1,0:T(8,128)S(1)} %get-tuple-element.89.base, f32[8,512]{1,0:T(8,128)S(1)} %get-tuple-element.90.refs_2_.line, f32[512,1152]{1,0:T(8,128)S(1)} %get-tuple-element.91.unit, ...), custom_call_target="tpu_custom_call" | custom-call | flops 1000 | tf_op jit(solution)/shard_map/image/pallas_call | solution.py:323
  99.2 2.9 %collective-permute-done.17.late = bf16[512,1152]{1,0:T(8,128)(2,1)S(1)} collective-permute-done((bf16[512,1152]{1,0:T(8,128)(2,1)S(1)}, bf16[512,1152]{1,0:T(8,128)(2,1)S(1)}, u32[]{:S(2)}, u32[]{:S(2)}) %collective-permute-start.17) | collective-permute-done | bytes 1179680 | tf_op jit(solution)/shard_map/ppermute | solution.py:343
  102.1 1.8 %text.1 = bf16[512,1152]{1,0:T(8,128)(2,1)} custom-call(f32[512,1152]{1,0:T(8,128)S(1)} %text_base.1.ready.base, f32[512,1152]{1,0:T(8,128)S(1)} %get-tuple-element.95.unit, f32[512,128]{1,0:T(8,128)S(1)} %get-tuple-element.59.refs_6_.refs_7_.refs_8_.refs_9_.refs_10_.refs_12_.factor, bf16[512,1152]{1,0:T(8,128)(2,1)S(1)} %collective-permute-done.17.late, ...), custom_call_target="tpu_custom_call" | custom-call | flops 1000 | tf_op jit(solution)/shard_map/text/pallas_call | solution.py:323
  (18 shorter events, 0.2 us)
Async XLA Ops:
  0.6 5.2 %copy-start = (bf16[512,1152]{1,0:T(8,128)(2,1)S(1)}, bf16[512,1152]{1,0:T(8,128)(2,1)}, u32[]{:S(2)}) copy-start(bf16[512,1152]{1,0:T(8,128)(2,1)} %refs_1_.2) | copy-start | bytes 3538948
  2.3 9.7 %collective-permute-start.3 = (bf16[512,1152]{1,0:T(8,128)(2,1)S(1)}, bf16[512,1152]{1,0:T(8,128)(2,1)S(1)}, u32[]{:S(2)}, u32[]{:S(2)}) collective-permute-start(bf16[512,1152]{1,0:T(8,128)(2,1)S(1)} %norm_text.1.refs_1_.refs_2_), channel_id=1, source_target_pairs={{0,1},{1,0},{2,3},{3,2},{4,5},{5,4},{6,7},{7,6},{8,9},{9,8},{10,11... | collective-permute-start | bytes 3538952 | tf_op jit(solution)/shard_map/ppermute | solution.py:343
  2.4 30.9 %collective-permute-start = (bf16[512,1152]{1,0:T(8,128)(2,1)S(1)}, bf16[512,1152]{1,0:T(8,128)(2,1)S(1)}, u32[]{:S(2)}, u32[]{:S(2)}) collective-permute-start(bf16[512,1152]{1,0:T(8,128)(2,1)S(1)} %norm_text.1.refs_1_.refs_2_), channel_id=1, source_target_pairs={{0,2},{1,3},{2,0},{3,1},{4,6},{5,7},{6,4},{7,5},{8,10},{9,11},{10,... | collective-permute-start | bytes 3538952 | tf_op jit(solution)/shard_map/ppermute | solution.py:343
  6.5 18.2 %collective-permute-start.1 = (bf16[256,1152]{1,0:T(8,128)(2,1)S(1)}, bf16[256,1152]{1,0:T(8,128)(2,1)S(1)}, u32[]{:S(2)}, u32[]{:S(2)}) collective-permute-start(bf16[256,1152]{1,0:T(8,128)(2,1)S(1)} %get-tuple-element.51.refs_0_), channel_id=1, source_target_pairs={{0,4},{1,5},{2,6},{3,7},{4,8},{5,9},{6,10},{7,11},{8,12},{9,13},{1... | collective-permute-start | bytes 1769480 | tf_op jit(solution)/shard_map/ppermute | solution.py:343
  8.4 16.2 %collective-permute-start.2 = (bf16[256,1152]{1,0:T(8,128)(2,1)S(1)}, bf16[256,1152]{1,0:T(8,128)(2,1)S(1)}, u32[]{:S(2)}, u32[]{:S(2)}) collective-permute-start(bf16[256,1152]{1,0:T(8,128)(2,1)S(1)} %get-tuple-element.52.refs_1_), channel_id=1, source_target_pairs={{0,12},{1,13},{2,14},{3,15},{4,0},{5,1},{6,2},{7,3},{8,4},{9,5},{1... | collective-permute-start | bytes 1769480 | tf_op jit(solution)/shard_map/ppermute | solution.py:343
  12.2 28.5 %collective-permute-start.5 = (bf16[256,1152]{1,0:T(8,128)(2,1)S(1)}, bf16[256,1152]{1,0:T(8,128)(2,1)S(1)}, u32[]{:S(2)}, u32[]{:S(2)}) collective-permute-start(bf16[256,1152]{1,0:T(8,128)(2,1)S(1)} %get-tuple-element.62), channel_id=1, source_target_pairs={{0,4},{1,5},{2,6},{3,7},{4,8},{5,9},{6,10},{7,11},{8,12},{9,13},{1... | collective-permute-start | bytes 1769480 | tf_op jit(solution)/shard_map/ppermute | solution.py:343
  12.2 28.4 %collective-permute-start.6 = (bf16[256,1152]{1,0:T(8,128)(2,1)S(1)}, bf16[256,1152]{1,0:T(8,128)(2,1)S(1)}, u32[]{:S(2)}, u32[]{:S(2)}) collective-permute-start(bf16[256,1152]{1,0:T(8,128)(2,1)S(1)} %get-tuple-element.53.refs_4_), channel_id=1, source_target_pairs={{0,12},{1,13},{2,14},{3,15},{4,0},{5,1},{6,2},{7,3},{8,4},{9,5},{1... | collective-permute-start | bytes 1769480 | tf_op jit(solution)/shard_map/ppermute | solution.py:343
  24.9 26.2 %collective-permute-start.9 = (bf16[256,1152]{1,0:T(8,128)(2,1)S(1)}, bf16[256,1152]{1,0:T(8,128)(2,1)S(1)}, u32[]{:S(2)}, u32[]{:S(2)}) collective-permute-start(bf16[256,1152]{1,0:T(8,128)(2,1)S(1)} %get-tuple-element.68), channel_id=1, source_target_pairs={{0,4},{1,5},{2,6},{3,7},{4,8},{5,9},{6,10},{7,11},{8,12},{9,13},{1... | collective-permute-start | bytes 1769480 | tf_op jit(solution)/shard_map/ppermute | solution.py:343
  26.8 24.3 %collective-permute-start.10 = (bf16[256,1152]{1,0:T(8,128)(2,1)S(1)}, bf16[256,1152]{1,0:T(8,128)(2,1)S(1)}, u32[]{:S(2)}, u32[]{:S(2)}) collective-permute-start(bf16[256,1152]{1,0:T(8,128)(2,1)S(1)} %get-tuple-element.69), channel_id=1, source_target_pairs={{0,12},{1,13},{2,14},{3,15},{4,0},{5,1},{6,2},{7,3},{8,4},{9,5},{1... | collective-permute-start | bytes 1769480 | tf_op jit(solution)/shard_map/ppermute | solution.py:343
  33.3 1.3 %copy-start.1 = (bf16[512,1152]{1,0:T(8,128)(2,1)S(1)}, bf16[512,1152]{1,0:T(8,128)(2,1)}, u32[]{:S(2)}) copy-start(bf16[512,1152]{1,0:T(8,128)(2,1)} %refs_1_.3) | copy-start | bytes 3538948
  33.4 2.9 %collective-permute-start.4 = (bf16[512,1152]{1,0:T(8,128)(2,1)S(1)}, bf16[512,1152]{1,0:T(8,128)(2,1)S(1)}, u32[]{:S(2)}, u32[]{:S(2)}) collective-permute-start(bf16[512,1152]{1,0:T(8,128)(2,1)S(1)} %hold_text.1.refs_2_.refs_4_), channel_id=1, source_target_pairs={{0,1},{1,0},{2,3},{3,2},{4,5},{5,4},{6,7},{7,6},{8,9},{9,8},{10,11... | collective-permute-start | bytes 3538952 | tf_op jit(solution)/shard_map/ppermute | solution.py:343
  47.6 27.8 %collective-permute-start.7 = (bf16[272,1152]{1,0:T(8,128)(2,1)S(1)}, bf16[272,1152]{1,0:T(8,128)(2,1)S(1)}, u32[]{:S(2)}, u32[]{:S(2)}) collective-permute-start(bf16[272,1152]{1,0:T(8,128)(2,1)S(1)} %get-tuple-element.63), channel_id=1, source_target_pairs={{0,4},{1,5},{2,6},{3,7},{4,8},{5,9},{6,10},{7,11},{8,12},{9,13},{1... | collective-permute-start | bytes 1880072 | tf_op jit(solution)/shard_map/ppermute | solution.py:343
  48.9 26.5 %collective-permute-start.8 = (bf16[272,1152]{1,0:T(8,128)(2,1)S(1)}, bf16[272,1152]{1,0:T(8,128)(2,1)S(1)}, u32[]{:S(2)}, u32[]{:S(2)}) collective-permute-start(bf16[272,1152]{1,0:T(8,128)(2,1)S(1)} %get-tuple-element.64.refs_2_), channel_id=1, source_target_pairs={{0,12},{1,13},{2,14},{3,15},{4,0},{5,1},{6,2},{7,3},{8,4},{9,5},{1... | collective-permute-start | bytes 1880072 | tf_op jit(solution)/shard_map/ppermute | solution.py:343
  58.0 20.8 %collective-permute-start.12 = (bf16[272,1152]{1,0:T(8,128)(2,1)S(1)}, bf16[272,1152]{1,0:T(8,128)(2,1)S(1)}, u32[]{:S(2)}, u32[]{:S(2)}) collective-permute-start(bf16[272,1152]{1,0:T(8,128)(2,1)S(1)} %get-tuple-element.75), channel_id=1, source_target_pairs={{0,4},{1,5},{2,6},{3,7},{4,8},{5,9},{6,10},{7,11},{8,12},{9,13},{1... | collective-permute-start | bytes 1880072 | tf_op jit(solution)/shard_map/ppermute | solution.py:343
  58.1 20.7 %collective-permute-start.11 = (bf16[272,1152]{1,0:T(8,128)(2,1)S(1)}, bf16[272,1152]{1,0:T(8,128)(2,1)S(1)}, u32[]{:S(2)}, u32[]{:S(2)}) collective-permute-start(bf16[272,1152]{1,0:T(8,128)(2,1)S(1)} %get-tuple-element.72.refs_6_), channel_id=1, source_target_pairs={{0,12},{1,13},{2,14},{3,15},{4,0},{5,1},{6,2},{7,3},{8,4},{9,5},{1... | collective-permute-start | bytes 1880072 | tf_op jit(solution)/shard_map/ppermute | solution.py:343
  68.6 3.1 %collective-permute-start.13 = (bf16[512,1152]{1,0:T(8,128)(2,1)S(1)}, bf16[512,1152]{1,0:T(8,128)(2,1)S(1)}, u32[]{:S(2)}, u32[]{:S(2)}) collective-permute-start(bf16[512,1152]{1,0:T(8,128)(2,1)S(1)} %cols_yc.1.refs_8_), channel_id=1, source_target_pairs={{0,1},{1,0},{2,3},{3,2},{4,5},{5,4},{6,7},{7,6},{8,9},{9,8},{10,11... | collective-permute-start | bytes 3538952 | tf_op jit(solution)/shard_map/ppermute | solution.py:343
  71.9 30.2 %collective-permute-start.17 = (bf16[512,1152]{1,0:T(8,128)(2,1)S(1)}, bf16[512,1152]{1,0:T(8,128)(2,1)S(1)}, u32[]{:S(2)}, u32[]{:S(2)}) collective-permute-start(bf16[512,1152]{1,0:T(8,128)(2,1)S(1)} %add_y.1.refs_8_), channel_id=1, source_target_pairs={{0,2},{1,3},{2,0},{3,1},{4,6},{5,7},{6,4},{7,5},{8,10},{9,11},{10,... | collective-permute-start | bytes 3538952 | tf_op jit(solution)/shard_map/ppermute | solution.py:343
  78.3 7.6 %collective-permute-start.16 = (bf16[512,1152]{1,0:T(8,128)(2,1)S(1)}, bf16[512,1152]{1,0:T(8,128)(2,1)S(1)}, u32[]{:S(2)}, u32[]{:S(2)}) collective-permute-start(bf16[512,1152]{1,0:T(8,128)(2,1)S(1)} %cols_c.1.refs_4_), channel_id=1, source_target_pairs={{0,1},{1,0},{2,3},{3,2},{4,5},{5,4},{6,7},{7,6},{8,9},{9,8},{10,11... | collective-permute-start | bytes 3538952 | tf_op jit(solution)/shard_map/ppermute | solution.py:343
  79.4 17.4 %collective-permute-start.15 = (bf16[272,1152]{1,0:T(8,128)(2,1)S(1)}, bf16[272,1152]{1,0:T(8,128)(2,1)S(1)}, u32[]{:S(2)}, u32[]{:S(2)}) collective-permute-start(bf16[272,1152]{1,0:T(8,128)(2,1)S(1)} %get-tuple-element.92), channel_id=1, source_target_pairs={{0,4},{1,5},{2,6},{3,7},{4,8},{5,9},{6,10},{7,11},{8,12},{9,13},{1... | collective-permute-start | bytes 1880072 | tf_op jit(solution)/shard_map/ppermute | solution.py:343
  80.7 16.1 %collective-permute-start.14 = (bf16[272,1152]{1,0:T(8,128)(2,1)S(1)}, bf16[272,1152]{1,0:T(8,128)(2,1)S(1)}, u32[]{:S(2)}, u32[]{:S(2)}) collective-permute-start(bf16[272,1152]{1,0:T(8,128)(2,1)S(1)} %get-tuple-element.88.refs_8_), channel_id=1, source_target_pairs={{0,12},{1,13},{2,14},{3,15},{4,0},{5,1},{6,2},{7,3},{8,4},{9,5},{1... | collective-permute-start | bytes 1880072 | tf_op jit(solution)/shard_map/ppermute | solution.py:343

commit v6 on v5

--- a/solution.py
+++ b/solution.py
@@ -359,9 +359,9 @@
     i_unit, i_factor = prepare(scal, image_embeds, "prep_image", s_first[1:])
     (txt_y,) = hold("hold_text", [txt_y], [i_factor])
     far_t = [txt_y, move(txt_y, dc=1)]
-    t_unit, t_factor = prepare(scal, text_embeds, "prep_text", [txt_y])
-    (own_y, own_yc), s_own = rows_step("own_y", scal, own, far_t, s_own, after=[t_factor, i_factor])
-    kept = [i_factor, t_factor, s_own[1]]
+    (own_y,), s_own = rows_step("own_y", scal, own, far_t[:1], s_own, after=[i_factor])
+    (own_yc,), s_own = rows_step("own_yc", scal, own, far_t[1:], s_own)
+    kept = [i_factor, s_own[1]]
     (last,) = merge("merge_last", prev_b, next_a, s_own[1:])
     (last_0, last_c, last_y, last_yc), (g_prev_b, g_next_a) = rows_step(
         "last", scal, last, near_t + far_t, finish=2, after=kept
@@ -399,10 +399,11 @@
     (t_base,) = call(
         text_base_kernel, "text_base", [gt_own, text_c], [pltpu.VMEM((rows, width), F32)], [line], cost=1000
     )
+    t_unit, t_factor = prepare(scal, text_embeds, "prep_text", [t_base])
     grad_image, loss, done = final(
         functools.partial(image_kernel, total),
         "image",
-        [i_base, line, i_unit, i_factor, sum_a, sum_b, t_base],
+        [i_base, line, i_unit, i_factor, sum_a, sum_b, t_factor],
         (rows, width),
         [jax.ShapeDtypeStruct((1, rows), F32), pltpu.VMEM((8, 128), F32)],
     )

time: 105 us -> 103 us (0.981)
  waiting for transfers between devices: 19.5 us -> 17.1 us
    ppermute x18, waiting for transfers between devices: 19.5 us -> 17.1 us  [move(): return lax.ppermute(value, 'loss', pairs)]
    pallas_call x22 -> x23, Pallas kernels: 46.7 us -> 47.7 us  [call(): pl.pallas_call(body, name=name, in_specs=specs, out_specs=[VMEM] * len(ou...]
  transfers between devices with their start and end apart: 18 -> 18, of which waited for: 5 -> 6; matrix products, arithmetic and copies ran while one was open for 0% -> 0% of each run, Pallas kernels for 47% -> 49%
where the time goes in v6:
time: 103 us; the launch traced here: 102 us
  Pallas kernels  53.4 us (52%)
  starting transfers between devices  28.4 us (28%)
  waiting for transfers between devices  17.1 us (17%)
  between operations  2.41 us (2%)
  local copies, waits for them, and re-layouts  1.07 us (1%)
    pallas_call x23, Pallas kernels, call(): pl.pallas_call(body, name=name, in_specs=specs, out_specs=[VMEM] * len(ou...  47.7 us
    ppermute x18, starting transfers between devices, move(): return lax.ppermute(value, 'loss', pairs)  28.4 us
    ppermute x18, waiting for transfers between devices, move(): return lax.ppermute(value, 'loss', pairs)  17.1 us
    pallas_call x2, Pallas kernels, final(): pl.pallas_call(kernel, name=name, in_specs=[VMEM] * len(inputs), out_spec...  4 us
  transfers between devices with their start and end apart: 18, of which 6 were waited for; matrix products, arithmetic and copies ran while one was open for 0% of the time, Pallas kernels for 49%

profile of v6, /device:TPU:0, one launch (start us, length us, event | category | flops | bytes accessed | tf_op | source)
XLA Modules:
  0.0 102.5 jit_solution(11357511163713266351)
XLA Ops:
  0.6 1.7 %norm_text.1.refs_1_.refs_2_ = bf16[512,1152]{1,0:T(8,128)(2,1)S(1)} custom-call(bf16[512,1152]{1,0:T(8,128)(2,1)} %refs_1_.3), custom_call_target="tpu_custom_call" | custom-call | flops 20000000000 | tf_op jit(solution)/shard_map/norm_text/pallas_call | solution.py:81
  2.3 0.1 collective-permute-start.3
  2.4 3.4 %collective-permute-start = (bf16[512,1152]{1,0:T(8,128)(2,1)S(1)}, bf16[512,1152]{1,0:T(8,128)(2,1)S(1)}, u32[]{:S(2)}, u32[]{:S(2)}) collective-permute-start(bf16[512,1152]{1,0:T(8,128)(2,1)S(1)} %norm_text.1.refs_1_.refs_2_), channel_id=1, source_target_pairs={{0,2},{1,3},{2,0},{3,1},{4,6},{5,7},{6,4},{7,5},{8,10},{9,11},{10,... | collective-permute-start | bytes 3538952 | tf_op jit(solution)/shard_map/ppermute | solution.py:343
  5.8 0.7 norm_image.1
  6.5 2.0 %collective-permute-start.1 = (bf16[256,1152]{1,0:T(8,128)(2,1)S(1)}, bf16[256,1152]{1,0:T(8,128)(2,1)S(1)}, u32[]{:S(2)}, u32[]{:S(2)}) collective-permute-start(bf16[256,1152]{1,0:T(8,128)(2,1)S(1)} %get-tuple-element.53.refs_0_), channel_id=1, source_target_pairs={{0,4},{1,5},{2,6},{3,7},{4,8},{5,9},{6,10},{7,11},{8,12},{9,13},{1... | collective-permute-start | bytes 1769480 | tf_op jit(solution)/shard_map/ppermute | solution.py:343
  8.4 2.2 %collective-permute-start.2 = (bf16[256,1152]{1,0:T(8,128)(2,1)S(1)}, bf16[256,1152]{1,0:T(8,128)(2,1)S(1)}, u32[]{:S(2)}, u32[]{:S(2)}) collective-permute-start(bf16[256,1152]{1,0:T(8,128)(2,1)S(1)} %get-tuple-element.54.refs_1_), channel_id=1, source_target_pairs={{0,12},{1,13},{2,14},{3,15},{4,0},{5,1},{6,2},{7,3},{8,4},{9,5},{1... | collective-permute-start | bytes 1769480 | tf_op jit(solution)/shard_map/ppermute | solution.py:343
  12.1 0.1 hold_last.1
  12.2 3.2 %collective-permute-start.6 = (bf16[256,1152]{1,0:T(8,128)(2,1)S(1)}, bf16[256,1152]{1,0:T(8,128)(2,1)S(1)}, u32[]{:S(2)}, u32[]{:S(2)}) collective-permute-start(bf16[256,1152]{1,0:T(8,128)(2,1)S(1)} %get-tuple-element.55.refs_4_), channel_id=1, source_target_pairs={{0,12},{1,13},{2,14},{3,15},{4,0},{5,1},{6,2},{7,3},{8,4},{9,5},{1... | collective-permute-start | bytes 1769480 | tf_op jit(solution)/shard_map/ppermute | solution.py:343
  15.5 4.0 %own_c.1 = (bf16[512,512]{1,0:T(8,128)(2,1)S(1)}, bf16[512,512]{1,0:T(8,128)(2,1)S(1)}, f32[512,1152]{1,0:T(8,128)S(1)}, f32[512,128]{1,0:T(8,128)S(1)}) custom-call(f32[3]{0:T(128)S(1)} %pad_maximum_fusion.refs_0_, bf16[512,1152]{1,0:T(8,128)(2,1)S(1)} %get-tuple-element.52.refs_1_.refs_4_, bf16[512,1152]{1,0:T(8,128)(2,1)S(1)} %norm_text.1.refs_1_.refs_2_, ...), custom_call_target="tpu_custom_call" | custom-call | flops 20000000000 | tf_op jit(solution)/shard_map/own_c/pallas_call | solution.py:30
  19.5 5.2 %collective-permute-done.1.refs_0_ = bf16[256,1152]{1,0:T(8,128)(2,1)S(1)} collective-permute-done((bf16[256,1152]{1,0:T(8,128)(2,1)S(1)}, bf16[256,1152]{1,0:T(8,128)(2,1)S(1)}, u32[]{:S(2)}, u32[]{:S(2)}) %collective-permute-start.1) | collective-permute-done | bytes 589856 | tf_op jit(solution)/shard_map/ppermute | solution.py:343
  24.7 0.2 merge_first.1
  24.9 2.0 %collective-permute-start.9 = (bf16[256,1152]{1,0:T(8,128)(2,1)S(1)}, bf16[256,1152]{1,0:T(8,128)(2,1)S(1)}, u32[]{:S(2)}, u32[]{:S(2)}) collective-permute-start(bf16[256,1152]{1,0:T(8,128)(2,1)S(1)} %get-tuple-element.71), channel_id=1, source_target_pairs={{0,4},{1,5},{2,6},{3,7},{4,8},{5,9},{6,10},{7,11},{8,12},{9,13},{1... | collective-permute-start | bytes 1769480 | tf_op jit(solution)/shard_map/ppermute | solution.py:343
  26.8 1.5 %collective-permute-start.10 = (bf16[256,1152]{1,0:T(8,128)(2,1)S(1)}, bf16[256,1152]{1,0:T(8,128)(2,1)S(1)}, u32[]{:S(2)}, u32[]{:S(2)}) collective-permute-start(bf16[256,1152]{1,0:T(8,128)(2,1)S(1)} %get-tuple-element.72), channel_id=1, source_target_pairs={{0,12},{1,13},{2,14},{3,15},{4,0},{5,1},{6,2},{7,3},{8,4},{9,5},{1... | collective-permute-start | bytes 1769480 | tf_op jit(solution)/shard_map/ppermute | solution.py:343
  28.4 3.8 %first_c.1 = (bf16[512,512]{1,0:T(8,128)(2,1)S(1)}, bf16[512,512]{1,0:T(8,128)(2,1)S(1)}, f32[512,1152]{1,0:T(8,128)S(1)}, f32[512,128]{1,0:T(8,128)S(1)}) custom-call(f32[3]{0:T(128)S(1)} %pad_maximum_fusion.refs_0_, bf16[512,1152]{1,0:T(8,128)(2,1)S(1)} %get-tuple-element.57.refs_1_.refs_5_, bf16[512,1152]{1,0:T(8,128)(2,1)S(1)} %norm_text.1.refs_1_.refs_2_, ...), custom_call_target="tpu_custom_call" | custom-call | flops 20000000000 | tf_op jit(solution)/shard_map/first_c/pallas_call | solution.py:30
  32.1 1.1 %prep_image.1 = (f32[512,1152]{1,0:T(8,128)S(1)}, f32[512,128]{1,0:T(8,128)S(1)}) custom-call(f32[3]{0:T(128)S(1)} %pad_maximum_fusion.refs_0_, bf16[512,1152]{1,0:T(8,128)(2,1)S(1)} %copy-done, f32[512,128]{1,0:T(8,128)S(1)} %get-tuple-element.58.refs_2_.refs_5_), custom_call_target="tpu_custom_call" | custom-call | flops 20000000000 | tf_op jit(solution)/shard_map/prep_image/pallas_call | solution.py:30
  33.3 0.1 hold_text.1.refs_2_.refs_4_
  33.4 0.1 collective-permute-start.4
  33.5 2.6 %own_y.1 = (bf16[512,512]{1,0:T(8,128)(2,1)S(1)}, f32[512,1152]{1,0:T(8,128)S(1)}, f32[512,128]{1,0:T(8,128)S(1)}) custom-call(f32[3]{0:T(128)S(1)} %pad_maximum_fusion.refs_0_, bf16[512,1152]{1,0:T(8,128)(2,1)S(1)} %get-tuple-element.52.refs_1_.refs_4_, bf16[512,1152]{1,0:T(8,128)(2,1)S(1)} %hold_text.1.refs_2_.refs_4_, ...), custom_call_target="tpu_custom_call" | custom-call | flops 20000000000 | tf_op jit(solution)/shard_map/own_y/pallas_call | solution.py:30
  36.1 0.2 collective-permute-done.4.refs_2_.refs_5_.refs_3_
  36.3 2.6 %own_yc.1 = (bf16[512,512]{1,0:T(8,128)(2,1)S(1)}, f32[512,1152]{1,0:T(8,128)S(1)}, f32[512,128]{1,0:T(8,128)S(1)}) custom-call(f32[3]{0:T(128)S(1)} %pad_maximum_fusion.refs_0_, bf16[512,1152]{1,0:T(8,128)(2,1)S(1)} %get-tuple-element.52.refs_1_.refs_4_, bf16[512,1152]{1,0:T(8,128)(2,1)S(1)} %collective-permute-done.4.refs_2_.refs_5_.refs_3_, ...), custom_call_target="tpu_custom_call" | custom-call | flops 20000000000 | tf_op jit(solution)/shard_map/own_yc/pallas_call | solution.py:30
  38.9 0.1 merge_last.1.refs_1_.refs_6_
  39.0 6.8 %last.1 = (bf16[512,512]{1,0:T(8,128)(2,1)S(1)}, bf16[512,512]{1,0:T(8,128)(2,1)S(1)}, bf16[512,512]{1,0:T(8,128)(2,1)S(1)}, bf16[512,512]{1,0:T(8,128)(2,1)S(1)...) custom-call(f32[3]{0:T(128)S(1)} %pad_maximum_fusion.refs_0_, ...), custom_call_target="tpu_custom_call" | custom-call | flops 20000000000 | tf_op jit(solution)/shard_map/last/pallas_call | solution.py:30
  45.8 1.1 %collective-permute-start.7 = (bf16[272,1152]{1,0:T(8,128)(2,1)S(1)}, bf16[272,1152]{1,0:T(8,128)(2,1)S(1)}, u32[]{:S(2)}, u32[]{:S(2)}) collective-permute-start(bf16[272,1152]{1,0:T(8,128)(2,1)S(1)} %get-tuple-element.66), channel_id=1, source_target_pairs={{0,4},{1,5},{2,6},{3,7},{4,8},{5,9},{6,10},{7,11},{8,12},{9,13},{1... | collective-permute-start | bytes 1880072 | tf_op jit(solution)/shard_map/ppermute | solution.py:343
  47.0 2.4 %collective-permute-start.8 = (bf16[272,1152]{1,0:T(8,128)(2,1)S(1)}, bf16[272,1152]{1,0:T(8,128)(2,1)S(1)}, u32[]{:S(2)}, u32[]{:S(2)}) collective-permute-start(bf16[272,1152]{1,0:T(8,128)(2,1)S(1)} %get-tuple-element.67.refs_2_), channel_id=1, source_target_pairs={{0,12},{1,13},{2,14},{3,15},{4,0},{5,1},{6,2},{7,3},{8,4},{9,5},{1... | collective-permute-start | bytes 1880072 | tf_op jit(solution)/shard_map/ppermute | solution.py:343
  49.3 0.1 collective-permute-done.9.refs_0_
  49.5 0.1 merge_far.1.refs_1_.refs_7_
  49.6 6.8 %far.1 = (bf16[512,512]{1,0:T(8,128)(2,1)S(1)}, bf16[512,512]{1,0:T(8,128)(2,1)S(1)}, bf16[512,512]{1,0:T(8,128)(2,1)S(1)}, bf16[512,512]{1,0:T(8,128)(2,1)S(1)}...) custom-call(f32[3]{0:T(128)S(1)} %pad_maximum_fusion.refs_0_, ...), custom_call_target="tpu_custom_call" | custom-call | flops 20000000000 | tf_op jit(solution)/shard_map/far/pallas_call | solution.py:30
  56.4 1.3 %collective-permute-start.12 = (bf16[272,1152]{1,0:T(8,128)(2,1)S(1)}, bf16[272,1152]{1,0:T(8,128)(2,1)S(1)}, u32[]{:S(2)}, u32[]{:S(2)}) collective-permute-start(bf16[272,1152]{1,0:T(8,128)(2,1)S(1)} %get-tuple-element.78), channel_id=1, source_target_pairs={{0,4},{1,5},{2,6},{3,7},{4,8},{5,9},{6,10},{7,11},{8,12},{9,13},{1... | collective-permute-start | bytes 1880072 | tf_op jit(solution)/shard_map/ppermute | solution.py:343
  57.7 2.0 %collective-permute-start.11 = (bf16[272,1152]{1,0:T(8,128)(2,1)S(1)}, bf16[272,1152]{1,0:T(8,128)(2,1)S(1)}, u32[]{:S(2)}, u32[]{:S(2)}) collective-permute-start(bf16[272,1152]{1,0:T(8,128)(2,1)S(1)} %get-tuple-element.75.refs_6_), channel_id=1, source_target_pairs={{0,12},{1,13},{2,14},{3,15},{4,0},{5,1},{6,2},{7,3},{8,4},{9,5},{1... | collective-permute-start | bytes 1880072 | tf_op jit(solution)/shard_map/ppermute | solution.py:343
  59.7 4.3 %first_y.1 = (bf16[512,512]{1,0:T(8,128)(2,1)S(1)}, bf16[512,512]{1,0:T(8,128)(2,1)S(1)}, f32[512,1152]{1,0:T(8,128)S(1)}, f32[512,128]{1,0:T(8,128)S(1)}) custom-call(f32[3]{0:T(128)S(1)} %pad_maximum_fusion.refs_0_, bf16[512,1152]{1,0:T(8,128)(2,1)S(1)} %get-tuple-element.57.refs_1_.refs_5_, bf16[512,1152]{1,0:T(8,128)(2,1)S(1)} %hold_text.1.refs_2_.refs_4_, ...), custom_call_target="tpu_custom_call" | custom-call | flops 20000000000 | tf_op jit(solution)/shard_map/first_y/pallas_call | solution.py:30
  64.1 3.0 %cols_yc.1.refs_8_ = bf16[512,1152]{1,0:T(8,128)(2,1)S(1)} custom-call(bf16[512,512]{1,0:T(8,128)(2,1)S(1)} %get-tuple-element.87.refs_0_, bf16[512,512]{1,0:T(8,128)(2,1)S(1)} %get-tuple-element.88.refs_1_, bf16[512,512]{1,0:T(8,128)(2,1)S(1)} %get-tuple-element.89.refs_2_, bf16[512,512]{1,0:T(8,128)(2,1)S(1)} %get-tuple-element.90.refs_3_, ...), custom_call_target="tpu_custom_call" | custom-call | flops 20000000000 | tf_op jit(solution)/shard_map/cols_yc/pallas_call | solution.py:30
  67.1 3.0 %cols_y.1.refs_0_ = f32[512,1152]{1,0:T(8,128)S(1)} custom-call(bf16[512,512]{1,0:T(8,128)(2,1)S(1)} %get-tuple-element.83.refs_0_, bf16[512,512]{1,0:T(8,128)(2,1)S(1)} %get-tuple-element.84.refs_1_, bf16[512,512]{1,0:T(8,128)(2,1)S(1)} %get-tuple-element.85.refs_2_, bf16[512,512]{1,0:T(8,128)(2,1)S(1)} %get-tuple-element.86.refs_3_, ...), custom_call_target="tpu_custom_call" | custom-call | flops 20000000000 | tf_op jit(solution)/shard_map/cols_y/pallas_call | solution.py:30
  70.1 0.3 add_y.1.refs_8_
  70.4 3.3 %collective-permute-start.17 = (bf16[512,1152]{1,0:T(8,128)(2,1)S(1)}, bf16[512,1152]{1,0:T(8,128)(2,1)S(1)}, u32[]{:S(2)}, u32[]{:S(2)}) collective-permute-start(bf16[512,1152]{1,0:T(8,128)(2,1)S(1)} %add_y.1.refs_8_), channel_id=1, source_target_pairs={{0,2},{1,3},{2,0},{3,1},{4,6},{5,7},{6,4},{7,5},{8,10},{9,11},{10,... | collective-permute-start | bytes 3538952 | tf_op jit(solution)/shard_map/ppermute | solution.py:343
  73.8 3.0 %cols_c.1.refs_4_ = bf16[512,1152]{1,0:T(8,128)(2,1)S(1)} custom-call(bf16[512,512]{1,0:T(8,128)(2,1)S(1)} %get-tuple-element.79.refs_0_, bf16[512,512]{1,0:T(8,128)(2,1)S(1)} %get-tuple-element.80.refs_1_, bf16[512,512]{1,0:T(8,128)(2,1)S(1)} %get-tuple-element.81.refs_2_, bf16[512,512]{1,0:T(8,128)(2,1)S(1)} %get-tuple-element.82.refs_3_, ...), custom_call_target="tpu_custom_call" | custom-call | flops 20000000000 | tf_op jit(solution)/shard_map/cols_c/pallas_call | solution.py:30
  76.8 0.3 collective-permute-start.16
  77.1 0.5 sums.1
  77.6 1.3 %collective-permute-start.15 = (bf16[272,1152]{1,0:T(8,128)(2,1)S(1)}, bf16[272,1152]{1,0:T(8,128)(2,1)S(1)}, u32[]{:S(2)}, u32[]{:S(2)}) collective-permute-start(bf16[272,1152]{1,0:T(8,128)(2,1)S(1)} %get-tuple-element.95), channel_id=1, source_target_pairs={{0,4},{1,5},{2,6},{3,7},{4,8},{5,9},{6,10},{7,11},{8,12},{9,13},{1... | collective-permute-start | bytes 1880072 | tf_op jit(solution)/shard_map/ppermute | solution.py:343
  78.9 2.0 %collective-permute-start.14 = (bf16[272,1152]{1,0:T(8,128)(2,1)S(1)}, bf16[272,1152]{1,0:T(8,128)(2,1)S(1)}, u32[]{:S(2)}, u32[]{:S(2)}) collective-permute-start(bf16[272,1152]{1,0:T(8,128)(2,1)S(1)} %get-tuple-element.91.refs_8_), channel_id=1, source_target_pairs={{0,12},{1,13},{2,14},{3,15},{4,0},{5,1},{6,2},{7,3},{8,4},{9,5},{1... | collective-permute-start | bytes 1880072 | tf_op jit(solution)/shard_map/ppermute | solution.py:343
  81.0 3.0 %cols_own.1.refs_4_.refs_0_ = f32[512,1152]{1,0:T(8,128)S(1)} custom-call(bf16[512,512]{1,0:T(8,128)(2,1)S(1)} %get-tuple-element.68.refs_0_, bf16[512,512]{1,0:T(8,128)(2,1)S(1)} %get-tuple-element.69.refs_1_, bf16[512,512]{1,0:T(8,128)(2,1)S(1)} %get-tuple-element.70.refs_2_, bf16[512,512]{1,0:T(8,128)(2,1)S(1)} %get-tuple-element.73.refs_3_, ...), custom_call_target="tpu_custom_call" | custom-call | flops 20000000000 | tf_op jit(solution)/shard_map/cols_own/pallas_call | solution.py:30
  84.0 0.3 image_base.1
  84.3 0.2 text_base.1.refs_2_.base
  84.6 1.1 %copy-done.1 = bf16[512,1152]{1,0:T(8,128)(2,1)S(1)} copy-done((bf16[512,1152]{1,0:T(8,128)(2,1)S(1)}, bf16[512,1152]{1,0:T(8,128)(2,1)}, u32[]{:S(2)}) %copy-start.1) | copy-done | bytes 1179672
  85.6 1.1 %prep_text.1 = (f32[512,1152]{1,0:T(8,128)S(1)}, f32[512,128]{1,0:T(8,128)S(1)}) custom-call(f32[3]{0:T(128)S(1)} %pad_maximum_fusion.refs_0_, bf16[512,1152]{1,0:T(8,128)(2,1)S(1)} %copy-done.1, f32[512,1152]{1,0:T(8,128)S(1)} %text_base.1.refs_2_.base), custom_call_target="tpu_custom_call" | custom-call | flops 20000000000 | tf_op jit(solution)/shard_map/prep_text/pallas_call | solution.py:30
  86.7 8.4 %collective-permute-done.15.sum_b = bf16[272,1152]{1,0:T(8,128)(2,1)S(1)} collective-permute-done((bf16[272,1152]{1,0:T(8,128)(2,1)S(1)}, bf16[272,1152]{1,0:T(8,128)(2,1)S(1)}, u32[]{:S(2)}, u32[]{:S(2)}) %collective-permute-start.15) | collective-permute-done | bytes 626720 | tf_op jit(solution)/shard_map/ppermute | solution.py:343
  95.2 2.3 %image.1 = (bf16[512,1152]{1,0:T(8,128)(2,1)}, f32[1,512]{1,0:T(1,128)}, f32[8,128]{1,0:T(8,128)S(1)}) custom-call(f32[512,1152]{1,0:T(8,128)S(1)} %get-tuple-element.92.base, f32[8,512]{1,0:T(8,128)S(1)} %get-tuple-element.93.refs_2_.line, f32[512,1152]{1,0:T(8,128)S(1)} %get-tuple-element.94.unit, ...), custom_call_target="tpu_custom_call" | custom-call | flops 1000 | tf_op jit(solution)/shard_map/image/pallas_call | solution.py:323
  97.5 3.1 %collective-permute-done.17.late = bf16[512,1152]{1,0:T(8,128)(2,1)S(1)} collective-permute-done((bf16[512,1152]{1,0:T(8,128)(2,1)S(1)}, bf16[512,1152]{1,0:T(8,128)(2,1)S(1)}, u32[]{:S(2)}, u32[]{:S(2)}) %collective-permute-start.17) | collective-permute-done | bytes 1179680 | tf_op jit(solution)/shard_map/ppermute | solution.py:343
  100.6 1.7 %text.1 = bf16[512,1152]{1,0:T(8,128)(2,1)} custom-call(f32[512,1152]{1,0:T(8,128)S(1)} %text_base.1.refs_2_.base, f32[512,1152]{1,0:T(8,128)S(1)} %get-tuple-element.99.unit, f32[512,128]{1,0:T(8,128)S(1)} %get-tuple-element.96.ready.factor, bf16[512,1152]{1,0:T(8,128)(2,1)S(1)} %collective-permute-done.17.late, f32[8,128]{1,0:T(8,128)S(1)} %get-tuple-element.100.done), custom_call_target="tpu_custom_call" | custom-call | flops 1000 | tf_op jit(solution)/shard_map/text/pallas_call | solution.py:323
  (19 shorter events, 0.3 us)
Async XLA Ops:
  0.6 5.2 %copy-start = (bf16[512,1152]{1,0:T(8,128)(2,1)S(1)}, bf16[512,1152]{1,0:T(8,128)(2,1)}, u32[]{:S(2)}) copy-start(bf16[512,1152]{1,0:T(8,128)(2,1)} %refs_1_.2) | copy-start | bytes 3538948
  2.3 9.7 %collective-permute-start.3 = (bf16[512,1152]{1,0:T(8,128)(2,1)S(1)}, bf16[512,1152]{1,0:T(8,128)(2,1)S(1)}, u32[]{:S(2)}, u32[]{:S(2)}) collective-permute-start(bf16[512,1152]{1,0:T(8,128)(2,1)S(1)} %norm_text.1.refs_1_.refs_2_), channel_id=1, source_target_pairs={{0,1},{1,0},{2,3},{3,2},{4,5},{5,4},{6,7},{7,6},{8,9},{9,8},{10,11... | collective-permute-start | bytes 3538952 | tf_op jit(solution)/shard_map/ppermute | solution.py:343
  2.4 30.8 %collective-permute-start = (bf16[512,1152]{1,0:T(8,128)(2,1)S(1)}, bf16[512,1152]{1,0:T(8,128)(2,1)S(1)}, u32[]{:S(2)}, u32[]{:S(2)}) collective-permute-start(bf16[512,1152]{1,0:T(8,128)(2,1)S(1)} %norm_text.1.refs_1_.refs_2_), channel_id=1, source_target_pairs={{0,2},{1,3},{2,0},{3,1},{4,6},{5,7},{6,4},{7,5},{8,10},{9,11},{10,... | collective-permute-start | bytes 3538952 | tf_op jit(solution)/shard_map/ppermute | solution.py:343
  6.5 18.2 %collective-permute-start.1 = (bf16[256,1152]{1,0:T(8,128)(2,1)S(1)}, bf16[256,1152]{1,0:T(8,128)(2,1)S(1)}, u32[]{:S(2)}, u32[]{:S(2)}) collective-permute-start(bf16[256,1152]{1,0:T(8,128)(2,1)S(1)} %get-tuple-element.53.refs_0_), channel_id=1, source_target_pairs={{0,4},{1,5},{2,6},{3,7},{4,8},{5,9},{6,10},{7,11},{8,12},{9,13},{1... | collective-permute-start | bytes 1769480 | tf_op jit(solution)/shard_map/ppermute | solution.py:343
  8.4 16.2 %collective-permute-start.2 = (bf16[256,1152]{1,0:T(8,128)(2,1)S(1)}, bf16[256,1152]{1,0:T(8,128)(2,1)S(1)}, u32[]{:S(2)}, u32[]{:S(2)}) collective-permute-start(bf16[256,1152]{1,0:T(8,128)(2,1)S(1)} %get-tuple-element.54.refs_1_), channel_id=1, source_target_pairs={{0,12},{1,13},{2,14},{3,15},{4,0},{5,1},{6,2},{7,3},{8,4},{9,5},{1... | collective-permute-start | bytes 1769480 | tf_op jit(solution)/shard_map/ppermute | solution.py:343
  12.2 26.8 %collective-permute-start.5 = (bf16[256,1152]{1,0:T(8,128)(2,1)S(1)}, bf16[256,1152]{1,0:T(8,128)(2,1)S(1)}, u32[]{:S(2)}, u32[]{:S(2)}) collective-permute-start(bf16[256,1152]{1,0:T(8,128)(2,1)S(1)} %get-tuple-element.65), channel_id=1, source_target_pairs={{0,4},{1,5},{2,6},{3,7},{4,8},{5,9},{6,10},{7,11},{8,12},{9,13},{1... | collective-permute-start | bytes 1769480 | tf_op jit(solution)/shard_map/ppermute | solution.py:343
  12.2 26.7 %collective-permute-start.6 = (bf16[256,1152]{1,0:T(8,128)(2,1)S(1)}, bf16[256,1152]{1,0:T(8,128)(2,1)S(1)}, u32[]{:S(2)}, u32[]{:S(2)}) collective-permute-start(bf16[256,1152]{1,0:T(8,128)(2,1)S(1)} %get-tuple-element.55.refs_4_), channel_id=1, source_target_pairs={{0,12},{1,13},{2,14},{3,15},{4,0},{5,1},{6,2},{7,3},{8,4},{9,5},{1... | collective-permute-start | bytes 1769480 | tf_op jit(solution)/shard_map/ppermute | solution.py:343
  24.9 24.6 %collective-permute-start.9 = (bf16[256,1152]{1,0:T(8,128)(2,1)S(1)}, bf16[256,1152]{1,0:T(8,128)(2,1)S(1)}, u32[]{:S(2)}, u32[]{:S(2)}) collective-permute-start(bf16[256,1152]{1,0:T(8,128)(2,1)S(1)} %get-tuple-element.71), channel_id=1, source_target_pairs={{0,4},{1,5},{2,6},{3,7},{4,8},{5,9},{6,10},{7,11},{8,12},{9,13},{1... | collective-permute-start | bytes 1769480 | tf_op jit(solution)/shard_map/ppermute | solution.py:343
  26.8 22.7 %collective-permute-start.10 = (bf16[256,1152]{1,0:T(8,128)(2,1)S(1)}, bf16[256,1152]{1,0:T(8,128)(2,1)S(1)}, u32[]{:S(2)}, u32[]{:S(2)}) collective-permute-start(bf16[256,1152]{1,0:T(8,128)(2,1)S(1)} %get-tuple-element.72), channel_id=1, source_target_pairs={{0,12},{1,13},{2,14},{3,15},{4,0},{5,1},{6,2},{7,3},{8,4},{9,5},{1... | collective-permute-start | bytes 1769480 | tf_op jit(solution)/shard_map/ppermute | solution.py:343
  33.4 2.9 %collective-permute-start.4 = (bf16[512,1152]{1,0:T(8,128)(2,1)S(1)}, bf16[512,1152]{1,0:T(8,128)(2,1)S(1)}, u32[]{:S(2)}, u32[]{:S(2)}) collective-permute-start(bf16[512,1152]{1,0:T(8,128)(2,1)S(1)} %hold_text.1.refs_2_.refs_4_), channel_id=1, source_target_pairs={{0,1},{1,0},{2,3},{3,2},{4,5},{5,4},{6,7},{7,6},{8,9},{9,8},{10,11... | collective-permute-start | bytes 3538952 | tf_op jit(solution)/shard_map/ppermute | solution.py:343
  45.8 27.9 %collective-permute-start.7 = (bf16[272,1152]{1,0:T(8,128)(2,1)S(1)}, bf16[272,1152]{1,0:T(8,128)(2,1)S(1)}, u32[]{:S(2)}, u32[]{:S(2)}) collective-permute-start(bf16[272,1152]{1,0:T(8,128)(2,1)S(1)} %get-tuple-element.66), channel_id=1, source_target_pairs={{0,4},{1,5},{2,6},{3,7},{4,8},{5,9},{6,10},{7,11},{8,12},{9,13},{1... | collective-permute-start | bytes 1880072 | tf_op jit(solution)/shard_map/ppermute | solution.py:343
  47.0 26.8 %collective-permute-start.8 = (bf16[272,1152]{1,0:T(8,128)(2,1)S(1)}, bf16[272,1152]{1,0:T(8,128)(2,1)S(1)}, u32[]{:S(2)}, u32[]{:S(2)}) collective-permute-start(bf16[272,1152]{1,0:T(8,128)(2,1)S(1)} %get-tuple-element.67.refs_2_), channel_id=1, source_target_pairs={{0,12},{1,13},{2,14},{3,15},{4,0},{5,1},{6,2},{7,3},{8,4},{9,5},{1... | collective-permute-start | bytes 1880072 | tf_op jit(solution)/shard_map/ppermute | solution.py:343
  56.4 20.7 %collective-permute-start.12 = (bf16[272,1152]{1,0:T(8,128)(2,1)S(1)}, bf16[272,1152]{1,0:T(8,128)(2,1)S(1)}, u32[]{:S(2)}, u32[]{:S(2)}) collective-permute-start(bf16[272,1152]{1,0:T(8,128)(2,1)S(1)} %get-tuple-element.78), channel_id=1, source_target_pairs={{0,4},{1,5},{2,6},{3,7},{4,8},{5,9},{6,10},{7,11},{8,12},{9,13},{1... | collective-permute-start | bytes 1880072 | tf_op jit(solution)/shard_map/ppermute | solution.py:343
  57.7 19.4 %collective-permute-start.11 = (bf16[272,1152]{1,0:T(8,128)(2,1)S(1)}, bf16[272,1152]{1,0:T(8,128)(2,1)S(1)}, u32[]{:S(2)}, u32[]{:S(2)}) collective-permute-start(bf16[272,1152]{1,0:T(8,128)(2,1)S(1)} %get-tuple-element.75.refs_6_), channel_id=1, source_target_pairs={{0,12},{1,13},{2,14},{3,15},{4,0},{5,1},{6,2},{7,3},{8,4},{9,5},{1... | collective-permute-start | bytes 1880072 | tf_op jit(solution)/shard_map/ppermute | solution.py:343
  67.0 3.1 %collective-permute-start.13 = (bf16[512,1152]{1,0:T(8,128)(2,1)S(1)}, bf16[512,1152]{1,0:T(8,128)(2,1)S(1)}, u32[]{:S(2)}, u32[]{:S(2)}) collective-permute-start(bf16[512,1152]{1,0:T(8,128)(2,1)S(1)} %cols_yc.1.refs_8_), channel_id=1, source_target_pairs={{0,1},{1,0},{2,3},{3,2},{4,5},{5,4},{6,7},{7,6},{8,9},{9,8},{10,11... | collective-permute-start | bytes 3538952 | tf_op jit(solution)/shard_map/ppermute | solution.py:343
  70.4 30.2 %collective-permute-start.17 = (bf16[512,1152]{1,0:T(8,128)(2,1)S(1)}, bf16[512,1152]{1,0:T(8,128)(2,1)S(1)}, u32[]{:S(2)}, u32[]{:S(2)}) collective-permute-start(bf16[512,1152]{1,0:T(8,128)(2,1)S(1)} %add_y.1.refs_8_), channel_id=1, source_target_pairs={{0,2},{1,3},{2,0},{3,1},{4,6},{5,7},{6,4},{7,5},{8,10},{9,11},{10,... | collective-permute-start | bytes 3538952 | tf_op jit(solution)/shard_map/ppermute | solution.py:343
  76.8 7.6 %collective-permute-start.16 = (bf16[512,1152]{1,0:T(8,128)(2,1)S(1)}, bf16[512,1152]{1,0:T(8,128)(2,1)S(1)}, u32[]{:S(2)}, u32[]{:S(2)}) collective-permute-start(bf16[512,1152]{1,0:T(8,128)(2,1)S(1)} %cols_c.1.refs_4_), channel_id=1, source_target_pairs={{0,1},{1,0},{2,3},{3,2},{4,5},{5,4},{6,7},{7,6},{8,9},{9,8},{10,11... | collective-permute-start | bytes 3538952 | tf_op jit(solution)/shard_map/ppermute | solution.py:343
  77.6 17.6 %collective-permute-start.15 = (bf16[272,1152]{1,0:T(8,128)(2,1)S(1)}, bf16[272,1152]{1,0:T(8,128)(2,1)S(1)}, u32[]{:S(2)}, u32[]{:S(2)}) collective-permute-start(bf16[272,1152]{1,0:T(8,128)(2,1)S(1)} %get-tuple-element.95), channel_id=1, source_target_pairs={{0,4},{1,5},{2,6},{3,7},{4,8},{5,9},{6,10},{7,11},{8,12},{9,13},{1... | collective-permute-start | bytes 1880072 | tf_op jit(solution)/shard_map/ppermute | solution.py:343
  78.9 16.2 %collective-permute-start.14 = (bf16[272,1152]{1,0:T(8,128)(2,1)S(1)}, bf16[272,1152]{1,0:T(8,128)(2,1)S(1)}, u32[]{:S(2)}, u32[]{:S(2)}) collective-permute-start(bf16[272,1152]{1,0:T(8,128)(2,1)S(1)} %get-tuple-element.91.refs_8_), channel_id=1, source_target_pairs={{0,12},{1,13},{2,14},{3,15},{4,0},{5,1},{6,2},{7,3},{8,4},{9,5},{1... | collective-permute-start | bytes 1880072 | tf_op jit(solution)/shard_map/ppermute | solution.py:343
  84.3 1.3 %copy-start.1 = (bf16[512,1152]{1,0:T(8,128)(2,1)S(1)}, bf16[512,1152]{1,0:T(8,128)(2,1)}, u32[]{:S(2)}) copy-start(bf16[512,1152]{1,0:T(8,128)(2,1)} %refs_1_.3) | copy-start | bytes 3538948

commit v7 on v6

--- a/solution.py
+++ b/solution.py
@@ -356,12 +356,11 @@
     first, prev_a, next_b = merge("merge_first", prev_a, next_b, s_own[1:], copies=True)
     far_a, far_b = move(prev_a, dz=1), move(next_b, dz=-1)
     (first_0, first_c), s_first = rows_step("first_c", scal, first, near_t)
-    i_unit, i_factor = prepare(scal, image_embeds, "prep_image", s_first[1:])
-    (txt_y,) = hold("hold_text", [txt_y], [i_factor])
+    (txt_y,) = hold("hold_text", [txt_y], s_first[1:])
     far_t = [txt_y, move(txt_y, dc=1)]
-    (own_y,), s_own = rows_step("own_y", scal, own, far_t[:1], s_own, after=[i_factor])
+    (own_y,), s_own = rows_step("own_y", scal, own, far_t[:1], s_own, after=[txt_y])
     (own_yc,), s_own = rows_step("own_yc", scal, own, far_t[1:], s_own)
-    kept = [i_factor, s_own[1]]
+    kept = [s_own[1]]
     (last,) = merge("merge_last", prev_b, next_a, s_own[1:])
     (last_0, last_c, last_y, last_yc), (g_prev_b, g_next_a) = rows_step(
         "last", scal, last, near_t + far_t, finish=2, after=kept
@@ -399,7 +398,8 @@
     (t_base,) = call(
         text_base_kernel, "text_base", [gt_own, text_c], [pltpu.VMEM((rows, width), F32)], [line], cost=1000
     )
-    t_unit, t_factor = prepare(scal, text_embeds, "prep_text", [t_base])
+    i_unit, i_factor = prepare(scal, image_embeds, "prep_image", [t_base])
+    t_unit, t_factor = prepare(scal, text_embeds, "prep_text", [i_factor])
     grad_image, loss, done = final(
         functools.partial(image_kernel, total),
         "image",

time: 103 us -> 103 us (level)
  waiting for transfers between devices: 17.1 us -> 16 us
    ppermute x18, waiting for transfers between devices: 17.1 us -> 16 us  [move(): return lax.ppermute(value, 'loss', pairs)]
  transfers between devices with their start and end apart: 18 -> 18, of which waited for: 6 -> 7; matrix products, arithmetic and copies ran while one was open for 0% -> 0% of each run, Pallas kernels for 49% -> 49%
where the time goes in v7:
time: 103 us; the launch traced here: 102 us
  Pallas kernels  53.4 us (52%)
  starting transfers between devices  29.3 us (28%)
  waiting for transfers between devices  16 us (16%)
  between operations  2.4 us (2%)
  local copies, waits for them, and re-layouts  1.21 us (1%)
    pallas_call x23, Pallas kernels, call(): pl.pallas_call(body, name=name, in_specs=specs, out_specs=[VMEM] * len(ou...  47.6 us
    ppermute x18, starting transfers between devices, move(): return lax.ppermute(value, 'loss', pairs)  29.3 us
    ppermute x18, waiting for transfers between devices, move(): return lax.ppermute(value, 'loss', pairs)  16 us
    pallas_call x2, Pallas kernels, final(): pl.pallas_call(kernel, name=name, in_specs=[VMEM] * len(inputs), out_spec...  4.08 us
  transfers between devices with their start and end apart: 18, of which 7 were waited for; matrix products, arithmetic and copies ran while one was open for 0% of the time, Pallas kernels for 49%

profile of v7, /device:TPU:0, one launch (start us, length us, event | category | flops | bytes accessed | tf_op | source)
XLA Modules:
  0.0 102.4 jit_solution(15321744180789840953)
XLA Ops:
  0.6 1.7 %norm_text.1.refs_1_.refs_2_ = bf16[512,1152]{1,0:T(8,128)(2,1)S(1)} custom-call(bf16[512,1152]{1,0:T(8,128)(2,1)} %refs_1_.3), custom_call_target="tpu_custom_call" | custom-call | flops 20000000000 | tf_op jit(solution)/shard_map/norm_text/pallas_call | solution.py:81
  2.4 3.4 %collective-permute-start = (bf16[512,1152]{1,0:T(8,128)(2,1)S(1)}, bf16[512,1152]{1,0:T(8,128)(2,1)S(1)}, u32[]{:S(2)}, u32[]{:S(2)}) collective-permute-start(bf16[512,1152]{1,0:T(8,128)(2,1)S(1)} %norm_text.1.refs_1_.refs_2_), channel_id=1, source_target_pairs={{0,2},{1,3},{2,0},{3,1},{4,6},{5,7},{6,4},{7,5},{8,10},{9,11},{10,... | collective-permute-start | bytes 3538952 | tf_op jit(solution)/shard_map/ppermute | solution.py:343
  5.8 0.7 norm_image.1
  6.5 2.0 %collective-permute-start.1 = (bf16[256,1152]{1,0:T(8,128)(2,1)S(1)}, bf16[256,1152]{1,0:T(8,128)(2,1)S(1)}, u32[]{:S(2)}, u32[]{:S(2)}) collective-permute-start(bf16[256,1152]{1,0:T(8,128)(2,1)S(1)} %get-tuple-element.53.refs_0_), channel_id=1, source_target_pairs={{0,4},{1,5},{2,6},{3,7},{4,8},{5,9},{6,10},{7,11},{8,12},{9,13},{1... | collective-permute-start | bytes 1769480 | tf_op jit(solution)/shard_map/ppermute | solution.py:343
  8.4 2.2 %collective-permute-start.2 = (bf16[256,1152]{1,0:T(8,128)(2,1)S(1)}, bf16[256,1152]{1,0:T(8,128)(2,1)S(1)}, u32[]{:S(2)}, u32[]{:S(2)}) collective-permute-start(bf16[256,1152]{1,0:T(8,128)(2,1)S(1)} %get-tuple-element.54.refs_1_), channel_id=1, source_target_pairs={{0,12},{1,13},{2,14},{3,15},{4,0},{5,1},{6,2},{7,3},{8,4},{9,5},{1... | collective-permute-start | bytes 1769480 | tf_op jit(solution)/shard_map/ppermute | solution.py:343
  12.2 3.2 %collective-permute-start.6 = (bf16[256,1152]{1,0:T(8,128)(2,1)S(1)}, bf16[256,1152]{1,0:T(8,128)(2,1)S(1)}, u32[]{:S(2)}, u32[]{:S(2)}) collective-permute-start(bf16[256,1152]{1,0:T(8,128)(2,1)S(1)} %get-tuple-element.55.refs_4_), channel_id=1, source_target_pairs={{0,12},{1,13},{2,14},{3,15},{4,0},{5,1},{6,2},{7,3},{8,4},{9,5},{1... | collective-permute-start | bytes 1769480 | tf_op jit(solution)/shard_map/ppermute | solution.py:343
  15.5 4.1 %own_c.1 = (bf16[512,512]{1,0:T(8,128)(2,1)S(1)}, bf16[512,512]{1,0:T(8,128)(2,1)S(1)}, f32[512,1152]{1,0:T(8,128)S(1)}, f32[512,128]{1,0:T(8,128)S(1)}) custom-call(f32[3]{0:T(128)S(1)} %pad_maximum_fusion.refs_0_, bf16[512,1152]{1,0:T(8,128)(2,1)S(1)} %get-tuple-element.52.refs_1_.refs_4_, bf16[512,1152]{1,0:T(8,128)(2,1)S(1)} %norm_text.1.refs_1_.refs_2_, ...), custom_call_target="tpu_custom_call" | custom-call | flops 20000000000 | tf_op jit(solution)/shard_map/own_c/pallas_call | solution.py:30
  19.5 5.1 %collective-permute-done.1.refs_0_ = bf16[256,1152]{1,0:T(8,128)(2,1)S(1)} collective-permute-done((bf16[256,1152]{1,0:T(8,128)(2,1)S(1)}, bf16[256,1152]{1,0:T(8,128)(2,1)S(1)}, u32[]{:S(2)}, u32[]{:S(2)}) %collective-permute-start.1) | collective-permute-done | bytes 589856 | tf_op jit(solution)/shard_map/ppermute | solution.py:343
  24.7 0.2 merge_first.1
  24.9 2.0 %collective-permute-start.9 = (bf16[256,1152]{1,0:T(8,128)(2,1)S(1)}, bf16[256,1152]{1,0:T(8,128)(2,1)S(1)}, u32[]{:S(2)}, u32[]{:S(2)}) collective-permute-start(bf16[256,1152]{1,0:T(8,128)(2,1)S(1)} %get-tuple-element.70), channel_id=1, source_target_pairs={{0,4},{1,5},{2,6},{3,7},{4,8},{5,9},{6,10},{7,11},{8,12},{9,13},{1... | collective-permute-start | bytes 1769480 | tf_op jit(solution)/shard_map/ppermute | solution.py:343
  26.8 1.5 %collective-permute-start.10 = (bf16[256,1152]{1,0:T(8,128)(2,1)S(1)}, bf16[256,1152]{1,0:T(8,128)(2,1)S(1)}, u32[]{:S(2)}, u32[]{:S(2)}) collective-permute-start(bf16[256,1152]{1,0:T(8,128)(2,1)S(1)} %get-tuple-element.71), channel_id=1, source_target_pairs={{0,12},{1,13},{2,14},{3,15},{4,0},{5,1},{6,2},{7,3},{8,4},{9,5},{1... | collective-permute-start | bytes 1769480 | tf_op jit(solution)/shard_map/ppermute | solution.py:343
  28.4 3.7 %first_c.1 = (bf16[512,512]{1,0:T(8,128)(2,1)S(1)}, bf16[512,512]{1,0:T(8,128)(2,1)S(1)}, f32[512,1152]{1,0:T(8,128)S(1)}, f32[512,128]{1,0:T(8,128)S(1)}) custom-call(f32[3]{0:T(128)S(1)} %pad_maximum_fusion.refs_0_, bf16[512,1152]{1,0:T(8,128)(2,1)S(1)} %get-tuple-element.57.refs_1_.refs_5_, bf16[512,1152]{1,0:T(8,128)(2,1)S(1)} %norm_text.1.refs_1_.refs_2_, ...), custom_call_target="tpu_custom_call" | custom-call | flops 20000000000 | tf_op jit(solution)/shard_map/first_c/pallas_call | solution.py:30
  32.1 0.2 collective-permute-done.refs_0_
  32.4 0.1 collective-permute-start.4
  32.5 2.6 %own_y.1 = (bf16[512,512]{1,0:T(8,128)(2,1)S(1)}, f32[512,1152]{1,0:T(8,128)S(1)}, f32[512,128]{1,0:T(8,128)S(1)}) custom-call(f32[3]{0:T(128)S(1)} %pad_maximum_fusion.refs_0_, bf16[512,1152]{1,0:T(8,128)(2,1)S(1)} %get-tuple-element.52.refs_1_.refs_4_, bf16[512,1152]{1,0:T(8,128)(2,1)S(1)} %hold_text.1.refs_2_.refs_5_.refs_4_, ...), custom_call_target="tpu_custom_call" | custom-call | flops 20000000000 | tf_op jit(solution)/shard_map/own_y/pallas_call | solution.py:30
  35.2 0.2 collective-permute-done.4.refs_2_.refs_5_.refs_3_
  35.3 2.6 %own_yc.1 = (bf16[512,512]{1,0:T(8,128)(2,1)S(1)}, f32[512,1152]{1,0:T(8,128)S(1)}, f32[512,128]{1,0:T(8,128)S(1)}) custom-call(f32[3]{0:T(128)S(1)} %pad_maximum_fusion.refs_0_, bf16[512,1152]{1,0:T(8,128)(2,1)S(1)} %get-tuple-element.52.refs_1_.refs_4_, bf16[512,1152]{1,0:T(8,128)(2,1)S(1)} %collective-permute-done.4.refs_2_.refs_5_.refs_3_, ...), custom_call_target="tpu_custom_call" | custom-call | flops 20000000000 | tf_op jit(solution)/shard_map/own_yc/pallas_call | solution.py:30
  38.0 0.1 merge_last.1.refs_1_.refs_6_
  38.1 6.8 %last.1 = (bf16[512,512]{1,0:T(8,128)(2,1)S(1)}, bf16[512,512]{1,0:T(8,128)(2,1)S(1)}, bf16[512,512]{1,0:T(8,128)(2,1)S(1)}, bf16[512,512]{1,0:T(8,128)(2,1)S(1)...) custom-call(f32[3]{0:T(128)S(1)} %pad_maximum_fusion.refs_0_, ...), custom_call_target="tpu_custom_call" | custom-call | flops 20000000000 | tf_op jit(solution)/shard_map/last/pallas_call | solution.py:30
  44.9 2.1 %collective-permute-start.7 = (bf16[272,1152]{1,0:T(8,128)(2,1)S(1)}, bf16[272,1152]{1,0:T(8,128)(2,1)S(1)}, u32[]{:S(2)}, u32[]{:S(2)}) collective-permute-start(bf16[272,1152]{1,0:T(8,128)(2,1)S(1)} %get-tuple-element.65), channel_id=1, source_target_pairs={{0,4},{1,5},{2,6},{3,7},{4,8},{5,9},{6,10},{7,11},{8,12},{9,13},{1... | collective-permute-start | bytes 1880072 | tf_op jit(solution)/shard_map/ppermute | solution.py:343
  47.0 2.4 %collective-permute-start.8 = (bf16[272,1152]{1,0:T(8,128)(2,1)S(1)}, bf16[272,1152]{1,0:T(8,128)(2,1)S(1)}, u32[]{:S(2)}, u32[]{:S(2)}) collective-permute-start(bf16[272,1152]{1,0:T(8,128)(2,1)S(1)} %get-tuple-element.66.refs_2_), channel_id=1, source_target_pairs={{0,12},{1,13},{2,14},{3,15},{4,0},{5,1},{6,2},{7,3},{8,4},{9,5},{1... | collective-permute-start | bytes 1880072 | tf_op jit(solution)/shard_map/ppermute | solution.py:343
  49.4 0.1 collective-permute-done.9.refs_0_
  49.5 0.1 merge_far.1.refs_1_.refs_7_
  49.6 6.8 %far.1 = (bf16[512,512]{1,0:T(8,128)(2,1)S(1)}, bf16[512,512]{1,0:T(8,128)(2,1)S(1)}, bf16[512,512]{1,0:T(8,128)(2,1)S(1)}, bf16[512,512]{1,0:T(8,128)(2,1)S(1)}...) custom-call(f32[3]{0:T(128)S(1)} %pad_maximum_fusion.refs_0_, ...), custom_call_target="tpu_custom_call" | custom-call | flops 20000000000 | tf_op jit(solution)/shard_map/far/pallas_call | solution.py:30
  56.4 1.3 %collective-permute-start.12 = (bf16[272,1152]{1,0:T(8,128)(2,1)S(1)}, bf16[272,1152]{1,0:T(8,128)(2,1)S(1)}, u32[]{:S(2)}, u32[]{:S(2)}) collective-permute-start(bf16[272,1152]{1,0:T(8,128)(2,1)S(1)} %get-tuple-element.77), channel_id=1, source_target_pairs={{0,4},{1,5},{2,6},{3,7},{4,8},{5,9},{6,10},{7,11},{8,12},{9,13},{1... | collective-permute-start | bytes 1880072 | tf_op jit(solution)/shard_map/ppermute | solution.py:343
  57.7 2.0 %collective-permute-start.11 = (bf16[272,1152]{1,0:T(8,128)(2,1)S(1)}, bf16[272,1152]{1,0:T(8,128)(2,1)S(1)}, u32[]{:S(2)}, u32[]{:S(2)}) collective-permute-start(bf16[272,1152]{1,0:T(8,128)(2,1)S(1)} %get-tuple-element.74.refs_6_), channel_id=1, source_target_pairs={{0,12},{1,13},{2,14},{3,15},{4,0},{5,1},{6,2},{7,3},{8,4},{9,5},{1... | collective-permute-start | bytes 1880072 | tf_op jit(solution)/shard_map/ppermute | solution.py:343
  59.7 4.3 %first_y.1 = (bf16[512,512]{1,0:T(8,128)(2,1)S(1)}, bf16[512,512]{1,0:T(8,128)(2,1)S(1)}, f32[512,1152]{1,0:T(8,128)S(1)}, f32[512,128]{1,0:T(8,128)S(1)}) custom-call(f32[3]{0:T(128)S(1)} %pad_maximum_fusion.refs_0_, bf16[512,1152]{1,0:T(8,128)(2,1)S(1)} %get-tuple-element.57.refs_1_.refs_5_, bf16[512,1152]{1,0:T(8,128)(2,1)S(1)} %hold_text.1.refs_2_.refs_5_.refs_4_, ...), custom_call_target="tpu_custom_call" | custom-call | flops 20000000000 | tf_op jit(solution)/shard_map/first_y/pallas_call | solution.py:30
  64.1 3.0 %cols_yc.1.refs_8_ = bf16[512,1152]{1,0:T(8,128)(2,1)S(1)} custom-call(bf16[512,512]{1,0:T(8,128)(2,1)S(1)} %get-tuple-element.86.refs_0_, bf16[512,512]{1,0:T(8,128)(2,1)S(1)} %get-tuple-element.87.refs_1_, bf16[512,512]{1,0:T(8,128)(2,1)S(1)} %get-tuple-element.88.refs_2_, bf16[512,512]{1,0:T(8,128)(2,1)S(1)} %get-tuple-element.89.refs_3_, ...), custom_call_target="tpu_custom_call" | custom-call | flops 20000000000 | tf_op jit(solution)/shard_map/cols_yc/pallas_call | solution.py:30
  67.1 3.0 %cols_y.1.refs_0_ = f32[512,1152]{1,0:T(8,128)S(1)} custom-call(bf16[512,512]{1,0:T(8,128)(2,1)S(1)} %get-tuple-element.82.refs_0_, bf16[512,512]{1,0:T(8,128)(2,1)S(1)} %get-tuple-element.83.refs_1_, bf16[512,512]{1,0:T(8,128)(2,1)S(1)} %get-tuple-element.84.refs_2_, bf16[512,512]{1,0:T(8,128)(2,1)S(1)} %get-tuple-element.85.refs_3_, ...), custom_call_target="tpu_custom_call" | custom-call | flops 20000000000 | tf_op jit(solution)/shard_map/cols_y/pallas_call | solution.py:30
  70.1 0.2 add_y.1.refs_8_
  70.3 3.3 %collective-permute-start.17 = (bf16[512,1152]{1,0:T(8,128)(2,1)S(1)}, bf16[512,1152]{1,0:T(8,128)(2,1)S(1)}, u32[]{:S(2)}, u32[]{:S(2)}) collective-permute-start(bf16[512,1152]{1,0:T(8,128)(2,1)S(1)} %add_y.1.refs_8_), channel_id=1, source_target_pairs={{0,2},{1,3},{2,0},{3,1},{4,6},{5,7},{6,4},{7,5},{8,10},{9,11},{10,... | collective-permute-start | bytes 3538952 | tf_op jit(solution)/shard_map/ppermute | solution.py:343
  73.7 3.0 %cols_c.1.refs_4_ = bf16[512,1152]{1,0:T(8,128)(2,1)S(1)} custom-call(bf16[512,512]{1,0:T(8,128)(2,1)S(1)} %get-tuple-element.78.refs_0_, bf16[512,512]{1,0:T(8,128)(2,1)S(1)} %get-tuple-element.79.refs_1_, bf16[512,512]{1,0:T(8,128)(2,1)S(1)} %get-tuple-element.80.refs_2_, bf16[512,512]{1,0:T(8,128)(2,1)S(1)} %get-tuple-element.81.refs_3_, ...), custom_call_target="tpu_custom_call" | custom-call | flops 20000000000 | tf_op jit(solution)/shard_map/cols_c/pallas_call | solution.py:30
  76.7 0.3 collective-permute-start.14
  77.0 0.1 collective-permute-done.12.refs_3_
  77.1 0.5 sums.1
  77.6 1.3 %collective-permute-start.16 = (bf16[272,1152]{1,0:T(8,128)(2,1)S(1)}, bf16[272,1152]{1,0:T(8,128)(2,1)S(1)}, u32[]{:S(2)}, u32[]{:S(2)}) collective-permute-start(bf16[272,1152]{1,0:T(8,128)(2,1)S(1)} %get-tuple-element.95), channel_id=1, source_target_pairs={{0,4},{1,5},{2,6},{3,7},{4,8},{5,9},{6,10},{7,11},{8,12},{9,13},{1... | collective-permute-start | bytes 1880072 | tf_op jit(solution)/shard_map/ppermute | solution.py:343
  79.0 2.0 %collective-permute-start.15 = (bf16[272,1152]{1,0:T(8,128)(2,1)S(1)}, bf16[272,1152]{1,0:T(8,128)(2,1)S(1)}, u32[]{:S(2)}, u32[]{:S(2)}) collective-permute-start(bf16[272,1152]{1,0:T(8,128)(2,1)S(1)} %get-tuple-element.90.refs_8_), channel_id=1, source_target_pairs={{0,12},{1,13},{2,14},{3,15},{4,0},{5,1},{6,2},{7,3},{8,4},{9,5},{1... | collective-permute-start | bytes 1880072 | tf_op jit(solution)/shard_map/ppermute | solution.py:343
  81.0 3.0 %cols_own.1.refs_4_.refs_0_ = f32[512,1152]{1,0:T(8,128)S(1)} custom-call(bf16[512,512]{1,0:T(8,128)(2,1)S(1)} %get-tuple-element.67.refs_0_, bf16[512,512]{1,0:T(8,128)(2,1)S(1)} %get-tuple-element.68.refs_1_, bf16[512,512]{1,0:T(8,128)(2,1)S(1)} %get-tuple-element.69.refs_2_, bf16[512,512]{1,0:T(8,128)(2,1)S(1)} %get-tuple-element.72.refs_3_, ...), custom_call_target="tpu_custom_call" | custom-call | flops 20000000000 | tf_op jit(solution)/shard_map/cols_own/pallas_call | solution.py:30
  84.0 0.3 image_base.1
  84.3 0.2 text_base.1.refs_2_.base
  84.5 1.1 %copy-done.1 = bf16[512,1152]{1,0:T(8,128)(2,1)S(1)} copy-done((bf16[512,1152]{1,0:T(8,128)(2,1)S(1)}, bf16[512,1152]{1,0:T(8,128)(2,1)}, u32[]{:S(2)}) %copy-start.1) | copy-done | bytes 1179672
  85.6 1.1 %prep_image.1 = (f32[512,1152]{1,0:T(8,128)S(1)}, f32[512,128]{1,0:T(8,128)S(1)}) custom-call(f32[3]{0:T(128)S(1)} %pad_maximum_fusion.refs_0_, bf16[512,1152]{1,0:T(8,128)(2,1)S(1)} %copy-done.1, f32[512,1152]{1,0:T(8,128)S(1)} %text_base.1.refs_2_.base), custom_call_target="tpu_custom_call" | custom-call | flops 20000000000 | tf_op jit(solution)/shard_map/prep_image/pallas_call | solution.py:30
  86.7 0.1 copy-done.2
  86.9 1.1 %prep_text.1 = (f32[512,1152]{1,0:T(8,128)S(1)}, f32[512,128]{1,0:T(8,128)S(1)}) custom-call(f32[3]{0:T(128)S(1)} %pad_maximum_fusion.refs_0_, bf16[512,1152]{1,0:T(8,128)(2,1)S(1)} %copy-done.2, f32[512,128]{1,0:T(8,128)S(1)} %get-tuple-element.94.refs_2_.factor), custom_call_target="tpu_custom_call" | custom-call | flops 20000000000 | tf_op jit(solution)/shard_map/prep_text/pallas_call | solution.py:30
  88.0 7.1 %collective-permute-done.16.sum_b = bf16[272,1152]{1,0:T(8,128)(2,1)S(1)} collective-permute-done((bf16[272,1152]{1,0:T(8,128)(2,1)S(1)}, bf16[272,1152]{1,0:T(8,128)(2,1)S(1)}, u32[]{:S(2)}, u32[]{:S(2)}) %collective-permute-start.16) | collective-permute-done | bytes 626720 | tf_op jit(solution)/shard_map/ppermute | solution.py:343
  95.1 2.4 %image.1 = (bf16[512,1152]{1,0:T(8,128)(2,1)}, f32[1,512]{1,0:T(1,128)}, f32[8,128]{1,0:T(8,128)S(1)}) custom-call(f32[512,1152]{1,0:T(8,128)S(1)} %get-tuple-element.91.base, f32[8,512]{1,0:T(8,128)S(1)} %get-tuple-element.92.refs_2_.line, f32[512,1152]{1,0:T(8,128)S(1)} %get-tuple-element.93.unit, f32[512,128]{1,0:T(8,128)S(1)} %get-tuple-element.94.refs_2_.factor, ...), custom_call_target="tpu_custom_call" | custom-call | flops 1000 | tf_op jit(solution)/shard_map/image/pallas_call | solution.py:323
  97.5 3.0 %collective-permute-done.17.late = bf16[512,1152]{1,0:T(8,128)(2,1)S(1)} collective-permute-done((bf16[512,1152]{1,0:T(8,128)(2,1)S(1)}, bf16[512,1152]{1,0:T(8,128)(2,1)S(1)}, u32[]{:S(2)}, u32[]{:S(2)}) %collective-permute-start.17) | collective-permute-done | bytes 1179680 | tf_op jit(solution)/shard_map/ppermute | solution.py:343
  100.5 1.7 %text.1 = bf16[512,1152]{1,0:T(8,128)(2,1)} custom-call(f32[512,1152]{1,0:T(8,128)S(1)} %text_base.1.refs_2_.base, f32[512,1152]{1,0:T(8,128)S(1)} %get-tuple-element.99.unit, f32[512,128]{1,0:T(8,128)S(1)} %get-tuple-element.96.ready.factor, bf16[512,1152]{1,0:T(8,128)(2,1)S(1)} %collective-permute-done.17.late, f32[8,128]{1,0:T(8,128)S(1)} %get-tuple-element.100.done), custom_call_target="tpu_custom_call" | custom-call | flops 1000 | tf_op jit(solution)/shard_map/text/pallas_call | solution.py:323
  (21 shorter events, 0.5 us)
Async XLA Ops:
  0.6 5.2 %copy-start = (bf16[512,1152]{1,0:T(8,128)(2,1)S(1)}, bf16[512,1152]{1,0:T(8,128)(2,1)}, u32[]{:S(2)}) copy-start(bf16[512,1152]{1,0:T(8,128)(2,1)} %refs_1_.2) | copy-start | bytes 3538948
  2.3 9.7 %collective-permute-start.3 = (bf16[512,1152]{1,0:T(8,128)(2,1)S(1)}, bf16[512,1152]{1,0:T(8,128)(2,1)S(1)}, u32[]{:S(2)}, u32[]{:S(2)}) collective-permute-start(bf16[512,1152]{1,0:T(8,128)(2,1)S(1)} %norm_text.1.refs_1_.refs_2_), channel_id=1, source_target_pairs={{0,1},{1,0},{2,3},{3,2},{4,5},{5,4},{6,7},{7,6},{8,9},{9,8},{10,11... | collective-permute-start | bytes 3538952 | tf_op jit(solution)/shard_map/ppermute | solution.py:343
  2.4 29.9 %collective-permute-start = (bf16[512,1152]{1,0:T(8,128)(2,1)S(1)}, bf16[512,1152]{1,0:T(8,128)(2,1)S(1)}, u32[]{:S(2)}, u32[]{:S(2)}) collective-permute-start(bf16[512,1152]{1,0:T(8,128)(2,1)S(1)} %norm_text.1.refs_1_.refs_2_), channel_id=1, source_target_pairs={{0,2},{1,3},{2,0},{3,1},{4,6},{5,7},{6,4},{7,5},{8,10},{9,11},{10,... | collective-permute-start | bytes 3538952 | tf_op jit(solution)/shard_map/ppermute | solution.py:343
  6.5 18.2 %collective-permute-start.1 = (bf16[256,1152]{1,0:T(8,128)(2,1)S(1)}, bf16[256,1152]{1,0:T(8,128)(2,1)S(1)}, u32[]{:S(2)}, u32[]{:S(2)}) collective-permute-start(bf16[256,1152]{1,0:T(8,128)(2,1)S(1)} %get-tuple-element.53.refs_0_), channel_id=1, source_target_pairs={{0,4},{1,5},{2,6},{3,7},{4,8},{5,9},{6,10},{7,11},{8,12},{9,13},{1... | collective-permute-start | bytes 1769480 | tf_op jit(solution)/shard_map/ppermute | solution.py:343
  8.4 16.2 %collective-permute-start.2 = (bf16[256,1152]{1,0:T(8,128)(2,1)S(1)}, bf16[256,1152]{1,0:T(8,128)(2,1)S(1)}, u32[]{:S(2)}, u32[]{:S(2)}) collective-permute-start(bf16[256,1152]{1,0:T(8,128)(2,1)S(1)} %get-tuple-element.54.refs_1_), channel_id=1, source_target_pairs={{0,12},{1,13},{2,14},{3,15},{4,0},{5,1},{6,2},{7,3},{8,4},{9,5},{1... | collective-permute-start | bytes 1769480 | tf_op jit(solution)/shard_map/ppermute | solution.py:343
  12.2 25.8 %collective-permute-start.5 = (bf16[256,1152]{1,0:T(8,128)(2,1)S(1)}, bf16[256,1152]{1,0:T(8,128)(2,1)S(1)}, u32[]{:S(2)}, u32[]{:S(2)}) collective-permute-start(bf16[256,1152]{1,0:T(8,128)(2,1)S(1)} %get-tuple-element.64), channel_id=1, source_target_pairs={{0,4},{1,5},{2,6},{3,7},{4,8},{5,9},{6,10},{7,11},{8,12},{9,13},{1... | collective-permute-start | bytes 1769480 | tf_op jit(solution)/shard_map/ppermute | solution.py:343
  12.2 25.7 %collective-permute-start.6 = (bf16[256,1152]{1,0:T(8,128)(2,1)S(1)}, bf16[256,1152]{1,0:T(8,128)(2,1)S(1)}, u32[]{:S(2)}, u32[]{:S(2)}) collective-permute-start(bf16[256,1152]{1,0:T(8,128)(2,1)S(1)} %get-tuple-element.55.refs_4_), channel_id=1, source_target_pairs={{0,12},{1,13},{2,14},{3,15},{4,0},{5,1},{6,2},{7,3},{8,4},{9,5},{1... | collective-permute-start | bytes 1769480 | tf_op jit(solution)/shard_map/ppermute | solution.py:343
  24.9 24.6 %collective-permute-start.9 = (bf16[256,1152]{1,0:T(8,128)(2,1)S(1)}, bf16[256,1152]{1,0:T(8,128)(2,1)S(1)}, u32[]{:S(2)}, u32[]{:S(2)}) collective-permute-start(bf16[256,1152]{1,0:T(8,128)(2,1)S(1)} %get-tuple-element.70), channel_id=1, source_target_pairs={{0,4},{1,5},{2,6},{3,7},{4,8},{5,9},{6,10},{7,11},{8,12},{9,13},{1... | collective-permute-start | bytes 1769480 | tf_op jit(solution)/shard_map/ppermute | solution.py:343
  26.8 22.7 %collective-permute-start.10 = (bf16[256,1152]{1,0:T(8,128)(2,1)S(1)}, bf16[256,1152]{1,0:T(8,128)(2,1)S(1)}, u32[]{:S(2)}, u32[]{:S(2)}) collective-permute-start(bf16[256,1152]{1,0:T(8,128)(2,1)S(1)} %get-tuple-element.71), channel_id=1, source_target_pairs={{0,12},{1,13},{2,14},{3,15},{4,0},{5,1},{6,2},{7,3},{8,4},{9,5},{1... | collective-permute-start | bytes 1769480 | tf_op jit(solution)/shard_map/ppermute | solution.py:343
  32.4 2.9 %collective-permute-start.4 = (bf16[512,1152]{1,0:T(8,128)(2,1)S(1)}, bf16[512,1152]{1,0:T(8,128)(2,1)S(1)}, u32[]{:S(2)}, u32[]{:S(2)}) collective-permute-start(bf16[512,1152]{1,0:T(8,128)(2,1)S(1)} %hold_text.1.refs_2_.refs_5_.refs_4_), channel_id=1, source_target_pairs={{0,1},{1,0},{2,3},{3,2},{4,5},{5,4},{6,7},{7,6},{8,9},{9,8},{10,11... | collective-permute-start | bytes 3538952 | tf_op jit(solution)/shard_map/ppermute | solution.py:343
  44.9 28.8 %collective-permute-start.7 = (bf16[272,1152]{1,0:T(8,128)(2,1)S(1)}, bf16[272,1152]{1,0:T(8,128)(2,1)S(1)}, u32[]{:S(2)}, u32[]{:S(2)}) collective-permute-start(bf16[272,1152]{1,0:T(8,128)(2,1)S(1)} %get-tuple-element.65), channel_id=1, source_target_pairs={{0,4},{1,5},{2,6},{3,7},{4,8},{5,9},{6,10},{7,11},{8,12},{9,13},{1... | collective-permute-start | bytes 1880072 | tf_op jit(solution)/shard_map/ppermute | solution.py:343
  47.0 26.7 %collective-permute-start.8 = (bf16[272,1152]{1,0:T(8,128)(2,1)S(1)}, bf16[272,1152]{1,0:T(8,128)(2,1)S(1)}, u32[]{:S(2)}, u32[]{:S(2)}) collective-permute-start(bf16[272,1152]{1,0:T(8,128)(2,1)S(1)} %get-tuple-element.66.refs_2_), channel_id=1, source_target_pairs={{0,12},{1,13},{2,14},{3,15},{4,0},{5,1},{6,2},{7,3},{8,4},{9,5},{1... | collective-permute-start | bytes 1880072 | tf_op jit(solution)/shard_map/ppermute | solution.py:343
  56.4 20.7 %collective-permute-start.12 = (bf16[272,1152]{1,0:T(8,128)(2,1)S(1)}, bf16[272,1152]{1,0:T(8,128)(2,1)S(1)}, u32[]{:S(2)}, u32[]{:S(2)}) collective-permute-start(bf16[272,1152]{1,0:T(8,128)(2,1)S(1)} %get-tuple-element.77), channel_id=1, source_target_pairs={{0,4},{1,5},{2,6},{3,7},{4,8},{5,9},{6,10},{7,11},{8,12},{9,13},{1... | collective-permute-start | bytes 1880072 | tf_op jit(solution)/shard_map/ppermute | solution.py:343
  57.7 19.4 %collective-permute-start.11 = (bf16[272,1152]{1,0:T(8,128)(2,1)S(1)}, bf16[272,1152]{1,0:T(8,128)(2,1)S(1)}, u32[]{:S(2)}, u32[]{:S(2)}) collective-permute-start(bf16[272,1152]{1,0:T(8,128)(2,1)S(1)} %get-tuple-element.74.refs_6_), channel_id=1, source_target_pairs={{0,12},{1,13},{2,14},{3,15},{4,0},{5,1},{6,2},{7,3},{8,4},{9,5},{1... | collective-permute-start | bytes 1880072 | tf_op jit(solution)/shard_map/ppermute | solution.py:343
  67.0 3.1 %collective-permute-start.13 = (bf16[512,1152]{1,0:T(8,128)(2,1)S(1)}, bf16[512,1152]{1,0:T(8,128)(2,1)S(1)}, u32[]{:S(2)}, u32[]{:S(2)}) collective-permute-start(bf16[512,1152]{1,0:T(8,128)(2,1)S(1)} %cols_yc.1.refs_8_), channel_id=1, source_target_pairs={{0,1},{1,0},{2,3},{3,2},{4,5},{5,4},{6,7},{7,6},{8,9},{9,8},{10,11... | collective-permute-start | bytes 3538952 | tf_op jit(solution)/shard_map/ppermute | solution.py:343
  70.3 30.2 %collective-permute-start.17 = (bf16[512,1152]{1,0:T(8,128)(2,1)S(1)}, bf16[512,1152]{1,0:T(8,128)(2,1)S(1)}, u32[]{:S(2)}, u32[]{:S(2)}) collective-permute-start(bf16[512,1152]{1,0:T(8,128)(2,1)S(1)} %add_y.1.refs_8_), channel_id=1, source_target_pairs={{0,2},{1,3},{2,0},{3,1},{4,6},{5,7},{6,4},{7,5},{8,10},{9,11},{10,... | collective-permute-start | bytes 3538952 | tf_op jit(solution)/shard_map/ppermute | solution.py:343
  76.7 7.6 %collective-permute-start.14 = (bf16[512,1152]{1,0:T(8,128)(2,1)S(1)}, bf16[512,1152]{1,0:T(8,128)(2,1)S(1)}, u32[]{:S(2)}, u32[]{:S(2)}) collective-permute-start(bf16[512,1152]{1,0:T(8,128)(2,1)S(1)} %cols_c.1.refs_4_), channel_id=1, source_target_pairs={{0,1},{1,0},{2,3},{3,2},{4,5},{5,4},{6,7},{7,6},{8,9},{9,8},{10,11... | collective-permute-start | bytes 3538952 | tf_op jit(solution)/shard_map/ppermute | solution.py:343
  77.6 17.5 %collective-permute-start.16 = (bf16[272,1152]{1,0:T(8,128)(2,1)S(1)}, bf16[272,1152]{1,0:T(8,128)(2,1)S(1)}, u32[]{:S(2)}, u32[]{:S(2)}) collective-permute-start(bf16[272,1152]{1,0:T(8,128)(2,1)S(1)} %get-tuple-element.95), channel_id=1, source_target_pairs={{0,4},{1,5},{2,6},{3,7},{4,8},{5,9},{6,10},{7,11},{8,12},{9,13},{1... | collective-permute-start | bytes 1880072 | tf_op jit(solution)/shard_map/ppermute | solution.py:343
  79.0 16.1 %collective-permute-start.15 = (bf16[272,1152]{1,0:T(8,128)(2,1)S(1)}, bf16[272,1152]{1,0:T(8,128)(2,1)S(1)}, u32[]{:S(2)}, u32[]{:S(2)}) collective-permute-start(bf16[272,1152]{1,0:T(8,128)(2,1)S(1)} %get-tuple-element.90.refs_8_), channel_id=1, source_target_pairs={{0,12},{1,13},{2,14},{3,15},{4,0},{5,1},{6,2},{7,3},{8,4},{9,5},{1... | collective-permute-start | bytes 1880072 | tf_op jit(solution)/shard_map/ppermute | solution.py:343
  84.3 1.3 %copy-start.1 = (bf16[512,1152]{1,0:T(8,128)(2,1)S(1)}, bf16[512,1152]{1,0:T(8,128)(2,1)}, u32[]{:S(2)}) copy-start(bf16[512,1152]{1,0:T(8,128)(2,1)} %refs_1_.2) | copy-start | bytes 3538948
  85.6 1.3 %copy-start.2 = (bf16[512,1152]{1,0:T(8,128)(2,1)S(1)}, bf16[512,1152]{1,0:T(8,128)(2,1)}, u32[]{:S(2)}) copy-start(bf16[512,1152]{1,0:T(8,128)(2,1)} %refs_1_.3) | copy-start | bytes 3538948
